TPU v7x, 256 devices: a whole 4x4x8 slice. The times are simulated.
256 devices in a mesh: leaf: 256 (over x, y, z, core).
Axes of the slice: x: 4, y: 4, z: 8, core: 2. Of those that a mesh axis runs over, the one named last changes fastest.
Arguments:
- right_sides: float32 [64, 262144], P(None, 'leaf'), may hold values from -6 to 6
- leaf_inverse: float32 [262144, 1024], P('leaf'), may hold values from -1.5 to 1.5
- coupling_first: float32 [262144, 256], P('leaf'), may hold values from -0.046875 to 0.046875
- coupling_second: float32 [262144, 256], P('leaf'), may hold values from -0.03125 to 0.03125
- coupling_third: float32 [262144, 256], P('leaf'), may hold values from -0.0234375 to 0.0234375
- coupling_fourth: float32 [262144, 256], P('leaf'), may hold values from -0.015625 to 0.015625
- solved_first: float32 [262144, 256], P('leaf'), may hold values from -0.375 to 0.375
- solved_second: float32 [262144, 256], P('leaf'), may hold values from -0.375 to 0.375
- solved_third: float32 [262144, 256], P('leaf'), may hold values from -0.375 to 0.375
- solved_fourth: float32 [262144, 256], P('leaf'), may hold values from -0.375 to 0.375
- first_level_inverse: float32 [4096, 512], P('leaf'), may hold values from -1.5 to 1.5
- second_level_inverse: float32 [2048, 512], P('leaf'), may hold values from -1.5 to 1.5
- third_level_inverse: float32 [1024, 512], P('leaf'), may hold values from -1.5 to 1.5
- root_level_inverse: float32 [512, 512], P('leaf'), may hold values from -1.5 to 1.5
Outputs:
- solution: float32 [64, 262144], P(None, 'leaf')
All inputs are finite; a program needn't handle non-finite values.
Results may differ from a plain program's by a relative error of at most 0.00028.
Values sent between devices are 32-bit elements; how exact they have to be, the bound alone decides.
No kernel may reach another device: no remote copies, remote signals or barrier semaphores. Data moves between devices by JAX's collectives and lax.ppermute only.
A program may use at most 64 MiB of HBM per device.

v0:
```python
import jax
import jax.numpy as jnp
from jax import lax
from jax.sharding import PartitionSpec as P


def swapped(value, axis, stride):
    mask = 2**stride
    pairs = [(source, source ^ mask) for source in range(lax.axis_size(axis))]
    return lax.ppermute(value, axis, pairs)


def product_nt(left, right):
    return lax.dot_general(
        left,
        right,
        (((1,), (1,)), ((), ())),
        precision=lax.Precision.HIGHEST,
        preferred_element_type=jnp.float32,
    )


def apply_tree_level(running_solution, coupling, solved, capacity, level_bit, device_id):
    local_sum = jnp.dot(
        running_solution,
        coupling,
        precision=lax.Precision.HIGHEST,
        preferred_element_type=jnp.float32,
    )
    own_sum = local_sum
    for step_bit in range(level_bit):
        own_sum = own_sum + swapped(own_sum, "leaf", step_bit)
    sibling = swapped(own_sum, "leaf", level_bit)
    first_half = device_id >> level_bit & 1 == 0
    upper = jnp.where(first_half, sibling, own_sum)
    lower = jnp.where(first_half, own_sum, sibling)
    stacked = jnp.concatenate([upper, lower], axis=1)
    collected = product_nt(stacked, capacity)
    for step_bit in range(level_bit):
        partner = swapped(collected, "leaf", step_bit)
        lower_side = device_id >> step_bit & 1 == 0
        collected = jnp.where(
            lower_side,
            jnp.concatenate([collected, partner], axis=1),
            jnp.concatenate([partner, collected], axis=1),
        )
    return running_solution - product_nt(collected, solved)


def per_device(
    right_sides,
    leaf_inverse,
    coupling_first,
    coupling_second,
    coupling_third,
    coupling_fourth,
    solved_first,
    solved_second,
    solved_third,
    solved_fourth,
    first_level_inverse,
    second_level_inverse,
    third_level_inverse,
    root_level_inverse,
):
    axis_count = lax.axis_size("leaf")
    tree_depth = axis_count.bit_length() - 1
    device_id = lax.axis_index("leaf")
    running_solution = product_nt(right_sides, leaf_inverse)
    coupling_factors = [coupling_first, coupling_second, coupling_third, coupling_fourth]
    solved_blocks = [solved_first, solved_second, solved_third, solved_fourth]
    capacitance_inverses = [
        first_level_inverse,
        second_level_inverse,
        third_level_inverse,
        root_level_inverse,
    ]
    for level_number in range(4):
        running_solution = apply_tree_level(
            running_solution,
            coupling_factors[level_number],
            solved_blocks[level_number],
            capacitance_inverses[level_number],
            tree_depth - 4 + level_number,
            device_id,
        )
    return running_solution


def solution(mesh):
    in_specs = (
        P(None, "leaf"),
        P("leaf", None),
        P("leaf", None),
        P("leaf", None),
        P("leaf", None),
        P("leaf", None),
        P("leaf", None),
        P("leaf", None),
        P("leaf", None),
        P("leaf", None),
        P("leaf", None),
        P("leaf", None),
        P("leaf", None),
        P("leaf", None),
    )
    out_specs = P(None, "leaf")
    return jax.shard_map(
        per_device, mesh=mesh, in_specs=in_specs, out_specs=out_specs, check_vma=False
    )
```

profile of v0, /device:TPU:18, one launch (start us, length us, event | category | flops | bytes accessed | tf_op | source)
XLA Modules:
  0.0 252.2 jit_solution(11959347950680477459)
XLA Ops:
  0.0 6.5 %fusion.48 = f32[64,1024]{1,0:T(8,128)S(1)} fusion(f32[64,1024]{1,0:T(8,128)} %param.14, f32[1024,1024]{1,0:T(8,128)} %param.15), kind=kOutput, calls=%fused_computation.88 | convolution fusion | flops 805306368 | bytes 4718592 | tf_op jit(solution)/shard_map/dot_general | solution.py:14
  18.9 7.4 %collective-permute-start.3 = (f32[64,256]{1,0:T(8,128)S(1)}, f32[64,256]{1,0:T(8,128)S(1)}, u32[]{:S(2)}, u32[]{:S(2)}) collective-permute-start(f32[64,256]{1,0:T(8,128)S(1)} %add.68), channel_id=1, source_target_pairs={{0,8},{1,9},{2,10},{3,11},{4,12},{5,13},{6,14},{7,15},{8,0},{9,1},... | collective-permute-start | bytes 196616 | tf_op jit(solution)/shard_map/ppermute | solution.py:10
  42.9 6.2 %collective-permute-start.8 = (f32[64,128]{0,1:T(8,128)S(1)}, f32[64,128]{0,1:T(8,128)S(1)}, u32[]{:S(2)}, u32[]{:S(2)}) collective-permute-start(f32[64,128]{0,1:T(8,128)S(1)} %maximum_select_fusion.2), channel_id=1, source_target_pairs={{0,8},{1,9},{2,10},{3,11},{4,12},{5,13},{6,14},{7,15},{8,0},{9,1},... | collective-permute-start | bytes 98312 | tf_op jit(solution)/shard_map/ppermute | solution.py:10
  56.6 4.2 %collective-permute-done.10 = f32[64,256]{1,0:T(8,128)S(1)} collective-permute-done((f32[64,256]{1,0:T(8,128)S(1)}, f32[64,256]{1,0:T(8,128)S(1)}, u32[]{:S(2)}, u32[]{:S(2)}) %collective-permute-start.10) | collective-permute-done | bytes 65568 | tf_op jit(solution)/shard_map/ppermute | solution.py:10
  62.0 4.4 %collective-permute-done.11 = f32[64,256]{1,0:T(8,128)S(1)} collective-permute-done((f32[64,256]{1,0:T(8,128)S(1)}, f32[64,256]{1,0:T(8,128)S(1)}, u32[]{:S(2)}, u32[]{:S(2)}) %collective-permute-start.11) | collective-permute-done | bytes 65568 | tf_op jit(solution)/shard_map/ppermute | solution.py:10
  66.4 5.5 %collective-permute-start.12 = (f32[64,256]{1,0:T(8,128)S(1)}, f32[64,256]{1,0:T(8,128)S(1)}, u32[]{:S(2)}, u32[]{:S(2)}) collective-permute-start(f32[64,256]{1,0:T(8,128)S(1)} %add.72), channel_id=1, source_target_pairs={{0,8},{1,9},{2,10},{3,11},{4,12},{5,13},{6,14},{7,15},{8,0},{9,1},... | collective-permute-start | bytes 196616 | tf_op jit(solution)/shard_map/ppermute | solution.py:10
  79.9 5.8 %collective-permute-done.14 = f32[64,256]{1,0:T(8,128)S(1)} collective-permute-done((f32[64,256]{1,0:T(8,128)S(1)}, f32[64,256]{1,0:T(8,128)S(1)}, u32[]{:S(2)}, u32[]{:S(2)}) %collective-permute-start.14) | collective-permute-done | bytes 65568 | tf_op jit(solution)/shard_map/ppermute | solution.py:10
  87.5 3.8 %collective-permute-done.16 = f32[64,16]{1,0:T(8,128)S(1)} collective-permute-done((f32[64,16]{1,0:T(8,128)S(1)}, f32[64,16]{1,0:T(8,128)S(1)}, u32[]{:S(2)}, u32[]{:S(2)}) %collective-permute-start.16) | collective-permute-done | bytes 4128 | tf_op jit(solution)/shard_map/ppermute | solution.py:10
  92.4 3.8 %collective-permute-done.17 = f32[64,32]{1,0:T(8,128)S(1)} collective-permute-done((f32[64,32]{1,0:T(8,128)S(1)}, f32[64,32]{1,0:T(8,128)S(1)}, u32[]{:S(2)}, u32[]{:S(2)}) %collective-permute-start.17) | collective-permute-done | bytes 8224 | tf_op jit(solution)/shard_map/ppermute | solution.py:10
  96.3 5.3 %collective-permute-start.18 = (f32[64,64]{1,0:T(8,128)S(1)}, f32[64,64]{1,0:T(8,128)S(1)}, u32[]{:S(2)}, u32[]{:S(2)}) collective-permute-start(f32[64,64]{1,0:T(8,128)S(1)} %maximum_select_fusion.11), channel_id=1, source_target_pairs={{0,8},{1,9},{2,10},{3,11},{4,12},{5,13},{6,14},{7,15},{8,0},{9,1},... | collective-permute-start | bytes 49160 | tf_op jit(solution)/shard_map/ppermute | solution.py:10
  113.0 4.1 %collective-permute-done.21 = f32[64,256]{1,0:T(8,128)S(1)} collective-permute-done((f32[64,256]{1,0:T(8,128)S(1)}, f32[64,256]{1,0:T(8,128)S(1)}, u32[]{:S(2)}, u32[]{:S(2)}) %collective-permute-start.21) | collective-permute-done | bytes 65568 | tf_op jit(solution)/shard_map/ppermute | solution.py:10
  118.4 4.3 %collective-permute-done.22 = f32[64,256]{1,0:T(8,128)S(1)} collective-permute-done((f32[64,256]{1,0:T(8,128)S(1)}, f32[64,256]{1,0:T(8,128)S(1)}, u32[]{:S(2)}, u32[]{:S(2)}) %collective-permute-start.22) | collective-permute-done | bytes 65568 | tf_op jit(solution)/shard_map/ppermute | solution.py:10
  122.7 5.3 %collective-permute-start.23 = (f32[64,256]{1,0:T(8,128)S(1)}, f32[64,256]{1,0:T(8,128)S(1)}, u32[]{:S(2)}, u32[]{:S(2)}) collective-permute-start(f32[64,256]{1,0:T(8,128)S(1)} %add.77), channel_id=1, source_target_pairs={{0,8},{1,9},{2,10},{3,11},{4,12},{5,13},{6,14},{7,15},{8,0},{9,1},... | collective-permute-start | bytes 196616 | tf_op jit(solution)/shard_map/ppermute | solution.py:10
  136.1 5.8 %collective-permute-done.25 = f32[64,256]{1,0:T(8,128)S(1)} collective-permute-done((f32[64,256]{1,0:T(8,128)S(1)}, f32[64,256]{1,0:T(8,128)S(1)}, u32[]{:S(2)}, u32[]{:S(2)}) %collective-permute-start.25) | collective-permute-done | bytes 65568 | tf_op jit(solution)/shard_map/ppermute | solution.py:10
  152.4 4.0 %collective-permute-done.29 = f32[64,16]{1,0:T(8,128)S(1)} collective-permute-done((f32[64,16]{1,0:T(8,128)S(1)}, f32[64,16]{1,0:T(8,128)S(1)}, u32[]{:S(2)}, u32[]{:S(2)}) %collective-permute-start.29) | collective-permute-done | bytes 4128 | tf_op jit(solution)/shard_map/ppermute | solution.py:10
  156.5 4.7 %collective-permute-start.30 = (f32[64,32]{1,0:T(8,128)S(1)}, f32[64,32]{1,0:T(8,128)S(1)}, u32[]{:S(2)}, u32[]{:S(2)}) collective-permute-start(f32[64,32]{1,0:T(8,128)S(1)} %maximum_select_fusion.13), channel_id=1, source_target_pairs={{0,8},{1,9},{2,10},{3,11},{4,12},{5,13},{6,14},{7,15},{8,0},{9,1},... | collective-permute-start | bytes 24584 | tf_op jit(solution)/shard_map/ppermute | solution.py:10
  168.9 5.4 %collective-permute-done.32 = f32[64,128]{1,0:T(8,128)S(1)} collective-permute-done((f32[64,128]{1,0:T(8,128)S(1)}, f32[64,128]{1,0:T(8,128)S(1)}, u32[]{:S(2)}, u32[]{:S(2)}) %collective-permute-start.32) | collective-permute-done | bytes 32800 | tf_op jit(solution)/shard_map/ppermute | solution.py:10
  180.0 4.3 %collective-permute-done.34 = f32[64,256]{1,0:T(8,128)S(1)} collective-permute-done((f32[64,256]{1,0:T(8,128)S(1)}, f32[64,256]{1,0:T(8,128)S(1)}, u32[]{:S(2)}, u32[]{:S(2)}) %collective-permute-start.34) | collective-permute-done | bytes 65568 | tf_op jit(solution)/shard_map/ppermute | solution.py:10
  185.2 4.6 %collective-permute-done.35 = f32[64,256]{1,0:T(8,128)S(1)} collective-permute-done((f32[64,256]{1,0:T(8,128)S(1)}, f32[64,256]{1,0:T(8,128)S(1)}, u32[]{:S(2)}, u32[]{:S(2)}) %collective-permute-start.35) | collective-permute-done | bytes 65568 | tf_op jit(solution)/shard_map/ppermute | solution.py:10
  189.8 4.7 %collective-permute-start.36 = (f32[64,256]{1,0:T(8,128)S(1)}, f32[64,256]{1,0:T(8,128)S(1)}, u32[]{:S(2)}, u32[]{:S(2)}) collective-permute-start(f32[64,256]{1,0:T(8,128)S(1)} %add.83), channel_id=1, source_target_pairs={{0,8},{1,9},{2,10},{3,11},{4,12},{5,13},{6,14},{7,15},{8,0},{9,1},... | collective-permute-start | bytes 196616 | tf_op jit(solution)/shard_map/ppermute | solution.py:10
  202.8 5.8 %collective-permute-done.38 = f32[64,256]{1,0:T(8,128)S(1)} collective-permute-done((f32[64,256]{1,0:T(8,128)S(1)}, f32[64,256]{1,0:T(8,128)S(1)}, u32[]{:S(2)}, u32[]{:S(2)}) %collective-permute-start.38) | collective-permute-done | bytes 65568 | tf_op jit(solution)/shard_map/ppermute | solution.py:10
  224.6 3.8 %collective-permute-done.43 = f32[64,8]{0,1:T(8,128)S(1)} collective-permute-done((f32[64,8]{0,1:T(8,128)S(1)}, f32[64,8]{0,1:T(8,128)S(1)}, u32[]{:S(2)}, u32[]{:S(2)}) %collective-permute-start.43) | collective-permute-done | bytes 2080 | tf_op jit(solution)/shard_map/ppermute | solution.py:10
  228.6 4.5 %collective-permute-start.44 = (f32[64,16]{1,0:T(8,128)S(1)}, f32[64,16]{1,0:T(8,128)S(1)}, u32[]{:S(2)}, u32[]{:S(2)}) collective-permute-start(f32[64,16]{1,0:T(8,128)S(1)} %broadcast_select_fusion.8), channel_id=1, source_target_pairs={{0,8},{1,9},{2,10},{3,11},{4,12},{5,13},{6,14},{7,15},{8,0},{9,1},... | collective-permute-start | bytes 12296 | tf_op jit(solution)/shard_map/ppermute | solution.py:10
  240.8 5.4 %collective-permute-done.46 = f32[64,64]{1,0:T(8,128)S(1)} collective-permute-done((f32[64,64]{1,0:T(8,128)S(1)}, f32[64,64]{1,0:T(8,128)S(1)}, u32[]{:S(2)}, u32[]{:S(2)}) %collective-permute-start.46) | collective-permute-done | bytes 16416 | tf_op jit(solution)/shard_map/ppermute | solution.py:10
  (154 shorter events, 132.4 us)
Async XLA Ops:
  12.9 5.9 %collective-permute-start.2 = (f32[64,256]{1,0:T(8,128)S(1)}, f32[64,256]{1,0:T(8,128)S(1)}, u32[]{:S(2)}, u32[]{:S(2)}) collective-permute-start(f32[64,256]{1,0:T(8,128)S(1)} %add.67), channel_id=1, source_target_pairs={{0,4},{1,5},{2,6},{3,7},{4,0},{5,1},{6,2},{7,3},{8,12},{9,13},{10,... | collective-permute-start | bytes 196616 | tf_op jit(solution)/shard_map/ppermute | solution.py:10
  18.9 9.6 %collective-permute-start.3 = (f32[64,256]{1,0:T(8,128)S(1)}, f32[64,256]{1,0:T(8,128)S(1)}, u32[]{:S(2)}, u32[]{:S(2)}) collective-permute-start(f32[64,256]{1,0:T(8,128)S(1)} %add.68), channel_id=1, source_target_pairs={{0,8},{1,9},{2,10},{3,11},{4,12},{5,13},{6,14},{7,15},{8,0},{9,1},... | collective-permute-start | bytes 196616 | tf_op jit(solution)/shard_map/ppermute | solution.py:10
  38.0 4.8 %collective-permute-start.7 = (f32[64,64]{0,1:T(8,128)S(1)}, f32[64,64]{0,1:T(8,128)S(1)}, u32[]{:S(2)}, u32[]{:S(2)}) collective-permute-start(f32[64,64]{0,1:T(8,128)S(1)} %maximum_select_fusion.9), channel_id=1, source_target_pairs={{0,4},{1,5},{2,6},{3,7},{4,0},{5,1},{6,2},{7,3},{8,12},{9,13},{10,... | collective-permute-start | bytes 49160 | tf_op jit(solution)/shard_map/ppermute | solution.py:10
  42.9 9.1 %collective-permute-start.8 = (f32[64,128]{0,1:T(8,128)S(1)}, f32[64,128]{0,1:T(8,128)S(1)}, u32[]{:S(2)}, u32[]{:S(2)}) collective-permute-start(f32[64,128]{0,1:T(8,128)S(1)} %maximum_select_fusion.2), channel_id=1, source_target_pairs={{0,8},{1,9},{2,10},{3,11},{4,12},{5,13},{6,14},{7,15},{8,0},{9,1},... | collective-permute-start | bytes 98312 | tf_op jit(solution)/shard_map/ppermute | solution.py:10
  60.8 5.6 %collective-permute-start.11 = (f32[64,256]{1,0:T(8,128)S(1)}, f32[64,256]{1,0:T(8,128)S(1)}, u32[]{:S(2)}, u32[]{:S(2)}) collective-permute-start(f32[64,256]{1,0:T(8,128)S(1)} %add.71), channel_id=1, source_target_pairs={{0,4},{1,5},{2,6},{3,7},{4,0},{5,1},{6,2},{7,3},{8,12},{9,13},{10,... | collective-permute-start | bytes 196616 | tf_op jit(solution)/shard_map/ppermute | solution.py:10
  66.4 8.7 %collective-permute-start.12 = (f32[64,256]{1,0:T(8,128)S(1)}, f32[64,256]{1,0:T(8,128)S(1)}, u32[]{:S(2)}, u32[]{:S(2)}) collective-permute-start(f32[64,256]{1,0:T(8,128)S(1)} %add.72), channel_id=1, source_target_pairs={{0,8},{1,9},{2,10},{3,11},{4,12},{5,13},{6,14},{7,15},{8,0},{9,1},... | collective-permute-start | bytes 196616 | tf_op jit(solution)/shard_map/ppermute | solution.py:10
  75.1 4.7 %collective-permute-start.13 = (f32[64,256]{1,0:T(8,128)S(1)}, f32[64,256]{1,0:T(8,128)S(1)}, u32[]{:S(2)}, u32[]{:S(2)}) collective-permute-start(f32[64,256]{1,0:T(8,128)S(1)} %add.73), channel_id=1, source_target_pairs={{0,16},{1,17},{2,18},{3,19},{4,20},{5,21},{6,22},{7,23},{8,24},{9,... | collective-permute-start | bytes 196616 | tf_op jit(solution)/shard_map/ppermute | solution.py:10
  79.8 5.9 %collective-permute-start.14 = (f32[64,256]{1,0:T(8,128)S(1)}, f32[64,256]{1,0:T(8,128)S(1)}, u32[]{:S(2)}, u32[]{:S(2)}) collective-permute-start(f32[64,256]{1,0:T(8,128)S(1)} %add.74), channel_id=1, source_target_pairs={{0,32},{1,33},{2,34},{3,35},{4,36},{5,37},{6,38},{7,39},{8,40},{9,... | collective-permute-start | bytes 196616 | tf_op jit(solution)/shard_map/ppermute | solution.py:10
  91.3 4.9 %collective-permute-start.17 = (f32[64,32]{1,0:T(8,128)S(1)}, f32[64,32]{1,0:T(8,128)S(1)}, u32[]{:S(2)}, u32[]{:S(2)}) collective-permute-start(f32[64,32]{1,0:T(8,128)S(1)} %maximum_select_fusion.10), channel_id=1, source_target_pairs={{0,4},{1,5},{2,6},{3,7},{4,0},{5,1},{6,2},{7,3},{8,12},{9,13},{10,... | collective-permute-start | bytes 24584 | tf_op jit(solution)/shard_map/ppermute | solution.py:10
  96.3 7.9 %collective-permute-start.18 = (f32[64,64]{1,0:T(8,128)S(1)}, f32[64,64]{1,0:T(8,128)S(1)}, u32[]{:S(2)}, u32[]{:S(2)}) collective-permute-start(f32[64,64]{1,0:T(8,128)S(1)} %maximum_select_fusion.11), channel_id=1, source_target_pairs={{0,8},{1,9},{2,10},{3,11},{4,12},{5,13},{6,14},{7,15},{8,0},{9,1},... | collective-permute-start | bytes 49160 | tf_op jit(solution)/shard_map/ppermute | solution.py:10
  117.2 5.6 %collective-permute-start.22 = (f32[64,256]{1,0:T(8,128)S(1)}, f32[64,256]{1,0:T(8,128)S(1)}, u32[]{:S(2)}, u32[]{:S(2)}) collective-permute-start(f32[64,256]{1,0:T(8,128)S(1)} %add.76), channel_id=1, source_target_pairs={{0,4},{1,5},{2,6},{3,7},{4,0},{5,1},{6,2},{7,3},{8,12},{9,13},{10,... | collective-permute-start | bytes 196616 | tf_op jit(solution)/shard_map/ppermute | solution.py:10
  122.7 8.9 %collective-permute-start.23 = (f32[64,256]{1,0:T(8,128)S(1)}, f32[64,256]{1,0:T(8,128)S(1)}, u32[]{:S(2)}, u32[]{:S(2)}) collective-permute-start(f32[64,256]{1,0:T(8,128)S(1)} %add.77), channel_id=1, source_target_pairs={{0,8},{1,9},{2,10},{3,11},{4,12},{5,13},{6,14},{7,15},{8,0},{9,1},... | collective-permute-start | bytes 196616 | tf_op jit(solution)/shard_map/ppermute | solution.py:10
  136.0 5.9 %collective-permute-start.25 = (f32[64,256]{1,0:T(8,128)S(1)}, f32[64,256]{1,0:T(8,128)S(1)}, u32[]{:S(2)}, u32[]{:S(2)}) collective-permute-start(f32[64,256]{1,0:T(8,128)S(1)} %add.79), channel_id=1, source_target_pairs={{0,32},{1,33},{2,34},{3,35},{4,36},{5,37},{6,38},{7,39},{8,40},{9,... | collective-permute-start | bytes 196616 | tf_op jit(solution)/shard_map/ppermute | solution.py:10
  151.5 4.9 %collective-permute-start.29 = (f32[64,16]{1,0:T(8,128)S(1)}, f32[64,16]{1,0:T(8,128)S(1)}, u32[]{:S(2)}, u32[]{:S(2)}) collective-permute-start(f32[64,16]{1,0:T(8,128)S(1)} %broadcast_select_fusion.9), channel_id=1, source_target_pairs={{0,4},{1,5},{2,6},{3,7},{4,0},{5,1},{6,2},{7,3},{8,12},{9,13},{10,... | collective-permute-start | bytes 12296 | tf_op jit(solution)/shard_map/ppermute | solution.py:10
  156.5 7.9 %collective-permute-start.30 = (f32[64,32]{1,0:T(8,128)S(1)}, f32[64,32]{1,0:T(8,128)S(1)}, u32[]{:S(2)}, u32[]{:S(2)}) collective-permute-start(f32[64,32]{1,0:T(8,128)S(1)} %maximum_select_fusion.13), channel_id=1, source_target_pairs={{0,8},{1,9},{2,10},{3,11},{4,12},{5,13},{6,14},{7,15},{8,0},{9,1},... | collective-permute-start | bytes 24584 | tf_op jit(solution)/shard_map/ppermute | solution.py:10
  168.8 5.5 %collective-permute-start.32 = (f32[64,128]{1,0:T(8,128)S(1)}, f32[64,128]{1,0:T(8,128)S(1)}, u32[]{:S(2)}, u32[]{:S(2)}) collective-permute-start(f32[64,128]{1,0:T(8,128)S(1)} %maximum_select_fusion.15), channel_id=1, source_target_pairs={{0,32},{1,33},{2,34},{3,35},{4,36},{5,37},{6,38},{7,39},{8,40},{9,... | collective-permute-start | bytes 98312 | tf_op jit(solution)/shard_map/ppermute | solution.py:10
  184.3 5.6 %collective-permute-start.35 = (f32[64,256]{1,0:T(8,128)S(1)}, f32[64,256]{1,0:T(8,128)S(1)}, u32[]{:S(2)}, u32[]{:S(2)}) collective-permute-start(f32[64,256]{1,0:T(8,128)S(1)} %add.82), channel_id=1, source_target_pairs={{0,4},{1,5},{2,6},{3,7},{4,0},{5,1},{6,2},{7,3},{8,12},{9,13},{10,... | collective-permute-start | bytes 196616 | tf_op jit(solution)/shard_map/ppermute | solution.py:10
  189.8 8.3 %collective-permute-start.36 = (f32[64,256]{1,0:T(8,128)S(1)}, f32[64,256]{1,0:T(8,128)S(1)}, u32[]{:S(2)}, u32[]{:S(2)}) collective-permute-start(f32[64,256]{1,0:T(8,128)S(1)} %add.83), channel_id=1, source_target_pairs={{0,8},{1,9},{2,10},{3,11},{4,12},{5,13},{6,14},{7,15},{8,0},{9,1},... | collective-permute-start | bytes 196616 | tf_op jit(solution)/shard_map/ppermute | solution.py:10
  198.1 4.6 %collective-permute-start.37 = (f32[64,256]{1,0:T(8,128)S(1)}, f32[64,256]{1,0:T(8,128)S(1)}, u32[]{:S(2)}, u32[]{:S(2)}) collective-permute-start(f32[64,256]{1,0:T(8,128)S(1)} %add.84), channel_id=1, source_target_pairs={{0,16},{1,17},{2,18},{3,19},{4,20},{5,21},{6,22},{7,23},{8,24},{9,... | collective-permute-start | bytes 196616 | tf_op jit(solution)/shard_map/ppermute | solution.py:10
  202.7 5.9 %collective-permute-start.38 = (f32[64,256]{1,0:T(8,128)S(1)}, f32[64,256]{1,0:T(8,128)S(1)}, u32[]{:S(2)}, u32[]{:S(2)}) collective-permute-start(f32[64,256]{1,0:T(8,128)S(1)} %add.85), channel_id=1, source_target_pairs={{0,32},{1,33},{2,34},{3,35},{4,36},{5,37},{6,38},{7,39},{8,40},{9,... | collective-permute-start | bytes 196616 | tf_op jit(solution)/shard_map/ppermute | solution.py:10
  212.9 5.9 %collective-permute-start.40 = (f32[64,256]{1,0:T(8,128)S(1)}, f32[64,256]{1,0:T(8,128)S(1)}, u32[]{:S(2)}, u32[]{:S(2)}) collective-permute-start(f32[64,256]{1,0:T(8,128)S(1)} %add.87), channel_id=1, source_target_pairs={{0,128},{1,129},{2,130},{3,131},{4,132},{5,133},{6,134},{7,135},{8... | collective-permute-start | bytes 196616 | tf_op jit(solution)/shard_map/ppermute | solution.py:10
  223.9 4.6 %collective-permute-start.43 = (f32[64,8]{0,1:T(8,128)S(1)}, f32[64,8]{0,1:T(8,128)S(1)}, u32[]{:S(2)}, u32[]{:S(2)}) collective-permute-start(f32[64,8]{0,1:T(8,128)S(1)} %maximum_select_fusion.21), channel_id=1, source_target_pairs={{0,4},{1,5},{2,6},{3,7},{4,0},{5,1},{6,2},{7,3},{8,12},{9,13},{10,... | collective-permute-start | bytes 6152 | tf_op jit(solution)/shard_map/ppermute | solution.py:10
  228.6 7.9 %collective-permute-start.44 = (f32[64,16]{1,0:T(8,128)S(1)}, f32[64,16]{1,0:T(8,128)S(1)}, u32[]{:S(2)}, u32[]{:S(2)}) collective-permute-start(f32[64,16]{1,0:T(8,128)S(1)} %broadcast_select_fusion.8), channel_id=1, source_target_pairs={{0,8},{1,9},{2,10},{3,11},{4,12},{5,13},{6,14},{7,15},{8,0},{9,1},... | collective-permute-start | bytes 12296 | tf_op jit(solution)/shard_map/ppermute | solution.py:10
  240.7 5.5 %collective-permute-start.46 = (f32[64,64]{1,0:T(8,128)S(1)}, f32[64,64]{1,0:T(8,128)S(1)}, u32[]{:S(2)}, u32[]{:S(2)}) collective-permute-start(f32[64,64]{1,0:T(8,128)S(1)} %maximum_select_fusion.17), channel_id=1, source_target_pairs={{0,32},{1,33},{2,34},{3,35},{4,36},{5,37},{6,38},{7,39},{8,40},{9,... | collective-permute-start | bytes 49160 | tf_op jit(solution)/shard_map/ppermute | solution.py:10
  (32 other events, 692.0 us)
where the time goes:
time: 252 us
  waiting for transfers between devices  159 us (63%)
  starting transfers between devices  71.6 us (28%)
  matrix products  20 us (8%)
    ppermute x48, waiting for transfers between devices, swapped(): return lax.ppermute(value, axis, pairs)  159 us
    ppermute x48, starting transfers between devices, swapped(): return lax.ppermute(value, axis, pairs)  71.6 us
    dot_general x9, matrix products, product_nt(): lax.dot_general(left, right, (((1,), (1,)), ((), ())), precision=lax.Prec...  13.7 us
    dot_general x4, matrix products, apply_tree_level(): jnp.dot(running_solution, coupling, precision=lax.Precision.HIGHEST, pref...  6.33 us
  transfers between devices with their start and end apart: 48, of which 48 were waited for; matrix products, arithmetic and copies ran while one was open for 0% of the time, Pallas kernels for 0%

commit v1 on v0

v1 whole, which is shorter than its diff:
```python
import jax
import jax.numpy as jnp
from jax import lax
from jax.sharding import PartitionSpec as P

CORE, Z_LOW, Z_MID, Z_FLIP = 1, 2, 4, 14
Y_LOW, Y_FLIP, X_LOW, X_FLIP = 16, 48, 64, 192


def swapped(value, mask):
    pairs = [(source, source ^ mask) for source in range(lax.axis_size("leaf"))]
    return lax.ppermute(value, "leaf", pairs)


def product(left, right, dims, precision=lax.Precision.HIGH):
    return lax.dot_general(
        left,
        right,
        ((dims[:1], dims[1:]), ((), ())),
        precision=precision,
        preferred_element_type=jnp.float32,
    )


def product_nn(left, right):
    return product(left, right, (1, 0))


def product_nt(left, right):
    return product(left, right, (1, 1))


def product_tn(left, right):
    return product(left, right, (0, 0))


def summed(value, masks):
    for mask in masks:
        value = value + swapped(value, mask)
    return value


def split_sum(value, bit, mask):
    half = value.shape[0] // 2
    low, high = value[:half], value[half:]
    kept = jnp.where(bit, high, low)
    sent = jnp.where(bit, low, high)
    return kept + swapped(sent, mask)


def ordered(own, other, bit, axis=0):
    return jnp.where(
        bit,
        jnp.concatenate([other, own], axis=axis),
        jnp.concatenate([own, other], axis=axis),
    )


def joined(value, bit, mask, axis=0):
    return ordered(value, swapped(value, mask), bit, axis)


def gather_first(capacity, bits):
    rows, width = capacity.shape
    held = joined(capacity, bits[3], Z_FLIP)
    held = joined(held, bits[2] != bits[3], Z_MID)
    held = joined(held, bits[1] != bits[3], Z_LOW)
    held = joined(held, bits[0], CORE)
    held = held.reshape(2, 2, 2, 2, rows, width)
    low = held[:, :, :, 0].transpose(2, 1, 0, 3, 4)
    high = held[:, ::-1, ::-1, 1].transpose(2, 1, 0, 3, 4)
    return jnp.stack([low, high]).reshape(16 * rows, width)


def gather_rest(second, third, fourth, bits):
    width = second.shape[1]
    a, b, c = second.shape[0], third.shape[0], fourth.shape[0]
    other = swapped(jnp.concatenate([second, third, fourth]), Y_LOW)
    second = ordered(second, other[:a], bits[4])
    third = ordered(third, other[a : a + b], bits[4])
    fourth = ordered(fourth, other[a + b :], bits[4])
    other = swapped(jnp.concatenate([third, fourth]), Y_FLIP)
    third = ordered(third, other[: 2 * b], bits[5])
    fourth = ordered(fourth, other[2 * b :], bits[5])
    fourth = joined(fourth, bits[6], X_LOW)
    rows = second.shape[0]
    count = lax.axis_size("leaf")
    groups = [list(range(first, first + 16)) for first in range(0, count, 16)]
    whole = lax.all_gather(
        jnp.concatenate([second, third, fourth]), "leaf", axis_index_groups=groups
    )
    out = []
    for number, block in enumerate((a, b, c)):
        part = whole[:, number * rows : (number + 1) * rows]
        part = part.reshape(16, rows // block, block, width).transpose(1, 0, 2, 3)
        out.append(part.reshape(16 * rows, width))
    return out


def cross_terms(solved_second, solved_third, coupling_third, coupling_fourth, bits):
    rank = coupling_third.shape[1]
    second = product_tn(
        solved_second, jnp.concatenate([coupling_third, coupling_fourth], axis=1)
    )
    third = product_tn(solved_third, coupling_fourth)
    both = jnp.concatenate([second, third], axis=1)
    both = split_sum(both, bits[0], CORE)
    low, mid = bits[1] != bits[3], bits[2] != bits[3]
    both = split_sum(both, low, Z_LOW)
    both = split_sum(both, mid, Z_MID)
    both = summed(both, (Z_FLIP, Y_LOW))
    both = jnp.concatenate(
        [both[:, : 2 * rank], summed(both[:, 2 * rank :], (Y_FLIP,))], axis=1
    )
    both = joined(both, mid, Z_MID)
    both = joined(both, low, Z_LOW)
    both = joined(both, bits[0], CORE)
    return both[:, : 2 * rank], both[:, 2 * rank :]


def weights_of(own, mask, bit, capacity):
    return product_nt(ordered(own, swapped(own, mask), ~bit, axis=1), capacity)


def per_device(
    right_sides,
    leaf_inverse,
    coupling_first,
    coupling_second,
    coupling_third,
    coupling_fourth,
    solved_first,
    solved_second,
    solved_third,
    solved_fourth,
    first_level_inverse,
    second_level_inverse,
    third_level_inverse,
    root_level_inverse,
):
    rank = coupling_first.shape[1]
    device_id = lax.axis_index("leaf")
    bits = [(device_id >> place) & 1 == 1 for place in range(8)]
    capacity_first = gather_first(first_level_inverse, bits)
    capacity_second, capacity_third, capacity_fourth = gather_rest(
        second_level_inverse, third_level_inverse, root_level_inverse, bits
    )
    cross_second, cross_third = cross_terms(
        solved_second, solved_third, coupling_third, coupling_fourth, bits
    )

    current = product_nt(right_sides, leaf_inverse)

    sums = split_sum(product_nn(current, coupling_first), bits[0], CORE)
    sums = summed(sums, (Z_LOW, Z_MID, Z_FLIP))
    weights = weights_of(sums, Y_LOW, bits[4], capacity_first)
    weights = joined(weights, bits[0], CORE)
    current = current - product_nt(weights, solved_first)

    coupling = jnp.concatenate([coupling_second, coupling_third, coupling_fourth], axis=1)
    sums = split_sum(product_nn(current, coupling), bits[0], CORE)
    sums = summed(sums, (Z_LOW, Z_MID, Z_FLIP, Y_LOW))
    second = weights_of(sums[:, :rank], Y_FLIP, bits[5], capacity_second)
    sums = sums[:, rank:] - product_nn(second, cross_second)
    sums = summed(sums, (Y_FLIP,))
    third = weights_of(sums[:, :rank], X_LOW, bits[6], capacity_third)
    sums = sums[:, rank:] - product_nn(third, cross_third)
    sums = summed(sums, (X_LOW,))
    fourth = weights_of(sums, X_FLIP, bits[7], capacity_fourth)
    weights = joined(jnp.concatenate([second, third, fourth], axis=1), bits[0], CORE)
    solved = jnp.concatenate([solved_second, solved_third, solved_fourth], axis=1)
    return current - product_nt(weights, solved)


def solution(mesh):
    in_specs = (P(None, "leaf"),) + (P("leaf", None),) * 13
    return jax.shard_map(
        per_device,
        mesh=mesh,
        in_specs=in_specs,
        out_specs=P(None, "leaf"),
        check_vma=False,
    )
```

time: 252 us -> 195 us (0.77)
  the two profiles are of different devices: /device:TPU:18 before, /device:TPU:1 now
where the time goes in v1:
time: 195 us
  waiting for transfers between devices  101 us (52%)
  starting transfers between devices  52.5 us (27%)
  matrix products  15.2 us (8%)
  between operations  14 us (7%)
  local copies, waits for them, and re-layouts  7.85 us (4%)
  other arithmetic  4.59 us (2%)
    ppermute x33, waiting for transfers between devices, swapped(): return lax.ppermute(value, 'leaf', pairs)  101 us
    ppermute x33, starting transfers between devices, swapped(): return lax.ppermute(value, 'leaf', pairs)  52.5 us
    dot_general x13, matrix products, product(): lax.dot_general(left, right, ((dims[:1], dims[1:]), ((), ())), precision=...  15.2 us
  transfers between devices with their start and end apart: 34, of which 18 were waited for; matrix products, arithmetic and copies ran while one was open for 11% of the time, Pallas kernels for 0%

profile of v1, /device:TPU:1, one launch (start us, length us, event | category | flops | bytes accessed | tf_op | source)
XLA Modules:
  0.0 194.7 jit_solution(17095570253524024710)
XLA Ops:
  7.5 2.2 %collective-permute-start.16 = (f32[14,512]{1,0:T(8,128)S(1)}, f32[14,512]{1,0:T(8,128)}, u32[]{:S(2)}, u32[]{:S(2)}) collective-permute-start(f32[14,512]{1,0:T(8,128)S(1)} %pad_maximum_fusion.5), channel_id=1, source_target_pairs={{0,16},{1,17},{2,18},{3,19},{4,20},{5,21},{6,22},{7,23},{8,24},{9,... | collective-permute-start | bytes 86024 | tf_op jit(solution)/shard_map/ppermute | solution.py:12
  9.7 5.6 %collective-permute-start.5 = (f32[16,512]{1,0:T(8,128)}, f32[16,512]{1,0:T(8,128)S(1)}, u32[]{:S(2)}, u32[]{:S(2)}) collective-permute-start(f32[16,512]{1,0:T(8,128)} %param.24), channel_id=1, source_target_pairs={{0,14},{1,15},{2,12},{3,13},{4,10},{5,11},{6,8},{7,9},{8,6},{9,7},... | collective-permute-start | bytes 98312 | tf_op jit(solution)/shard_map/ppermute | solution.py:12
  15.3 4.4 %fusion.83 = f32[64,1024]{1,0:T(8,128)S(1)} fusion(f32[64,1024]{1,0:T(8,128)} %param.14, f32[1024,1024]{1,0:T(8,128)} %param.15), kind=kOutput, calls=%fused_computation.124 | convolution fusion | flops 402653184 | bytes 4718592 | tf_op jit(solution)/shard_map/dot_general | solution.py:16
  29.5 2.2 %collective-permute-start.6 = (f32[32,512]{1,0:T(8,128)S(1)}, f32[32,512]{1,0:T(8,128)S(1)}, u32[]{:S(2)}, u32[]{:S(2)}) collective-permute-start(f32[32,512]{1,0:T(8,128)S(1)} %maximum_select_fusion.10), channel_id=1, source_target_pairs={{0,4},{1,5},{2,6},{3,7},{4,0},{5,1},{6,2},{7,3},{8,12},{9,13},{10,... | collective-permute-start | bytes 196616 | tf_op jit(solution)/shard_map/ppermute | solution.py:12
  39.6 3.3 %collective-permute-done.3 = f32[32,256]{1,0:T(8,128)S(1)} collective-permute-done((f32[32,256]{1,0:T(8,128)S(1)}, f32[32,256]{1,0:T(8,128)S(1)}, u32[]{:S(2)}, u32[]{:S(2)}) %collective-permute-start.3) | collective-permute-done | bytes 32800 | tf_op jit(solution)/shard_map/ppermute | solution.py:12
  43.4 4.6 %collective-permute-start.8 = (f32[128,512]{1,0:T(8,128)S(1)}, f32[128,512]{1,0:T(8,128)S(1)}, u32[]{:S(2)}, u32[]{:S(2)}) collective-permute-start(f32[128,512]{1,0:T(8,128)S(1)} %maximum_select_fusion.3), channel_id=1, source_target_pairs={{0,1},{1,0},{2,3},{3,2},{4,5},{5,4},{6,7},{7,6},{8,9},{9,8},{10,11... | collective-permute-start | bytes 786440 | tf_op jit(solution)/shard_map/ppermute | solution.py:12
  49.2 2.2 %collective-permute-start.20 = (f32[64,768]{0,1:T(8,128)S(1)}, f32[64,768]{0,1:T(8,128)S(1)}, u32[]{:S(2)}, u32[]{:S(2)}) collective-permute-start(f32[64,768]{0,1:T(8,128)S(1)} %slice_select_fusion.1), channel_id=1, source_target_pairs={{0,2},{1,3},{2,0},{3,1},{4,6},{5,7},{6,4},{7,5},{8,10},{9,11},{10,... | collective-permute-start | bytes 589832 | tf_op jit(solution)/shard_map/ppermute | solution.py:12
  51.5 12.7 %collective-permute-done.20 = f32[64,768]{0,1:T(8,128)S(1)} collective-permute-done((f32[64,768]{0,1:T(8,128)S(1)}, f32[64,768]{0,1:T(8,128)S(1)}, u32[]{:S(2)}, u32[]{:S(2)}) %collective-permute-start.20) | collective-permute-done | bytes 196640 | tf_op jit(solution)/shard_map/ppermute | solution.py:12
  66.2 21.3 %collective-permute-done.21 = f32[32,768]{0,1:T(8,128)S(1)} collective-permute-done((f32[32,768]{0,1:T(8,128)S(1)}, f32[32,768]{0,1:T(8,128)S(1)}, u32[]{:S(2)}, u32[]{:S(2)}) %collective-permute-start.21) | collective-permute-done | bytes 98336 | tf_op jit(solution)/shard_map/ppermute | solution.py:12
  89.2 18.2 %collective-permute-done.22 = f32[32,768]{0,1:T(8,128)S(1)} collective-permute-done((f32[32,768]{0,1:T(8,128)S(1)}, f32[32,768]{0,1:T(8,128)S(1)}, u32[]{:S(2)}, u32[]{:S(2)}) %collective-permute-start.22) | collective-permute-done | bytes 98336 | tf_op jit(solution)/shard_map/ppermute | solution.py:12
  109.4 8.4 %collective-permute-done.23 = f32[32,768]{0,1:T(8,128)S(1)} collective-permute-done((f32[32,768]{0,1:T(8,128)S(1)}, f32[32,768]{0,1:T(8,128)S(1)}, u32[]{:S(2)}, u32[]{:S(2)}) %collective-permute-start.23) | collective-permute-done | bytes 98336 | tf_op jit(solution)/shard_map/ppermute | solution.py:12
  120.6 2.4 %collective-permute-done.24 = f32[32,256]{0,1:T(8,128)S(1)} collective-permute-done((f32[32,256]{0,1:T(8,128)S(1)}, f32[32,256]{0,1:T(8,128)S(1)}, u32[]{:S(2)}, u32[]{:S(2)}) %collective-permute-start.24) | collective-permute-done | bytes 32800 | tf_op jit(solution)/shard_map/ppermute | solution.py:12
  123.2 2.6 %collective-permute-start.10 = (f32[32,768]{1,0:T(8,128)S(1)}, f32[32,768]{1,0:T(8,128)S(1)}, u32[]{:S(2)}, u32[]{:S(2)}) collective-permute-start(f32[32,768]{1,0:T(8,128)S(1)} %slice_select_fusion.2), channel_id=1, source_target_pairs={{0,1},{1,0},{2,3},{3,2},{4,5},{5,4},{6,7},{7,6},{8,9},{9,8},{10,11... | collective-permute-start | bytes 294920 | tf_op jit(solution)/shard_map/ppermute | solution.py:12
  125.7 2.5 %collective-permute-done.25 = f32[32,768]{1,0:T(8,128)S(1)} collective-permute-done((f32[32,768]{1,0:T(8,128)S(1)}, f32[32,768]{1,0:T(8,128)S(1)}, u32[]{:S(2)}, u32[]{:S(2)}) %collective-permute-start.25) | collective-permute-done | bytes 98336 | tf_op jit(solution)/shard_map/ppermute | solution.py:12
  130.0 3.1 %collective-permute-done.26 = f32[64,768]{1,0:T(8,128)S(1)} collective-permute-done((f32[64,768]{1,0:T(8,128)S(1)}, f32[64,768]{1,0:T(8,128)S(1)}, u32[]{:S(2)}, u32[]{:S(2)}) %collective-permute-start.26) | collective-permute-done | bytes 196640 | tf_op jit(solution)/shard_map/ppermute | solution.py:12
  133.1 4.5 %collective-permute-start.27 = (f32[128,768]{1,0:T(8,128)S(1)}, f32[128,768]{1,0:T(8,128)S(1)}, u32[]{:S(2)}, u32[]{:S(2)}) collective-permute-start(f32[128,768]{1,0:T(8,128)S(1)} %maximum_select_fusion.2), channel_id=1, source_target_pairs={{0,1},{1,0},{2,3},{3,2},{4,5},{5,4},{6,7},{7,6},{8,9},{9,8},{10,11... | collective-permute-start | bytes 1179656 | tf_op jit(solution)/shard_map/ppermute | solution.py:12
  137.8 6.7 %collective-permute-done.12 = f32[32,768]{1,0:T(8,128)S(1)} collective-permute-done((f32[32,768]{1,0:T(8,128)S(1)}, f32[32,768]{1,0:T(8,128)S(1)}, u32[]{:S(2)}, u32[]{:S(2)}) %collective-permute-start.12) | collective-permute-done | bytes 98336 | tf_op jit(solution)/shard_map/ppermute | solution.py:12
  144.6 7.3 %collective-permute-done.13 = f32[32,768]{1,0:T(8,128)S(1)} collective-permute-done((f32[32,768]{1,0:T(8,128)S(1)}, f32[32,768]{1,0:T(8,128)S(1)}, u32[]{:S(2)}, u32[]{:S(2)}) %collective-permute-start.13) | collective-permute-done | bytes 98336 | tf_op jit(solution)/shard_map/ppermute | solution.py:12
  152.0 3.4 %collective-permute-done.14 = f32[32,768]{1,0:T(8,128)S(1)} collective-permute-done((f32[32,768]{1,0:T(8,128)S(1)}, f32[32,768]{1,0:T(8,128)S(1)}, u32[]{:S(2)}, u32[]{:S(2)}) %collective-permute-start.14) | collective-permute-done | bytes 98336 | tf_op jit(solution)/shard_map/ppermute | solution.py:12
  156.6 2.3 %slice_bitcast_fusion = (f32[2,16,8,512]{3,2,0,1:T(8,128)S(1)}, f32[16,16,512]{2,1,0:T(8,128)}, f32[16,16,512]{2,1,0:T(8,128)S(1)}) fusion(f32[16,48,512]{2,1,0:T(8,128)} %bitcast.50), kind=kLoop, calls=%fused_computation.24 | loop fusion | bytes 3145728 | tf_op jit(solution)/shard_map/transpose | solution.py:95
  161.4 3.1 %collective-permute-done.28 = f32[32,512]{1,0:T(8,128)S(1)} collective-permute-done((f32[32,512]{1,0:T(8,128)S(1)}, f32[32,512]{1,0:T(8,128)S(1)}, u32[]{:S(2)}, u32[]{:S(2)}) %collective-permute-start.28) | collective-permute-done | bytes 65568 | tf_op jit(solution)/shard_map/ppermute | solution.py:12
  171.4 2.3 %collective-permute-start.31 = (f32[32,256]{1,0:T(8,128)S(1)}, f32[32,256]{1,0:T(8,128)S(1)}, u32[]{:S(2)}, u32[]{:S(2)}) collective-permute-start(f32[32,256]{1,0:T(8,128)S(1)} %add.67), channel_id=1, source_target_pairs={{0,192},{1,193},{2,194},{3,195},{4,196},{5,197},{6,198},{7,199},{8... | collective-permute-start | bytes 98312 | tf_op jit(solution)/shard_map/ppermute | solution.py:12
  176.2 6.9 %collective-permute-start.32 = (f32[32,768]{1,0:T(8,128)S(1)}, f32[32,768]{1,0:T(8,128)S(1)}, u32[]{:S(2)}, u32[]{:S(2)}) collective-permute-start(f32[32,768]{1,0:T(8,128)S(1)} %pad_maximum_fusion.4), channel_id=1, source_target_pairs={{0,1},{1,0},{2,3},{3,2},{4,5},{5,4},{6,7},{7,6},{8,9},{9,8},{10,11... | collective-permute-start | bytes 294920 | tf_op jit(solution)/shard_map/ppermute | solution.py:12
  184.0 3.8 %fusion.19 = f32[64,1024]{1,0:T(8,128)} fusion(f32[64,1024]{1,0:T(8,128)S(1)} %convolution_subtract_fusion, f32[1024,256]{1,0:T(8,128)} %param.23, f32[1024,256]{1,0:T(8,128)} %param.22, f32[1024,256]{1,0:T(8,128)S(1)} %copy-done.5, f32[32,256]{1,0:T(8,128)S(1)} %fusion.64, f32[32,256]{1,0:T(8,128)S(1)} %fusion.58, f32[32,256]{1,0:T(8,128)S(1)} %fusion.52, ...), kind=kOutput, calls=%fused_computation.17 | convolution fusion | flops 303972352 | bytes 3866625 | tf_op jit(solution)/shard_map/dot_general | solution.py:16
  (147 shorter events, 44.8 us)
Async XLA Ops:
  6.5 150.1 %all-gather.3.cloned.1.call-start = ((), (), s32[]{:S(2)}) async-start(), calls=%async_computation | async-start | bytes 1671168 | tf_op jit(solution)/shard_map/all_gather | solution.py:89
  7.5 17.8 %collective-permute-start.16 = (f32[14,512]{1,0:T(8,128)S(1)}, f32[14,512]{1,0:T(8,128)}, u32[]{:S(2)}, u32[]{:S(2)}) collective-permute-start(f32[14,512]{1,0:T(8,128)S(1)} %pad_maximum_fusion.5), channel_id=1, source_target_pairs={{0,16},{1,17},{2,18},{3,19},{4,20},{5,21},{6,22},{7,23},{8,24},{9,... | collective-permute-start | bytes 86024 | tf_op jit(solution)/shard_map/ppermute | solution.py:12
  9.7 19.8 %collective-permute-start.5 = (f32[16,512]{1,0:T(8,128)}, f32[16,512]{1,0:T(8,128)S(1)}, u32[]{:S(2)}, u32[]{:S(2)}) collective-permute-start(f32[16,512]{1,0:T(8,128)} %param.24), channel_id=1, source_target_pairs={{0,14},{1,15},{2,12},{3,13},{4,10},{5,11},{6,8},{7,9},{8,6},{9,7},... | collective-permute-start | bytes 98312 | tf_op jit(solution)/shard_map/ppermute | solution.py:12
  20.2 11.5 %collective-permute-start = (f32[32,256]{1,0:T(8,128)S(1)}, f32[32,256]{1,0:T(8,128)S(1)}, u32[]{:S(2)}, u32[]{:S(2)}) collective-permute-start(f32[32,256]{1,0:T(8,128)S(1)} %slice_select_fusion.3), channel_id=1, source_target_pairs={{0,1},{1,0},{2,3},{3,2},{4,5},{5,4},{6,7},{7,6},{8,9},{9,8},{10,11... | collective-permute-start | bytes 98312 | tf_op jit(solution)/shard_map/ppermute | solution.py:12
  25.2 22.7 %collective-permute-start.19 = (f32[128,768]{0,1:T(8,128)}, f32[128,768]{0,1:T(8,128)}, u32[]{:S(2)}, u32[]{:S(2)}) collective-permute-start(f32[128,768]{0,1:T(8,128)} %broadcast_select_fusion), channel_id=1, source_target_pairs={{0,1},{1,0},{2,3},{3,2},{4,5},{5,4},{6,7},{7,6},{8,9},{9,8},{10,11... | collective-permute-start | bytes 1179656 | tf_op jit(solution)/shard_map/ppermute | solution.py:12
  29.5 6.1 %collective-permute-start.6 = (f32[32,512]{1,0:T(8,128)S(1)}, f32[32,512]{1,0:T(8,128)S(1)}, u32[]{:S(2)}, u32[]{:S(2)}) collective-permute-start(f32[32,512]{1,0:T(8,128)S(1)} %maximum_select_fusion.10), channel_id=1, source_target_pairs={{0,4},{1,5},{2,6},{3,7},{4,0},{5,1},{6,2},{7,3},{8,12},{9,13},{10,... | collective-permute-start | bytes 196616 | tf_op jit(solution)/shard_map/ppermute | solution.py:12
  31.8 5.2 %collective-permute-start.18 = (f32[8,512]{1,0:T(8,128)S(1)}, f32[8,512]{1,0:T(8,128)S(1)}, u32[]{:S(2)}, u32[]{:S(2)}) collective-permute-start(f32[8,512]{1,0:T(8,128)S(1)} %maximum_select_fusion.23), channel_id=1, source_target_pairs={{0,64},{1,65},{2,66},{3,67},{4,68},{5,69},{6,70},{7,71},{8,72},{9,... | collective-permute-start | bytes 49160 | tf_op jit(solution)/shard_map/ppermute | solution.py:12
  35.6 7.8 %collective-permute-start.7 = (f32[64,512]{1,0:T(8,128)S(1)}, f32[64,512]{1,0:T(8,128)S(1)}, u32[]{:S(2)}, u32[]{:S(2)}) collective-permute-start(f32[64,512]{1,0:T(8,128)S(1)} %maximum_select_fusion.7), channel_id=1, source_target_pairs={{0,2},{1,3},{2,0},{3,1},{4,6},{5,7},{6,4},{7,5},{8,10},{9,11},{10,... | collective-permute-start | bytes 393224 | tf_op jit(solution)/shard_map/ppermute | solution.py:12
  42.9 44.9 %collective-permute-start.4 = (f32[32,256]{1,0:T(8,128)S(1)}, f32[32,256]{1,0:T(8,128)S(1)}, u32[]{:S(2)}, u32[]{:S(2)}) collective-permute-start(f32[32,256]{1,0:T(8,128)S(1)} %add.54), channel_id=1, source_target_pairs={{0,16},{1,17},{2,18},{3,19},{4,20},{5,21},{6,22},{7,23},{8,24},{9,... | collective-permute-start | bytes 98312 | tf_op jit(solution)/shard_map/ppermute | solution.py:12
  43.4 8.0 %collective-permute-start.8 = (f32[128,512]{1,0:T(8,128)S(1)}, f32[128,512]{1,0:T(8,128)S(1)}, u32[]{:S(2)}, u32[]{:S(2)}) collective-permute-start(f32[128,512]{1,0:T(8,128)S(1)} %maximum_select_fusion.3), channel_id=1, source_target_pairs={{0,1},{1,0},{2,3},{3,2},{4,5},{5,4},{6,7},{7,6},{8,9},{9,8},{10,11... | collective-permute-start | bytes 786440 | tf_op jit(solution)/shard_map/ppermute | solution.py:12
  49.2 15.1 %collective-permute-start.20 = (f32[64,768]{0,1:T(8,128)S(1)}, f32[64,768]{0,1:T(8,128)S(1)}, u32[]{:S(2)}, u32[]{:S(2)}) collective-permute-start(f32[64,768]{0,1:T(8,128)S(1)} %slice_select_fusion.1), channel_id=1, source_target_pairs={{0,2},{1,3},{2,0},{3,1},{4,6},{5,7},{6,4},{7,5},{8,10},{9,11},{10,... | collective-permute-start | bytes 589832 | tf_op jit(solution)/shard_map/ppermute | solution.py:12
  64.6 22.9 %collective-permute-start.21 = (f32[32,768]{0,1:T(8,128)S(1)}, f32[32,768]{0,1:T(8,128)S(1)}, u32[]{:S(2)}, u32[]{:S(2)}) collective-permute-start(f32[32,768]{0,1:T(8,128)S(1)} %slice_select_fusion), channel_id=1, source_target_pairs={{0,4},{1,5},{2,6},{3,7},{4,0},{5,1},{6,2},{7,3},{8,12},{9,13},{10,... | collective-permute-start | bytes 294920 | tf_op jit(solution)/shard_map/ppermute | solution.py:12
  87.7 19.7 %collective-permute-start.22 = (f32[32,768]{0,1:T(8,128)S(1)}, f32[32,768]{0,1:T(8,128)S(1)}, u32[]{:S(2)}, u32[]{:S(2)}) collective-permute-start(f32[32,768]{0,1:T(8,128)S(1)} %select_add_fusion), channel_id=1, source_target_pairs={{0,14},{1,15},{2,12},{3,13},{4,10},{5,11},{6,8},{7,9},{8,6},{9,7},... | collective-permute-start | bytes 294920 | tf_op jit(solution)/shard_map/ppermute | solution.py:12
  88.2 20.6 %collective-permute-start.9 = (f32[32,256]{1,0:T(8,128)S(1)}, f32[32,256]{1,0:T(8,128)S(1)}, u32[]{:S(2)}, u32[]{:S(2)}) collective-permute-start(f32[32,256]{1,0:T(8,128)S(1)} %fusion.41), channel_id=1, source_target_pairs={{0,1},{1,0},{2,3},{3,2},{4,5},{5,4},{6,7},{7,6},{8,9},{9,8},{10,11... | collective-permute-start | bytes 98312 | tf_op jit(solution)/shard_map/ppermute | solution.py:12
  107.5 10.3 %collective-permute-start.23 = (f32[32,768]{0,1:T(8,128)S(1)}, f32[32,768]{0,1:T(8,128)S(1)}, u32[]{:S(2)}, u32[]{:S(2)}) collective-permute-start(f32[32,768]{0,1:T(8,128)S(1)} %add.63), channel_id=1, source_target_pairs={{0,16},{1,17},{2,18},{3,19},{4,20},{5,21},{6,22},{7,23},{8,24},{9,... | collective-permute-start | bytes 294920 | tf_op jit(solution)/shard_map/ppermute | solution.py:12
  117.8 5.1 %collective-permute-start.24 = (f32[32,256]{0,1:T(8,128)S(1)}, f32[32,256]{0,1:T(8,128)S(1)}, u32[]{:S(2)}, u32[]{:S(2)}) collective-permute-start(f32[32,256]{0,1:T(8,128)S(1)} %slice.133), channel_id=1, source_target_pairs={{0,48},{1,49},{2,50},{3,51},{4,52},{5,53},{6,54},{7,55},{8,56},{9,... | collective-permute-start | bytes 98312 | tf_op jit(solution)/shard_map/ppermute | solution.py:12
  123.0 5.2 %collective-permute-start.25 = (f32[32,768]{1,0:T(8,128)S(1)}, f32[32,768]{1,0:T(8,128)S(1)}, u32[]{:S(2)}, u32[]{:S(2)}) collective-permute-start(f32[32,768]{1,0:T(8,128)S(1)} %pad_maximum_fusion.3), channel_id=1, source_target_pairs={{0,4},{1,5},{2,6},{3,7},{4,0},{5,1},{6,2},{7,3},{8,12},{9,13},{10,... | collective-permute-start | bytes 294920 | tf_op jit(solution)/shard_map/ppermute | solution.py:12
  123.2 5.3 %collective-permute-start.10 = (f32[32,768]{1,0:T(8,128)S(1)}, f32[32,768]{1,0:T(8,128)S(1)}, u32[]{:S(2)}, u32[]{:S(2)}) collective-permute-start(f32[32,768]{1,0:T(8,128)S(1)} %slice_select_fusion.2), channel_id=1, source_target_pairs={{0,1},{1,0},{2,3},{3,2},{4,5},{5,4},{6,7},{7,6},{8,9},{9,8},{10,11... | collective-permute-start | bytes 294920 | tf_op jit(solution)/shard_map/ppermute | solution.py:12
  128.3 4.8 %collective-permute-start.26 = (f32[64,768]{1,0:T(8,128)S(1)}, f32[64,768]{1,0:T(8,128)S(1)}, u32[]{:S(2)}, u32[]{:S(2)}) collective-permute-start(f32[64,768]{1,0:T(8,128)S(1)} %maximum_select_fusion.4), channel_id=1, source_target_pairs={{0,2},{1,3},{2,0},{3,1},{4,6},{5,7},{6,4},{7,5},{8,10},{9,11},{10,... | collective-permute-start | bytes 589832 | tf_op jit(solution)/shard_map/ppermute | solution.py:12
  128.5 9.0 %collective-permute-start.11 = (f32[32,768]{1,0:T(8,128)S(1)}, f32[32,768]{1,0:T(8,128)S(1)}, u32[]{:S(2)}, u32[]{:S(2)}) collective-permute-start(f32[32,768]{1,0:T(8,128)S(1)} %select_add_fusion.3), channel_id=1, source_target_pairs={{0,2},{1,3},{2,0},{3,1},{4,6},{5,7},{6,4},{7,5},{8,10},{9,11},{10,... | collective-permute-start | bytes 294920 | tf_op jit(solution)/shard_map/ppermute | solution.py:12
  133.1 23.4 %collective-permute-start.27 = (f32[128,768]{1,0:T(8,128)S(1)}, f32[128,768]{1,0:T(8,128)S(1)}, u32[]{:S(2)}, u32[]{:S(2)}) collective-permute-start(f32[128,768]{1,0:T(8,128)S(1)} %maximum_select_fusion.2), channel_id=1, source_target_pairs={{0,1},{1,0},{2,3},{3,2},{4,5},{5,4},{6,7},{7,6},{8,9},{9,8},{10,11... | collective-permute-start | bytes 1179656 | tf_op jit(solution)/shard_map/ppermute | solution.py:12
  137.6 6.9 %collective-permute-start.12 = (f32[32,768]{1,0:T(8,128)S(1)}, f32[32,768]{1,0:T(8,128)S(1)}, u32[]{:S(2)}, u32[]{:S(2)}) collective-permute-start(f32[32,768]{1,0:T(8,128)S(1)} %add.56), channel_id=1, source_target_pairs={{0,4},{1,5},{2,6},{3,7},{4,0},{5,1},{6,2},{7,3},{8,12},{9,13},{10,... | collective-permute-start | bytes 294920 | tf_op jit(solution)/shard_map/ppermute | solution.py:12
  144.5 7.4 %collective-permute-start.13 = (f32[32,768]{1,0:T(8,128)S(1)}, f32[32,768]{1,0:T(8,128)S(1)}, u32[]{:S(2)}, u32[]{:S(2)}) collective-permute-start(f32[32,768]{1,0:T(8,128)S(1)} %add.57), channel_id=1, source_target_pairs={{0,14},{1,15},{2,12},{3,13},{4,10},{5,11},{6,8},{7,9},{8,6},{9,7},... | collective-permute-start | bytes 294920 | tf_op jit(solution)/shard_map/ppermute | solution.py:12
  176.2 7.8 %collective-permute-start.32 = (f32[32,768]{1,0:T(8,128)S(1)}, f32[32,768]{1,0:T(8,128)S(1)}, u32[]{:S(2)}, u32[]{:S(2)}) collective-permute-start(f32[32,768]{1,0:T(8,128)S(1)} %pad_maximum_fusion.4), channel_id=1, source_target_pairs={{0,1},{1,0},{2,3},{3,2},{4,5},{5,4},{6,7},{7,6},{8,9},{9,8},{10,11... | collective-permute-start | bytes 294920 | tf_op jit(solution)/shard_map/ppermute | solution.py:12
  (23 other events, 337.9 us)
Sparse Core Ops, SparseCore 0:
  39.8 50.1 all-gather.2

commit v2 on v0

v2 whole, which is shorter than its diff:
```python
import jax
import jax.numpy as jnp
import numpy as np
from jax import lax
from jax.experimental.layout import Layout, with_layout_constraint
from jax.sharding import PartitionSpec as P

CORE, Y_A, Y_B, X_A, X_B = ([i ^ m for i in range(256)] for m in (1, 16, 48, 64, 192))


def ring_pairs(partner):
    return [i - i % 16 + 2 * partner[i // 2 % 8] + i % 2 for i in range(256)]


Z_A = ring_pairs([1, 0, 3, 2, 5, 4, 7, 6])
Z_B = ring_pairs([7, 2, 1, 4, 3, 6, 5, 0])
Z_C = ring_pairs([3, 6, 5, 0, 7, 2, 1, 4])
SIDE_A, SIDE_B, SIDE_C = 0b01100110, 0b10110100, 0b11101000
RING_ORDER = [0, 3, 4, 7, 1, 6, 2, 5]


def tree_order(groups, rows):
    size = 16 * groups * rows
    source = [
        ((group * 8 + z) * 2 + core) * rows + row
        for core in range(2)
        for group in range(groups)
        for z in RING_ORDER
        for row in range(rows)
    ]
    matrix = np.zeros((size, size), np.float32)
    matrix[np.arange(size), source] = 1
    return matrix


def by_rows(value):
    return with_layout_constraint(value, Layout(major_to_minor=(0, 1)))


def together(*values):
    return lax.optimization_barrier(values)


def swapped(value, partner):
    return lax.ppermute(value, "leaf", list(enumerate(partner)))


def sent(partner, *parts):
    got = swapped(jnp.concatenate(parts), partner)
    ends = [0]
    for part in parts:
        ends.append(ends[-1] + part.shape[0])
    return [got[first:last] for first, last in zip(ends, ends[1:])]


def product(left, right, dims, precision=lax.Precision.HIGH):
    return lax.dot_general(
        left,
        right,
        ((dims[:1], dims[1:]), ((), ())),
        precision=precision,
        preferred_element_type=jnp.float32,
    )


def product_nn(left, right):
    return product(left, right, (1, 0))


def product_nt(left, right):
    return product(left, right, (1, 1))


def product_tn(left, right):
    return product(left, right, (0, 0))


def halves(value, side, blocks=1):
    value = value.reshape(blocks, 2, -1, value.shape[1])
    kept = jnp.where(side, value[:, 1], value[:, 0])
    other = jnp.where(side, value[:, 0], value[:, 1])
    return kept.reshape(-1, value.shape[3]), other.reshape(-1, value.shape[3])


def ordered(own, other, side, blocks=1):
    width = own.shape[1]
    own, other = own.reshape(blocks, -1, width), other.reshape(blocks, -1, width)
    both = jnp.where(
        side,
        jnp.concatenate([other, own], axis=1),
        jnp.concatenate([own, other], axis=1),
    )
    return both.reshape(-1, width)


def two_halves(capacity):
    rank = capacity.shape[1] // 2
    return jnp.concatenate([capacity[:, :rank], capacity[:, rank:]])


def solved_weights(own, other, side, capacity, order):
    upper, lower = jnp.where(side, own, other), jnp.where(side, other, own)
    rank = capacity.shape[1]
    weights = product_nt(upper, capacity[:rank]) + product_nt(lower, capacity[rank:])
    return product_nn(weights, order)


def corrected(current, weights, solved, core):
    weights = ordered(weights, swapped(weights, CORE), core)
    return current - product_nt(weights, solved)


def per_device(
    right_sides,
    leaf_inverse,
    coupling_first,
    coupling_second,
    coupling_third,
    coupling_fourth,
    solved_first,
    solved_second,
    solved_third,
    solved_fourth,
    first_level_inverse,
    second_level_inverse,
    third_level_inverse,
    root_level_inverse,
):
    rank = coupling_first.shape[1]
    device_id = lax.axis_index("leaf")
    core, y_low, y_high, x_low, x_high = (
        (device_id >> place) & 1 == 1 for place in (0, 4, 5, 6, 7)
    )
    z = (device_id >> 1) & 7
    side_a, side_b, side_c = ((side >> z) & 1 == 1 for side in (SIDE_A, SIDE_B, SIDE_C))
    y_side = y_low != y_high
    sizes = [
        level.shape[0]
        for level in (second_level_inverse, third_level_inverse, root_level_inverse)
    ]
    orders = [
        jnp.asarray(tree_order(2**level, first_level_inverse.shape[0] >> level))
        for level in range(4)
    ]

    current = product_nt(right_sides, leaf_inverse)
    kept, away = halves(product_nn(current, coupling_first), core)

    away, *inputs = together(
        away,
        first_level_inverse,
        second_level_inverse,
        third_level_inverse,
        root_level_inverse,
        solved_second,
        solved_third,
    )
    sums = kept + swapped(away, CORE)
    near = two_halves(inputs[0])
    far = jnp.zeros((first_level_inverse.shape[0] - sum(sizes), 2 * rank), jnp.float32)
    far = two_halves(jnp.concatenate([*inputs[1:4], far]))
    cross = by_rows(
        jnp.concatenate(
            [
                product_tn(inputs[4], coupling_third),
                product_tn(inputs[4], coupling_fourth),
                product_tn(inputs[5], coupling_fourth),
            ]
        )
    )

    sums, near, far = together(sums, near, far)
    other, near_other, far_other = sent(Z_C, sums, near, far)
    cross, cross_away = halves(cross, core, 3)
    cross = cross + swapped(cross_away, CORE)
    sums = sums + other
    near, far = ordered(near, near_other, side_c, 2), ordered(far, far_other, side_c, 2)

    cross, cross_away = halves(cross, y_side, 3)
    sums, near, far, cross_away = together(sums, near, far, cross_away)
    other, near_other, far_other = sent(Z_B, sums, near, far)
    cross = cross + swapped(cross_away, Y_A)
    sums = sums + other
    near, far = ordered(near, near_other, side_b, 2), ordered(far, far_other, side_b, 2)

    sums, near, cross = together(sums, near, cross)
    other, near_other = sent(Z_A, sums, near)
    last = cross.shape[0] // 3 * 2
    cross = jnp.concatenate([cross[:last], cross[last:] + swapped(cross[last:], Y_B)])
    sums, near = sums + other, ordered(near, near_other, side_a, 2)

    cross, cross_away = halves(cross, side_a, 3)
    sums, near, cross_away = together(sums, near, cross_away)
    other = swapped(sums, Y_A)
    near = ordered(near, swapped(near, CORE), core, 2)
    cross = cross + swapped(cross_away, Z_A)
    first = solved_weights(sums, other, y_low, near, orders[0])

    cross, cross_away = halves(cross, side_b, 3)
    first, cross_away, far = together(first, cross_away, far)
    cross_other = swapped(cross_away, Z_B)
    far_other = swapped(far, Z_A)
    current = corrected(current, first, solved_first, core)

    sums = [
        product_nn(current, coupling)
        for coupling in (coupling_second, coupling_third, coupling_fourth)
    ]
    kept, away = halves(jnp.concatenate(sums), core, 3)
    cross = cross + cross_other
    far = ordered(far, far_other, side_a, 2).reshape(16, -1, rank)
    ends = [0, sizes[0], sizes[0] + sizes[1], sum(sizes)]
    far = [far[:, a:b].reshape(-1, rank) for a, b in zip(ends, ends[1:])]

    away, cross, *far = together(away, cross, *far)
    sums = kept + swapped(away, CORE)
    share = sums.shape[0] // 3
    cross_other = swapped(cross, Z_C)
    far_other = sent(Y_A, *far)

    sums, = together(sums)
    sums = sums + swapped(sums, Z_A)

    cross = cross + cross_other
    far = [ordered(own, got, y_low, 2) for own, got in zip(far, far_other)]
    sums, cross, *far = together(sums, cross, *far)
    other, cross_other = sent(Z_B, sums, cross)
    far_other = sent(Y_B, *far[1:])
    sums, cross = sums + other, ordered(cross, cross_other, side_b, 3)

    far[1:] = [ordered(own, got, y_high, 2) for own, got in zip(far[1:], far_other)]
    sums, cross, *far = together(sums, cross, *far)
    other = swapped(sums, Z_C)
    cross = ordered(cross, swapped(cross, Z_A), side_a, 3)
    far[0] = ordered(far[0], swapped(far[0], CORE), core, 2)
    sums = sums + other

    sums, cross, *far = together(sums, cross, *far)
    other = swapped(sums, Y_A)
    cross = ordered(cross, swapped(cross, Y_A), y_side, 3)
    far_other = swapped(far[2], X_A)
    far[1] = ordered(far[1], swapped(far[1], CORE), core, 2)
    sums = sums + other

    sums, cross, *far = together(sums, cross, *far)
    own = sums[:share]
    other = swapped(own, Y_B)
    cross = ordered(cross, swapped(cross, CORE), core, 3)
    second = solved_weights(own, other, y_high, far[0], orders[1])
    sums = sums[share:] - jnp.concatenate(
        [product_nn(second, cross[:rank]), product_nn(second, cross[rank : 2 * rank])]
    )

    sums, second, cross, *far = together(sums, second, cross, far[1], far[2], far_other)
    sums = sums + swapped(sums, Y_B)
    capacity = ordered(far[1], far[2], x_low, 2)
    capacity = ordered(capacity, swapped(capacity, CORE), core, 2)
    current = corrected(current, second, solved_second, core)

    sums, current, capacity = together(sums, current, capacity)
    own = sums[:share]
    third = solved_weights(own, swapped(own, X_A), x_low, far[0], orders[2])
    sums = sums[share:] - product_nn(third, cross[2 * rank :])

    sums, third = together(sums, third)
    sums = sums + swapped(sums, X_A)
    current = corrected(current, third, solved_third, core)

    sums, current = together(sums, current)
    fourth = solved_weights(sums, swapped(sums, X_B), x_high, capacity, orders[3])
    return corrected(current, fourth, solved_fourth, core)


def solution(mesh):
    in_specs = (P(None, "leaf"),) + (P("leaf", None),) * 13
    return jax.shard_map(
        per_device,
        mesh=mesh,
        in_specs=in_specs,
        out_specs=P(None, "leaf"),
        check_vma=False,
    )
```

time: 252 us -> 124 us (0.49)
  the two profiles are of different devices: /device:TPU:18 before, /device:TPU:1 now
where the time goes in v2:
time: 124 us
  starting transfers between devices  56.6 us (46%)
  waiting for transfers between devices  40.7 us (33%)
  matrix products  17.9 us (14%)
  other arithmetic  6.38 us (5%)
    ppermute x36, starting transfers between devices, swapped(): return lax.ppermute(value, 'leaf', list(enumerate(partner)))  56.6 us
    ppermute x36, waiting for transfers between devices, swapped(): return lax.ppermute(value, 'leaf', list(enumerate(partner)))  40.7 us
    dot_general x27, matrix products, product(): lax.dot_general(left, right, ((dims[:1], dims[1:]), ((), ())), precision=...  17.9 us
  transfers between devices with their start and end apart: 36, of which 24 were waited for; matrix products, arithmetic and copies ran while one was open for 9% of the time, Pallas kernels for 0%

profile of v2, /device:TPU:1, one launch (start us, length us, event | category | flops | bytes accessed | tf_op | source)
XLA Modules:
  0.0 123.7 jit_solution(4047876162216779583)
XLA Ops:
  0.1 4.5 %fusion.68 = f32[64,1024]{1,0:T(8,128)S(1)} fusion(f32[64,1024]{1,0:T(8,128)} %param.18, f32[1024,1024]{1,0:T(8,128)} %param.19), kind=kOutput, calls=%fused_computation.139 | convolution fusion | flops 402653184 | bytes 4718592 | tf_op jit(solution)/shard_map/dot_general | solution.py:57
  5.0 3.3 %collective-permute-start = (f32[32,256]{1,0:T(8,128)S(1)}, f32[32,256]{1,0:T(8,128)S(1)}, u32[]{:S(2)}, u32[]{:S(2)}) collective-permute-start(f32[32,256]{1,0:T(8,128)S(1)} %select_bitcast_fusion), channel_id=1, source_target_pairs={{0,1},{1,0},{2,3},{3,2},{4,5},{5,4},{6,7},{7,6},{8,9},{9,8},{10,11... | collective-permute-start | bytes 98312 | tf_op jit(solution)/shard_map/ppermute | solution.py:45
  11.7 2.7 %collective-permute-start.1 = (f32[96,256]{1,0:T(8,128)S(1)}, f32[96,256]{1,0:T(8,128)S(1)}, u32[]{:S(2)}, u32[]{:S(2)}) collective-permute-start(f32[96,256]{1,0:T(8,128)S(1)} %pad_maximum_fusion.8), channel_id=1, source_target_pairs={{0,6},{1,7},{2,12},{3,13},{4,10},{5,11},{6,0},{7,1},{8,14},{9,15},... | collective-permute-start | bytes 294920 | tf_op jit(solution)/shard_map/ppermute | solution.py:45
  15.7 2.3 %collective-permute-done.1 = f32[96,256]{1,0:T(8,128)S(1)} collective-permute-done((f32[96,256]{1,0:T(8,128)S(1)}, f32[96,256]{1,0:T(8,128)S(1)}, u32[]{:S(2)}, u32[]{:S(2)}) %collective-permute-start.1) | collective-permute-done | bytes 98336 | tf_op jit(solution)/shard_map/ppermute | solution.py:45
  20.0 3.9 %collective-permute-start.3 = (f32[160,256]{1,0:T(8,128)S(1)}, f32[160,256]{1,0:T(8,128)}, u32[]{:S(2)}, u32[]{:S(2)}) collective-permute-start(f32[160,256]{1,0:T(8,128)S(1)} %pad_maximum_fusion.5), channel_id=1, source_target_pairs={{0,14},{1,15},{2,4},{3,5},{4,2},{5,3},{6,8},{7,9},{8,6},{9,7},{10,... | collective-permute-start | bytes 491528 | tf_op jit(solution)/shard_map/ppermute | solution.py:45
  25.2 2.6 %collective-permute-done.3 = f32[160,256]{1,0:T(8,128)} collective-permute-done((f32[160,256]{1,0:T(8,128)S(1)}, f32[160,256]{1,0:T(8,128)}, u32[]{:S(2)}, u32[]{:S(2)}) %collective-permute-start.3) | collective-permute-done | bytes 163872 | tf_op jit(solution)/shard_map/ppermute | solution.py:45
  30.5 2.8 %collective-permute-start.6 = (f32[64,256]{1,0:T(8,128)S(1)}, f32[64,256]{1,0:T(8,128)S(1)}, u32[]{:S(2)}, u32[]{:S(2)}) collective-permute-start(f32[64,256]{1,0:T(8,128)S(1)} %slice.196), channel_id=1, source_target_pairs={{0,48},{1,49},{2,50},{3,51},{4,52},{5,53},{6,54},{7,55},{8,56},{9,... | collective-permute-start | bytes 196616 | tf_op jit(solution)/shard_map/ppermute | solution.py:45
  35.0 2.6 %collective-permute-done.5 = f32[160,256]{1,0:T(8,128)S(1)} collective-permute-done((f32[160,256]{1,0:T(8,128)S(1)}, f32[160,256]{1,0:T(8,128)S(1)}, u32[]{:S(2)}, u32[]{:S(2)}) %collective-permute-start.5) | collective-permute-done | bytes 163872 | tf_op jit(solution)/shard_map/ppermute | solution.py:45
  37.8 3.5 %collective-permute-start.8 = (f32[256,256]{1,0:T(8,128)S(1)}, f32[256,256]{1,0:T(8,128)S(1)}, u32[]{:S(2)}, u32[]{:S(2)}) collective-permute-start(f32[256,256]{1,0:T(8,128)S(1)} %bitcast.143), channel_id=1, source_target_pairs={{0,1},{1,0},{2,3},{3,2},{4,5},{5,4},{6,7},{7,6},{8,9},{9,8},{10,11... | collective-permute-start | bytes 786440 | tf_op jit(solution)/shard_map/ppermute | solution.py:45
  42.5 1.9 %collective-permute-done.7 = f32[32,256]{1,0:T(8,128)S(1)} collective-permute-done((f32[32,256]{1,0:T(8,128)S(1)}, f32[32,256]{1,0:T(8,128)S(1)}, u32[]{:S(2)}, u32[]{:S(2)}) %collective-permute-start.7) | collective-permute-done | bytes 32800 | tf_op jit(solution)/shard_map/ppermute | solution.py:45
  46.7 2.8 %collective-permute-start.11 = (f32[48,256]{1,0:T(8,128)S(1)}, f32[48,256]{1,0:T(8,128)S(1)}, u32[]{:S(2)}, u32[]{:S(2)}) collective-permute-start(f32[48,256]{1,0:T(8,128)S(1)} %bitcast.188), channel_id=1, source_target_pairs={{0,14},{1,15},{2,4},{3,5},{4,2},{5,3},{6,8},{7,9},{8,6},{9,7},{10,... | collective-permute-start | bytes 147464 | tf_op jit(solution)/shard_map/ppermute | solution.py:45
  58.6 3.6 %collective-permute-done.15 = f32[48,256]{1,0:T(8,128)S(1)} collective-permute-done((f32[48,256]{1,0:T(8,128)S(1)}, f32[48,256]{1,0:T(8,128)S(1)}, u32[]{:S(2)}, u32[]{:S(2)}) %collective-permute-start.15) | collective-permute-done | bytes 49184 | tf_op jit(solution)/shard_map/ppermute | solution.py:45
  63.6 5.4 %collective-permute-done.17 = f32[144,256]{1,0:T(8,128)S(1)} collective-permute-done((f32[144,256]{1,0:T(8,128)S(1)}, f32[144,256]{1,0:T(8,128)S(1)}, u32[]{:S(2)}, u32[]{:S(2)}) %collective-permute-start.17) | collective-permute-done | bytes 147488 | tf_op jit(solution)/shard_map/ppermute | solution.py:45
  69.8 2.5 %collective-permute-start.21 = (f32[256,256]{1,0:T(8,128)S(1)}, f32[256,256]{1,0:T(8,128)S(1)}, u32[]{:S(2)}, u32[]{:S(2)}) collective-permute-start(f32[256,256]{1,0:T(8,128)S(1)} %bitcast.141), channel_id=1, source_target_pairs={{0,1},{1,0},{2,3},{3,2},{4,5},{5,4},{6,7},{7,6},{8,9},{9,8},{10,11... | collective-permute-start | bytes 786440 | tf_op jit(solution)/shard_map/ppermute | solution.py:45
  72.3 2.6 %collective-permute-start.19 = (f32[96,256]{1,0:T(8,128)S(1)}, f32[96,256]{1,0:T(8,128)S(1)}, u32[]{:S(2)}, u32[]{:S(2)}) collective-permute-start(f32[96,256]{1,0:T(8,128)S(1)} %slice_add_fusion), channel_id=1, source_target_pairs={{0,6},{1,7},{2,12},{3,13},{4,10},{5,11},{6,0},{7,1},{8,14},{9,15},... | collective-permute-start | bytes 294920 | tf_op jit(solution)/shard_map/ppermute | solution.py:45
  74.8 2.8 %collective-permute-start.20 = (f32[96,256]{1,0:T(8,128)S(1)}, f32[96,256]{1,0:T(8,128)S(1)}, u32[]{:S(2)}, u32[]{:S(2)}) collective-permute-start(f32[96,256]{1,0:T(8,128)S(1)} %bitcast.163), channel_id=1, source_target_pairs={{0,2},{1,3},{2,0},{3,1},{4,6},{5,7},{6,4},{7,5},{8,10},{9,11},{10,... | collective-permute-start | bytes 294920 | tf_op jit(solution)/shard_map/ppermute | solution.py:45
  78.5 4.2 %collective-permute-done.20 = f32[96,256]{1,0:T(8,128)S(1)} collective-permute-done((f32[96,256]{1,0:T(8,128)S(1)}, f32[96,256]{1,0:T(8,128)S(1)}, u32[]{:S(2)}, u32[]{:S(2)}) %collective-permute-start.20) | collective-permute-done | bytes 98336 | tf_op jit(solution)/shard_map/ppermute | solution.py:45
  85.4 5.0 %collective-permute-done.22 = f32[96,256]{1,0:T(8,128)S(1)} collective-permute-done((f32[96,256]{1,0:T(8,128)S(1)}, f32[96,256]{1,0:T(8,128)S(1)}, u32[]{:S(2)}, u32[]{:S(2)}) %collective-permute-start.22) | collective-permute-done | bytes 98336 | tf_op jit(solution)/shard_map/ppermute | solution.py:45
  92.0 2.2 %collective-permute-start.26 = (f32[384,256]{1,0:T(8,128)S(1)}, f32[384,256]{1,0:T(8,128)S(1)}, u32[]{:S(2)}, u32[]{:S(2)}) collective-permute-start(f32[384,256]{1,0:T(8,128)S(1)} %bitcast.136), channel_id=1, source_target_pairs={{0,1},{1,0},{2,3},{3,2},{4,5},{5,4},{6,7},{7,6},{8,9},{9,8},{10,11... | collective-permute-start | bytes 1179656 | tf_op jit(solution)/shard_map/ppermute | solution.py:45
  96.1 2.8 %collective-permute-start.28 = (f32[64,256]{1,0:T(8,128)S(1)}, f32[64,256]{1,0:T(8,128)S(1)}, u32[]{:S(2)}, u32[]{:S(2)}) collective-permute-start(f32[64,256]{1,0:T(8,128)S(1)} %maximum_subtract_fusion), channel_id=1, source_target_pairs={{0,48},{1,49},{2,50},{3,51},{4,52},{5,53},{6,54},{7,55},{8,56},{9,... | collective-permute-start | bytes 196616 | tf_op jit(solution)/shard_map/ppermute | solution.py:45
  98.9 1.8 %collective-permute-start.29 = (f32[32,256]{1,0:T(8,128)S(1)}, f32[32,256]{1,0:T(8,128)S(1)}, u32[]{:S(2)}, u32[]{:S(2)}) collective-permute-start(f32[32,256]{1,0:T(8,128)S(1)} %fusion.77), channel_id=1, source_target_pairs={{0,1},{1,0},{2,3},{3,2},{4,5},{5,4},{6,7},{7,6},{8,9},{9,8},{10,11... | collective-permute-start | bytes 98312 | tf_op jit(solution)/shard_map/ppermute | solution.py:45
  107.2 3.4 %collective-permute-start.33 = (f32[32,256]{1,0:T(8,128)S(1)}, f32[32,256]{1,0:T(8,128)S(1)}, u32[]{:S(2)}, u32[]{:S(2)}) collective-permute-start(f32[32,256]{1,0:T(8,128)S(1)} %fusion.78), channel_id=1, source_target_pairs={{0,1},{1,0},{2,3},{3,2},{4,5},{5,4},{6,7},{7,6},{8,9},{9,8},{10,11... | collective-permute-start | bytes 98312 | tf_op jit(solution)/shard_map/ppermute | solution.py:45
  113.4 2.5 %collective-permute-start.34 = (f32[32,256]{1,0:T(8,128)S(1)}, f32[32,256]{1,0:T(8,128)S(1)}, u32[]{:S(2)}, u32[]{:S(2)}) collective-permute-start(f32[32,256]{1,0:T(8,128)S(1)} %add.82), channel_id=1, source_target_pairs={{0,192},{1,193},{2,194},{3,195},{4,196},{5,197},{6,198},{7,199},{8... | collective-permute-start | bytes 98312 | tf_op jit(solution)/shard_map/ppermute | solution.py:45
  119.0 2.5 %collective-permute-start.35 = (f32[32,256]{1,0:T(8,128)S(1)}, f32[32,256]{1,0:T(8,128)S(1)}, u32[]{:S(2)}, u32[]{:S(2)}) collective-permute-start(f32[32,256]{1,0:T(8,128)S(1)} %fusion.79), channel_id=1, source_target_pairs={{0,1},{1,0},{2,3},{3,2},{4,5},{5,4},{6,7},{7,6},{8,9},{9,8},{10,11... | collective-permute-start | bytes 98312 | tf_op jit(solution)/shard_map/ppermute | solution.py:45
  (185 shorter events, 48.7 us)
Async XLA Ops:
  5.0 6.7 %collective-permute-start = (f32[32,256]{1,0:T(8,128)S(1)}, f32[32,256]{1,0:T(8,128)S(1)}, u32[]{:S(2)}, u32[]{:S(2)}) collective-permute-start(f32[32,256]{1,0:T(8,128)S(1)} %select_bitcast_fusion), channel_id=1, source_target_pairs={{0,1},{1,0},{2,3},{3,2},{4,5},{5,4},{6,7},{7,6},{8,9},{9,8},{10,11... | collective-permute-start | bytes 98312 | tf_op jit(solution)/shard_map/ppermute | solution.py:45
  11.7 6.3 %collective-permute-start.1 = (f32[96,256]{1,0:T(8,128)S(1)}, f32[96,256]{1,0:T(8,128)S(1)}, u32[]{:S(2)}, u32[]{:S(2)}) collective-permute-start(f32[96,256]{1,0:T(8,128)S(1)} %pad_maximum_fusion.8), channel_id=1, source_target_pairs={{0,6},{1,7},{2,12},{3,13},{4,10},{5,11},{6,0},{7,1},{8,14},{9,15},... | collective-permute-start | bytes 294920 | tf_op jit(solution)/shard_map/ppermute | solution.py:45
  20.0 7.8 %collective-permute-start.3 = (f32[160,256]{1,0:T(8,128)S(1)}, f32[160,256]{1,0:T(8,128)}, u32[]{:S(2)}, u32[]{:S(2)}) collective-permute-start(f32[160,256]{1,0:T(8,128)S(1)} %pad_maximum_fusion.5), channel_id=1, source_target_pairs={{0,14},{1,15},{2,4},{3,5},{4,2},{5,3},{6,8},{7,9},{8,6},{9,7},{10,... | collective-permute-start | bytes 491528 | tf_op jit(solution)/shard_map/ppermute | solution.py:45
  23.9 5.5 %collective-permute-start.4 = (f32[192,256]{1,0:T(8,128)}, f32[192,256]{1,0:T(8,128)S(1)}, u32[]{:S(2)}, u32[]{:S(2)}) collective-permute-start(f32[192,256]{1,0:T(8,128)} %bitcast.178), channel_id=1, source_target_pairs={{0,16},{1,17},{2,18},{3,19},{4,20},{5,21},{6,22},{7,23},{8,24},{9,... | collective-permute-start | bytes 589832 | tf_op jit(solution)/shard_map/ppermute | solution.py:45
  30.5 4.5 %collective-permute-start.6 = (f32[64,256]{1,0:T(8,128)S(1)}, f32[64,256]{1,0:T(8,128)S(1)}, u32[]{:S(2)}, u32[]{:S(2)}) collective-permute-start(f32[64,256]{1,0:T(8,128)S(1)} %slice.196), channel_id=1, source_target_pairs={{0,48},{1,49},{2,50},{3,51},{4,52},{5,53},{6,54},{7,55},{8,56},{9,... | collective-permute-start | bytes 196616 | tf_op jit(solution)/shard_map/ppermute | solution.py:45
  33.3 4.3 %collective-permute-start.5 = (f32[160,256]{1,0:T(8,128)S(1)}, f32[160,256]{1,0:T(8,128)S(1)}, u32[]{:S(2)}, u32[]{:S(2)}) collective-permute-start(f32[160,256]{1,0:T(8,128)S(1)} %pad_maximum_fusion.6), channel_id=1, source_target_pairs={{0,2},{1,3},{2,0},{3,1},{4,6},{5,7},{6,4},{7,5},{8,10},{9,11},{10,... | collective-permute-start | bytes 491528 | tf_op jit(solution)/shard_map/ppermute | solution.py:45
  37.8 4.6 %collective-permute-start.8 = (f32[256,256]{1,0:T(8,128)S(1)}, f32[256,256]{1,0:T(8,128)S(1)}, u32[]{:S(2)}, u32[]{:S(2)}) collective-permute-start(f32[256,256]{1,0:T(8,128)S(1)} %bitcast.143), channel_id=1, source_target_pairs={{0,1},{1,0},{2,3},{3,2},{4,5},{5,4},{6,7},{7,6},{8,9},{9,8},{10,11... | collective-permute-start | bytes 786440 | tf_op jit(solution)/shard_map/ppermute | solution.py:45
  45.1 4.8 %collective-permute-start.10 = (f32[32,256]{1,0:T(8,128)S(1)}, f32[32,256]{1,0:T(8,128)S(1)}, u32[]{:S(2)}, u32[]{:S(2)}) collective-permute-start(f32[32,256]{1,0:T(8,128)S(1)} %fusion.73), channel_id=1, source_target_pairs={{0,1},{1,0},{2,3},{3,2},{4,5},{5,4},{6,7},{7,6},{8,9},{9,8},{10,11... | collective-permute-start | bytes 98312 | tf_op jit(solution)/shard_map/ppermute | solution.py:45
  46.7 6.0 %collective-permute-start.11 = (f32[48,256]{1,0:T(8,128)S(1)}, f32[48,256]{1,0:T(8,128)S(1)}, u32[]{:S(2)}, u32[]{:S(2)}) collective-permute-start(f32[48,256]{1,0:T(8,128)S(1)} %bitcast.188), channel_id=1, source_target_pairs={{0,14},{1,15},{2,4},{3,5},{4,2},{5,3},{6,8},{7,9},{8,6},{9,7},{10,... | collective-permute-start | bytes 147464 | tf_op jit(solution)/shard_map/ppermute | solution.py:45
  49.5 4.5 %collective-permute-start.12 = (f32[128,256]{1,0:T(8,128)S(1)}, f32[128,256]{1,0:T(8,128)S(1)}, u32[]{:S(2)}, u32[]{:S(2)}) collective-permute-start(f32[128,256]{1,0:T(8,128)S(1)} %bitcast.158), channel_id=1, source_target_pairs={{0,2},{1,3},{2,0},{3,1},{4,6},{5,7},{6,4},{7,5},{8,10},{9,11},{10,... | collective-permute-start | bytes 393224 | tf_op jit(solution)/shard_map/ppermute | solution.py:45
  55.7 7.3 %collective-permute-start.16 = (f32[224,256]{1,0:T(8,128)S(1)}, f32[224,256]{1,0:T(8,128)S(1)}, u32[]{:S(2)}, u32[]{:S(2)}) collective-permute-start(f32[224,256]{1,0:T(8,128)S(1)} %pad_maximum_fusion.1), channel_id=1, source_target_pairs={{0,16},{1,17},{2,18},{3,19},{4,20},{5,21},{6,22},{7,23},{8,24},{9,... | collective-permute-start | bytes 688136 | tf_op jit(solution)/shard_map/ppermute | solution.py:45
  56.6 5.6 %collective-permute-start.14 = (f32[96,256]{1,0:T(8,128)S(1)}, f32[96,256]{1,0:T(8,128)S(1)}, u32[]{:S(2)}, u32[]{:S(2)}) collective-permute-start(f32[96,256]{1,0:T(8,128)S(1)} %bitcast_add_fusion.2), channel_id=1, source_target_pairs={{0,2},{1,3},{2,0},{3,1},{4,6},{5,7},{6,4},{7,5},{8,10},{9,11},{10,... | collective-permute-start | bytes 294920 | tf_op jit(solution)/shard_map/ppermute | solution.py:45
  57.1 5.1 %collective-permute-start.15 = (f32[48,256]{1,0:T(8,128)S(1)}, f32[48,256]{1,0:T(8,128)S(1)}, u32[]{:S(2)}, u32[]{:S(2)}) collective-permute-start(f32[48,256]{1,0:T(8,128)S(1)} %bitcast_add_fusion.4), channel_id=1, source_target_pairs={{0,6},{1,7},{2,12},{3,13},{4,10},{5,11},{6,0},{7,1},{8,14},{9,15},... | collective-permute-start | bytes 147464 | tf_op jit(solution)/shard_map/ppermute | solution.py:45
  63.1 5.9 %collective-permute-start.17 = (f32[144,256]{1,0:T(8,128)S(1)}, f32[144,256]{1,0:T(8,128)S(1)}, u32[]{:S(2)}, u32[]{:S(2)}) collective-permute-start(f32[144,256]{1,0:T(8,128)S(1)} %pad_maximum_fusion.7), channel_id=1, source_target_pairs={{0,14},{1,15},{2,4},{3,5},{4,2},{5,3},{6,8},{7,9},{8,6},{9,7},{10,... | collective-permute-start | bytes 442376 | tf_op jit(solution)/shard_map/ppermute | solution.py:45
  63.5 6.2 %collective-permute-start.18 = (f32[192,256]{1,0:T(8,128)S(1)}, f32[192,256]{1,0:T(8,128)S(1)}, u32[]{:S(2)}, u32[]{:S(2)}) collective-permute-start(f32[192,256]{1,0:T(8,128)S(1)} %pad_maximum_fusion.4), channel_id=1, source_target_pairs={{0,48},{1,49},{2,50},{3,51},{4,52},{5,53},{6,54},{7,55},{8,56},{9,... | collective-permute-start | bytes 589832 | tf_op jit(solution)/shard_map/ppermute | solution.py:45
  69.8 12.9 %collective-permute-start.21 = (f32[256,256]{1,0:T(8,128)S(1)}, f32[256,256]{1,0:T(8,128)S(1)}, u32[]{:S(2)}, u32[]{:S(2)}) collective-permute-start(f32[256,256]{1,0:T(8,128)S(1)} %bitcast.141), channel_id=1, source_target_pairs={{0,1},{1,0},{2,3},{3,2},{4,5},{5,4},{6,7},{7,6},{8,9},{9,8},{10,11... | collective-permute-start | bytes 786440 | tf_op jit(solution)/shard_map/ppermute | solution.py:45
  72.3 6.2 %collective-permute-start.19 = (f32[96,256]{1,0:T(8,128)S(1)}, f32[96,256]{1,0:T(8,128)S(1)}, u32[]{:S(2)}, u32[]{:S(2)}) collective-permute-start(f32[96,256]{1,0:T(8,128)S(1)} %slice_add_fusion), channel_id=1, source_target_pairs={{0,6},{1,7},{2,12},{3,13},{4,10},{5,11},{6,0},{7,1},{8,14},{9,15},... | collective-permute-start | bytes 294920 | tf_op jit(solution)/shard_map/ppermute | solution.py:45
  74.8 7.8 %collective-permute-start.20 = (f32[96,256]{1,0:T(8,128)S(1)}, f32[96,256]{1,0:T(8,128)S(1)}, u32[]{:S(2)}, u32[]{:S(2)}) collective-permute-start(f32[96,256]{1,0:T(8,128)S(1)} %bitcast.163), channel_id=1, source_target_pairs={{0,2},{1,3},{2,0},{3,1},{4,6},{5,7},{6,4},{7,5},{8,10},{9,11},{10,... | collective-permute-start | bytes 294920 | tf_op jit(solution)/shard_map/ppermute | solution.py:45
  82.7 7.8 %collective-permute-start.23 = (f32[192,256]{1,0:T(8,128)S(1)}, f32[192,256]{1,0:T(8,128)S(1)}, u32[]{:S(2)}, u32[]{:S(2)}) collective-permute-start(f32[192,256]{1,0:T(8,128)S(1)} %bitcast.150), channel_id=1, source_target_pairs={{0,16},{1,17},{2,18},{3,19},{4,20},{5,21},{6,22},{7,23},{8,24},{9,... | collective-permute-start | bytes 589832 | tf_op jit(solution)/shard_map/ppermute | solution.py:45
  82.8 7.7 %collective-permute-start.24 = (f32[256,256]{1,0:T(8,128)S(1)}, f32[256,256]{1,0:T(8,128)S(1)}, u32[]{:S(2)}, u32[]{:S(2)}) collective-permute-start(f32[256,256]{1,0:T(8,128)S(1)} %bitcast.142), channel_id=1, source_target_pairs={{0,1},{1,0},{2,3},{3,2},{4,5},{5,4},{6,7},{7,6},{8,9},{9,8},{10,11... | collective-permute-start | bytes 786440 | tf_op jit(solution)/shard_map/ppermute | solution.py:45
  83.8 6.7 %collective-permute-start.22 = (f32[96,256]{1,0:T(8,128)S(1)}, f32[96,256]{1,0:T(8,128)S(1)}, u32[]{:S(2)}, u32[]{:S(2)}) collective-permute-start(f32[96,256]{1,0:T(8,128)S(1)} %add.77), channel_id=1, source_target_pairs={{0,16},{1,17},{2,18},{3,19},{4,20},{5,21},{6,22},{7,23},{8,24},{9,... | collective-permute-start | bytes 294920 | tf_op jit(solution)/shard_map/ppermute | solution.py:45
  90.7 5.4 %collective-permute-start.27 = (f32[128,256]{1,0:T(8,128)S(1)}, f32[128,256]{1,0:T(8,128)S(1)}, u32[]{:S(2)}, u32[]{:S(2)}) collective-permute-start(f32[128,256]{1,0:T(8,128)S(1)} %bitcast.157), channel_id=1, source_target_pairs={{0,64},{1,65},{2,66},{3,67},{4,68},{5,69},{6,70},{7,71},{8,72},{9,... | collective-permute-start | bytes 393224 | tf_op jit(solution)/shard_map/ppermute | solution.py:45
  96.1 6.0 %collective-permute-start.28 = (f32[64,256]{1,0:T(8,128)S(1)}, f32[64,256]{1,0:T(8,128)S(1)}, u32[]{:S(2)}, u32[]{:S(2)}) collective-permute-start(f32[64,256]{1,0:T(8,128)S(1)} %maximum_subtract_fusion), channel_id=1, source_target_pairs={{0,48},{1,49},{2,50},{3,51},{4,52},{5,53},{6,54},{7,55},{8,56},{9,... | collective-permute-start | bytes 196616 | tf_op jit(solution)/shard_map/ppermute | solution.py:45
  107.2 4.6 %collective-permute-start.33 = (f32[32,256]{1,0:T(8,128)S(1)}, f32[32,256]{1,0:T(8,128)S(1)}, u32[]{:S(2)}, u32[]{:S(2)}) collective-permute-start(f32[32,256]{1,0:T(8,128)S(1)} %fusion.78), channel_id=1, source_target_pairs={{0,1},{1,0},{2,3},{3,2},{4,5},{5,4},{6,7},{7,6},{8,9},{9,8},{10,11... | collective-permute-start | bytes 98312 | tf_op jit(solution)/shard_map/ppermute | solution.py:45
  (28 other events, 258.0 us)

commit v3 on v2

v3 whole, which is shorter than its diff:
```python
import jax
import jax.numpy as jnp
import numpy as np
from jax import lax
from jax.experimental.layout import Layout, with_layout_constraint
from jax.sharding import PartitionSpec as P

CORE, Y_A, Y_B, X_A, X_B = ([i ^ m for i in range(256)] for m in (1, 16, 48, 64, 192))


def ring_pairs(partner):
    return [i - i % 16 + 2 * partner[i // 2 % 8] + i % 2 for i in range(256)]


Z_A = ring_pairs([1, 0, 3, 2, 5, 4, 7, 6])
Z_B = ring_pairs([7, 2, 1, 4, 3, 6, 5, 0])
Z_C = ring_pairs([3, 6, 5, 0, 7, 2, 1, 4])
SIDE_A, SIDE_B, SIDE_C = 0b01100110, 0b10110100, 0b11101000
RING_ORDER = [0, 3, 4, 7, 1, 6, 2, 5]


def tree_order(groups, rows):
    size = 16 * groups * rows
    source = [
        ((group * 8 + z) * 2 + core) * rows + row
        for core in range(2)
        for group in range(groups)
        for z in RING_ORDER
        for row in range(rows)
    ]
    matrix = np.zeros((size, size), np.float32)
    matrix[np.arange(size), source] = 1
    return matrix


def by_rows(value):
    return with_layout_constraint(value, Layout(major_to_minor=(0, 1)))


def after(value, token):
    return lax.optimization_barrier((value, token))[0]


def swapped(value, partner):
    return lax.ppermute(value, "leaf", list(enumerate(partner)))


def sent(partner, *parts):
    got = swapped(jnp.concatenate(parts), partner)
    ends = [0]
    for part in parts:
        ends.append(ends[-1] + part.shape[0])
    return [got[first:last] for first, last in zip(ends, ends[1:])]


def product(left, right, dims, precision=lax.Precision.HIGH):
    return lax.dot_general(
        left,
        right,
        ((dims[:1], dims[1:]), ((), ())),
        precision=precision,
        preferred_element_type=jnp.float32,
    )


def product_nn(left, right):
    return product(left, right, (1, 0))


def product_nt(left, right):
    return product(left, right, (1, 1))


def product_tn(left, right):
    return product(left, right, (0, 0))


def halves(value, side, blocks=1):
    value = value.reshape(blocks, 2, -1, value.shape[1])
    kept = jnp.where(side, value[:, 1], value[:, 0])
    other = jnp.where(side, value[:, 0], value[:, 1])
    return kept.reshape(-1, value.shape[3]), other.reshape(-1, value.shape[3])


def ordered(own, other, side, blocks=1):
    width = own.shape[1]
    own, other = own.reshape(blocks, -1, width), other.reshape(blocks, -1, width)
    both = jnp.where(
        side,
        jnp.concatenate([other, own], axis=1),
        jnp.concatenate([own, other], axis=1),
    )
    return both.reshape(-1, width)


def two_halves(capacity):
    rank = capacity.shape[1] // 2
    return jnp.concatenate([capacity[:, :rank], capacity[:, rank:]])


def solved_weights(own, other, side, capacity):
    upper, lower = jnp.where(side, own, other), jnp.where(side, other, own)
    rank = capacity.shape[1]
    return product_nt(upper, capacity[:rank]) + product_nt(lower, capacity[rank:])


def corrected(current, weights, solved, core):
    weights = ordered(weights, swapped(weights, CORE), core)
    return current - product_nt(weights, solved)


def per_device(
    right_sides,
    leaf_inverse,
    coupling_first,
    coupling_second,
    coupling_third,
    coupling_fourth,
    solved_first,
    solved_second,
    solved_third,
    solved_fourth,
    first_level_inverse,
    second_level_inverse,
    third_level_inverse,
    root_level_inverse,
):
    rank = coupling_first.shape[1]
    device_id = lax.axis_index("leaf")
    core, y_low, y_high, x_low, x_high = (
        (device_id >> place) & 1 == 1 for place in (0, 4, 5, 6, 7)
    )
    z = (device_id >> 1) & 7
    side_a, side_b, side_c = ((side >> z) & 1 == 1 for side in (SIDE_A, SIDE_B, SIDE_C))
    y_side = y_low != y_high
    sizes = [
        level.shape[0]
        for level in (second_level_inverse, third_level_inverse, root_level_inverse)
    ]
    orders = [
        jnp.asarray(tree_order(2**level, first_level_inverse.shape[0] >> level))
        for level in range(4)
    ]

    current = product_nt(right_sides, leaf_inverse)
    kept, away = halves(product_nn(current, coupling_first), core)

    near = two_halves(after(first_level_inverse, away))
    far = jnp.zeros((first_level_inverse.shape[0] - sum(sizes), 2 * rank), jnp.float32)
    far = [second_level_inverse, third_level_inverse, root_level_inverse, far]
    far = two_halves(after(jnp.concatenate(far), away))
    sums = kept + swapped(away, CORE)

    other, near_other, far_other = sent(Z_C, sums, near, far)
    cross_second, cross_third = after((solved_second, solved_third), sums)
    cross = by_rows(
        jnp.concatenate(
            [
                product_tn(cross_second, coupling_third),
                product_tn(cross_second, coupling_fourth),
                product_tn(cross_third, coupling_fourth),
            ]
        )
    )
    cross, cross_away = halves(cross, core, 3)
    cross_other = swapped(cross_away, CORE)
    sums = sums + other
    near, far = ordered(near, near_other, side_c, 2), ordered(far, far_other, side_c, 2)

    other, near_other, far_other = sent(Z_B, sums, near, far)
    cross, cross_away = halves(cross + after(cross_other, sums), y_side, 3)
    cross_other = swapped(cross_away, Y_A)
    sums = sums + other
    near, far = ordered(near, near_other, side_b, 2), ordered(far, far_other, side_b, 2)

    other, near_other = sent(Z_A, sums, near)
    cross = cross + after(cross_other, sums)
    last = cross.shape[0] // 3 * 2
    cross_other = swapped(cross[last:], Y_B)
    sums, near = sums + other, ordered(near, near_other, side_a, 2)

    other = swapped(sums, Y_A)
    near = ordered(near, swapped(near, CORE), core, 2)
    cross = jnp.concatenate([cross[:last], cross[last:] + after(cross_other, sums)])
    cross, cross_away = halves(cross, side_a, 3)
    cross_other = swapped(cross_away, Z_A)
    solved_first = product_nt(after(solved_first, sums), orders[0])
    first = solved_weights(sums, other, y_low, near)

    cross, cross_away = halves(cross + after(cross_other, first), side_b, 3)
    cross_other = swapped(cross_away, Z_B)
    far_other = swapped(after(far, first), Z_A)
    current = corrected(current, first, solved_first, core)

    sums = [
        product_nn(current, coupling)
        for coupling in (coupling_second, coupling_third, coupling_fourth)
    ]
    kept, away = halves(jnp.concatenate(sums), core, 3)
    share = kept.shape[0] // 3
    sums = kept + swapped(away, CORE)

    cross = cross + after(cross_other, away)
    other, cross_other = sent(Z_C, sums, cross)
    far = ordered(far, after(far_other, sums), side_a, 2).reshape(16, -1, rank)
    ends = [0, sizes[0], sizes[0] + sizes[1], sum(sizes)]
    far = [far[:, a:b].reshape(-1, rank) for a, b in zip(ends, ends[1:])]
    far_other = sent(Y_A, *far)
    solved_fourth = product_nt(after(solved_fourth, sums), orders[3])
    sums, cross = sums + other, cross + cross_other

    other, cross_other = sent(Z_B, sums, cross)
    far_other = after(far_other, sums)
    far = [ordered(own, got, y_low, 2) for own, got in zip(far, far_other)]
    far_other = sent(Y_B, *far[1:])
    capacity_other = swapped(far[0], CORE)
    sums, cross = sums + other, ordered(cross, cross_other, side_b, 3)

    other, cross_other = sent(Z_A, sums, cross)
    capacity = [ordered(far[0], after(capacity_other, sums), core, 2)]
    far_other = after(far_other, sums)
    far = [ordered(own, got, y_high, 2) for own, got in zip(far[1:], far_other)]
    far_other = swapped(far[1], X_A)
    capacity_other = swapped(far[0], CORE)
    sums, cross = sums + other, ordered(cross, cross_other, side_a, 3)

    other = swapped(sums, Y_A)
    cross_other = swapped(cross, Y_A)
    capacity.append(ordered(far[0], after(capacity_other, sums), core, 2))
    far = ordered(far[1], after(far_other, sums), x_low, 2)
    capacity_other = swapped(far, CORE)
    sums = sums + other

    own = sums[:share]
    other = swapped(own, Y_B)
    cross = ordered(cross, after(cross_other, sums), y_side, 3)
    cross_other = swapped(cross, CORE)
    capacity.append(ordered(far, after(capacity_other, sums), core, 2))
    second = product_nn(solved_weights(own, other, y_high, capacity[0]), orders[1])
    cross = ordered(cross, after(cross_other, other), core, 3)
    sums = sums[share:] - jnp.concatenate(
        [product_nn(second, cross[:rank]), product_nn(second, cross[rank : 2 * rank])]
    )

    other = swapped(sums, Y_B)
    second_other = swapped(after(second, sums), CORE)
    sums = sums + other

    own = sums[:share]
    other = swapped(own, X_A)
    second = ordered(second, after(second_other, sums), core)
    current = current - product_nt(second, solved_second)
    third = product_nn(solved_weights(own, other, x_low, capacity[1]), orders[2])
    sums = sums[share:] - product_nn(third, cross[2 * rank :])

    other = swapped(sums, X_A)
    third_other = swapped(after(third, sums), CORE)
    sums = sums + other

    other = swapped(sums, X_B)
    third = ordered(third, after(third_other, sums), core)
    current = after(current, sums) - product_nt(third, solved_third)
    fourth = solved_weights(sums, other, x_high, capacity[2])
    return corrected(current, fourth, solved_fourth, core)


def solution(mesh):
    in_specs = (P(None, "leaf"),) + (P("leaf", None),) * 13
    return jax.shard_map(
        per_device,
        mesh=mesh,
        in_specs=in_specs,
        out_specs=P(None, "leaf"),
        check_vma=False,
    )
```

time: 124 us -> 111 us (0.90)
  waiting for transfers between devices: 40.7 us -> 21.7 us
  starting transfers between devices: 56.6 us -> 65.7 us
  other arithmetic: 6.38 us -> 3.33 us
    ppermute x36 -> x34, waiting for transfers between devices: 40.7 us -> 21.7 us  [swapped(): return lax.ppermute(value, 'leaf', list(enumerate(partner)))]
    ppermute x36 -> x34, starting transfers between devices: 56.6 us -> 65.7 us  [swapped(): return lax.ppermute(value, 'leaf', list(enumerate(partner)))]
    add x9 -> x7, other arithmetic: 2.19 us -> 0.13 us  [the longest x1 0.05 us: per_device(): cross, cross_away = halves(cross + after(cross_other, sums), y_side, 3)]
    select_n x5, other arithmetic: 1.83 us -> 0.14 us  [halves(): kept = jnp.where(side, value[:, 1], value[:, 0])]
  transfers between devices with their start and end apart: 36 -> 34, of which waited for: 24 -> 15; matrix products, arithmetic and copies ran while one was open for 9% -> 12% of each run, Pallas kernels for 0% -> 0%
where the time goes in v3:
time: 111 us; the launch traced here: 110 us
  starting transfers between devices  65.7 us (59%)
  waiting for transfers between devices  21.7 us (20%)
  matrix products  17.8 us (16%)
  other arithmetic  3.33 us (3%)
    ppermute x34, starting transfers between devices, swapped(): return lax.ppermute(value, 'leaf', list(enumerate(partner)))  65.7 us
    ppermute x34, waiting for transfers between devices, swapped(): return lax.ppermute(value, 'leaf', list(enumerate(partner)))  21.7 us
    dot_general x27, matrix products, product(): lax.dot_general(left, right, ((dims[:1], dims[1:]), ((), ())), precision=...  17.8 us
  transfers between devices with their start and end apart: 34, of which 15 were waited for; matrix products, arithmetic and copies ran while one was open for 12% of the time, Pallas kernels for 0%

profile of v3, /device:TPU:1, one launch (start us, length us, event | category | flops | bytes accessed | tf_op | source)
XLA Modules:
  0.0 110.5 jit_solution(12084175236766346080)
XLA Ops:
  0.1 4.4 %fusion.62 = f32[64,1024]{1,0:T(8,128)S(1)} fusion(f32[64,1024]{1,0:T(8,128)} %param.18, f32[1024,1024]{1,0:T(8,128)} %param.19), kind=kOutput, calls=%fused_computation.150 | convolution fusion | flops 402653184 | bytes 4718592 | tf_op jit(solution)/shard_map/dot_general | solution.py:57
  5.6 3.2 %collective-permute-start = (f32[32,256]{1,0:T(8,128)}, f32[32,256]{1,0:T(8,128)}, u32[]{:S(2)}, u32[]{:S(2)}) collective-permute-start(f32[32,256]{1,0:T(8,128)} %select_bitcast_fusion), channel_id=1, source_target_pairs={{0,1},{1,0},{2,3},{3,2},{4,5},{5,4},{6,7},{7,6},{8,9},{9,8},{10,11... | collective-permute-start | bytes 98312 | tf_op jit(solution)/shard_map/ppermute | solution.py:45
  10.9 2.7 %collective-permute-start.1 = (f32[96,256]{1,0:T(8,128)S(1)}, f32[96,256]{1,0:T(8,128)S(1)}, u32[]{:S(2)}, u32[]{:S(2)}) collective-permute-start(f32[96,256]{1,0:T(8,128)S(1)} %constant_dynamic-update-slice_fusion), channel_id=1, source_target_pairs={{0,6},{1,7},{2,12},{3,13},{4,10},{5,11},{6,0},{7,1},{8,14},{9,15},... | collective-permute-start | bytes 294920 | tf_op jit(solution)/shard_map/ppermute | solution.py:45
  13.6 2.2 %fusion.70 = f32[256,256]{1,0:T(8,128)S(1)} fusion(f32[1024,256]{1,0:T(8,128)} %param.26, f32[1024,256]{1,0:T(8,128)S(1)} %copy-done.2), kind=kOutput, calls=%fused_computation.158 | convolution fusion | flops 402653184 | bytes 2359296 | tf_op jit(solution)/shard_map/dot_general | solution.py:57
  18.0 2.9 %collective-permute-start.2 = (f32[160,256]{1,0:T(8,128)S(1)}, f32[160,256]{1,0:T(8,128)S(1)}, u32[]{:S(2)}, u32[]{:S(2)}) collective-permute-start(f32[160,256]{1,0:T(8,128)S(1)} %pad_maximum_fusion.6), channel_id=1, source_target_pairs={{0,14},{1,15},{2,4},{3,5},{4,2},{5,3},{6,8},{7,9},{8,6},{9,7},{10,... | collective-permute-start | bytes 491528 | tf_op jit(solution)/shard_map/ppermute | solution.py:45
  22.4 2.1 %collective-permute-done.2 = f32[160,256]{1,0:T(8,128)S(1)} collective-permute-done((f32[160,256]{1,0:T(8,128)S(1)}, f32[160,256]{1,0:T(8,128)S(1)}, u32[]{:S(2)}, u32[]{:S(2)}) %collective-permute-start.2) | collective-permute-done | bytes 163872 | tf_op jit(solution)/shard_map/ppermute | solution.py:45
  30.3 3.0 %collective-permute-start.5 = (f32[256,256]{1,0:T(8,128)S(1)}, f32[256,256]{1,0:T(8,128)S(1)}, u32[]{:S(2)}, u32[]{:S(2)}) collective-permute-start(f32[256,256]{1,0:T(8,128)S(1)} %bitcast.141), channel_id=1, source_target_pairs={{0,1},{1,0},{2,3},{3,2},{4,5},{5,4},{6,7},{7,6},{8,9},{9,8},{10,11... | collective-permute-start | bytes 786440 | tf_op jit(solution)/shard_map/ppermute | solution.py:45
  33.3 2.0 %collective-permute-start.10 = (f32[64,256]{1,0:T(8,128)S(1)}, f32[64,256]{1,0:T(8,128)S(1)}, u32[]{:S(2)}, u32[]{:S(2)}) collective-permute-start(f32[64,256]{1,0:T(8,128)S(1)} %slice.295), channel_id=1, source_target_pairs={{0,48},{1,49},{2,50},{3,51},{4,52},{5,53},{6,54},{7,55},{8,56},{9,... | collective-permute-start | bytes 196616 | tf_op jit(solution)/shard_map/ppermute | solution.py:45
  38.4 2.2 %collective-permute-start.6 = (f32[32,256]{1,0:T(8,128)S(1)}, f32[32,256]{1,0:T(8,128)S(1)}, u32[]{:S(2)}, u32[]{:S(2)}) collective-permute-start(f32[32,256]{1,0:T(8,128)S(1)} %convolution_add_fusion.3), channel_id=1, source_target_pairs={{0,1},{1,0},{2,3},{3,2},{4,5},{5,4},{6,7},{7,6},{8,9},{9,8},{10,11... | collective-permute-start | bytes 98312 | tf_op jit(solution)/shard_map/ppermute | solution.py:45
  45.3 2.0 %collective-permute-start.12 = (f32[48,256]{1,0:T(8,128)S(1)}, f32[48,256]{1,0:T(8,128)S(1)}, u32[]{:S(2)}, u32[]{:S(2)}) collective-permute-start(f32[48,256]{1,0:T(8,128)S(1)} %bitcast.185), channel_id=1, source_target_pairs={{0,14},{1,15},{2,4},{3,5},{4,2},{5,3},{6,8},{7,9},{8,6},{9,7},{10,... | collective-permute-start | bytes 147464 | tf_op jit(solution)/shard_map/ppermute | solution.py:45
  50.0 2.3 %collective-permute-start.13 = (f32[144,256]{1,0:T(8,128)S(1)}, f32[144,256]{1,0:T(8,128)S(1)}, u32[]{:S(2)}, u32[]{:S(2)}) collective-permute-start(f32[144,256]{1,0:T(8,128)S(1)} %pad_maximum_fusion.8), channel_id=1, source_target_pairs={{0,6},{1,7},{2,12},{3,13},{4,10},{5,11},{6,0},{7,1},{8,14},{9,15},... | collective-permute-start | bytes 442376 | tf_op jit(solution)/shard_map/ppermute | solution.py:45
  53.2 2.7 %collective-permute-done.13 = f32[144,256]{1,0:T(8,128)S(1)} collective-permute-done((f32[144,256]{1,0:T(8,128)S(1)}, f32[144,256]{1,0:T(8,128)S(1)}, u32[]{:S(2)}, u32[]{:S(2)}) %collective-permute-start.13) | collective-permute-done | bytes 147488 | tf_op jit(solution)/shard_map/ppermute | solution.py:45
  56.0 3.1 %collective-permute-start.14 = (f32[144,256]{1,0:T(8,128)S(1)}, f32[144,256]{1,0:T(8,128)S(1)}, u32[]{:S(2)}, u32[]{:S(2)}) collective-permute-start(f32[144,256]{1,0:T(8,128)S(1)} %pad_maximum_fusion.9), channel_id=1, source_target_pairs={{0,14},{1,15},{2,4},{3,5},{4,2},{5,3},{6,8},{7,9},{8,6},{9,7},{10,... | collective-permute-start | bytes 442376 | tf_op jit(solution)/shard_map/ppermute | solution.py:45
  59.2 3.7 %collective-permute-start.20 = (f32[256,256]{1,0:T(8,128)S(1)}, f32[256,256]{1,0:T(8,128)S(1)}, u32[]{:S(2)}, u32[]{:S(2)}) collective-permute-start(f32[256,256]{1,0:T(8,128)S(1)} %bitcast.140), channel_id=1, source_target_pairs={{0,1},{1,0},{2,3},{3,2},{4,5},{5,4},{6,7},{7,6},{8,9},{9,8},{10,11... | collective-permute-start | bytes 786440 | tf_op jit(solution)/shard_map/ppermute | solution.py:45
  63.7 2.5 %collective-permute-start.26 = (f32[192,256]{1,0:T(8,128)S(1)}, f32[192,256]{1,0:T(8,128)S(1)}, u32[]{:S(2)}, u32[]{:S(2)}) collective-permute-start(f32[192,256]{1,0:T(8,128)S(1)} %pad_maximum_fusion.5), channel_id=1, source_target_pairs={{0,48},{1,49},{2,50},{3,51},{4,52},{5,53},{6,54},{7,55},{8,56},{9,... | collective-permute-start | bytes 589832 | tf_op jit(solution)/shard_map/ppermute | solution.py:45
  67.1 4.4 %collective-permute-done.26 = f32[192,256]{1,0:T(8,128)S(1)} collective-permute-done((f32[192,256]{1,0:T(8,128)S(1)}, f32[192,256]{1,0:T(8,128)S(1)}, u32[]{:S(2)}, u32[]{:S(2)}) %collective-permute-start.26) | collective-permute-done | bytes 196640 | tf_op jit(solution)/shard_map/ppermute | solution.py:45
  75.5 2.2 %collective-permute-done.31 = f32[128,256]{1,0:T(8,128)S(1)} collective-permute-done((f32[128,256]{1,0:T(8,128)S(1)}, f32[128,256]{1,0:T(8,128)S(1)}, u32[]{:S(2)}, u32[]{:S(2)}) %collective-permute-start.31) | collective-permute-done | bytes 131104 | tf_op jit(solution)/shard_map/ppermute | solution.py:45
  78.0 2.5 %collective-permute-start.17 = (f32[32,256]{1,0:T(8,128)S(1)}, f32[32,256]{1,0:T(8,128)S(1)}, u32[]{:S(2)}, u32[]{:S(2)}) collective-permute-start(f32[32,256]{1,0:T(8,128)S(1)} %slice.305), channel_id=1, source_target_pairs={{0,48},{1,49},{2,50},{3,51},{4,52},{5,53},{6,54},{7,55},{8,56},{9,... | collective-permute-start | bytes 98312 | tf_op jit(solution)/shard_map/ppermute | solution.py:45
  80.5 2.2 %collective-permute-start.32 = (f32[256,256]{1,0:T(8,128)S(1)}, f32[256,256]{1,0:T(8,128)S(1)}, u32[]{:S(2)}, u32[]{:S(2)}) collective-permute-start(f32[256,256]{1,0:T(8,128)S(1)} %bitcast.139), channel_id=1, source_target_pairs={{0,1},{1,0},{2,3},{3,2},{4,5},{5,4},{6,7},{7,6},{8,9},{9,8},{10,11... | collective-permute-start | bytes 786440 | tf_op jit(solution)/shard_map/ppermute | solution.py:45
  83.1 2.4 %collective-permute-start.22 = (f32[384,256]{1,0:T(8,128)S(1)}, f32[384,256]{1,0:T(8,128)S(1)}, u32[]{:S(2)}, u32[]{:S(2)}) collective-permute-start(f32[384,256]{1,0:T(8,128)S(1)} %bitcast.134), channel_id=1, source_target_pairs={{0,1},{1,0},{2,3},{3,2},{4,5},{5,4},{6,7},{7,6},{8,9},{9,8},{10,11... | collective-permute-start | bytes 1179656 | tf_op jit(solution)/shard_map/ppermute | solution.py:45
  87.4 2.7 %collective-permute-start.24 = (f32[64,256]{1,0:T(8,128)S(1)}, f32[64,256]{1,0:T(8,128)S(1)}, u32[]{:S(2)}, u32[]{:S(2)}) collective-permute-start(f32[64,256]{1,0:T(8,128)S(1)} %slice_subtract_fusion), channel_id=1, source_target_pairs={{0,48},{1,49},{2,50},{3,51},{4,52},{5,53},{6,54},{7,55},{8,56},{9,... | collective-permute-start | bytes 196616 | tf_op jit(solution)/shard_map/ppermute | solution.py:45
  96.9 3.0 %collective-permute-start.29 = (f32[32,256]{1,0:T(8,128)S(1)}, f32[32,256]{1,0:T(8,128)S(1)}, u32[]{:S(2)}, u32[]{:S(2)}) collective-permute-start(f32[32,256]{1,0:T(8,128)S(1)} %fusion.72), channel_id=1, source_target_pairs={{0,1},{1,0},{2,3},{3,2},{4,5},{5,4},{6,7},{7,6},{8,9},{9,8},{10,11... | collective-permute-start | bytes 98312 | tf_op jit(solution)/shard_map/ppermute | solution.py:45
  99.9 1.9 %collective-permute-start.30 = (f32[32,256]{1,0:T(8,128)S(1)}, f32[32,256]{1,0:T(8,128)S(1)}, u32[]{:S(2)}, u32[]{:S(2)}) collective-permute-start(f32[32,256]{1,0:T(8,128)S(1)} %add.82), channel_id=1, source_target_pairs={{0,192},{1,193},{2,194},{3,195},{4,196},{5,197},{6,198},{7,199},{8... | collective-permute-start | bytes 98312 | tf_op jit(solution)/shard_map/ppermute | solution.py:45
  104.5 3.8 %collective-permute-start.33 = (f32[32,256]{1,0:T(8,128)S(1)}, f32[32,256]{1,0:T(8,128)S(1)}, u32[]{:S(2)}, u32[]{:S(2)}) collective-permute-start(f32[32,256]{1,0:T(8,128)S(1)} %convolution_add_fusion), channel_id=1, source_target_pairs={{0,1},{1,0},{2,3},{3,2},{4,5},{5,4},{6,7},{7,6},{8,9},{9,8},{10,11... | collective-permute-start | bytes 98312 | tf_op jit(solution)/shard_map/ppermute | solution.py:45
  (188 shorter events, 43.3 us)
Async XLA Ops:
  5.6 4.4 %collective-permute-start = (f32[32,256]{1,0:T(8,128)}, f32[32,256]{1,0:T(8,128)}, u32[]{:S(2)}, u32[]{:S(2)}) collective-permute-start(f32[32,256]{1,0:T(8,128)} %select_bitcast_fusion), channel_id=1, source_target_pairs={{0,1},{1,0},{2,3},{3,2},{4,5},{5,4},{6,7},{7,6},{8,9},{9,8},{10,11... | collective-permute-start | bytes 98312 | tf_op jit(solution)/shard_map/ppermute | solution.py:45
  10.9 7.1 %collective-permute-start.1 = (f32[96,256]{1,0:T(8,128)S(1)}, f32[96,256]{1,0:T(8,128)S(1)}, u32[]{:S(2)}, u32[]{:S(2)}) collective-permute-start(f32[96,256]{1,0:T(8,128)S(1)} %constant_dynamic-update-slice_fusion), channel_id=1, source_target_pairs={{0,6},{1,7},{2,12},{3,13},{4,10},{5,11},{6,0},{7,1},{8,14},{9,15},... | collective-permute-start | bytes 294920 | tf_op jit(solution)/shard_map/ppermute | solution.py:45
  18.0 6.5 %collective-permute-start.2 = (f32[160,256]{1,0:T(8,128)S(1)}, f32[160,256]{1,0:T(8,128)S(1)}, u32[]{:S(2)}, u32[]{:S(2)}) collective-permute-start(f32[160,256]{1,0:T(8,128)S(1)} %pad_maximum_fusion.6), channel_id=1, source_target_pairs={{0,14},{1,15},{2,4},{3,5},{4,2},{5,3},{6,8},{7,9},{8,6},{9,7},{10,... | collective-permute-start | bytes 491528 | tf_op jit(solution)/shard_map/ppermute | solution.py:45
  21.0 5.2 %collective-permute-start.8 = (f32[384,256]{1,0:T(8,128)S(1)}, f32[384,256]{1,0:T(8,128)S(1)}, u32[]{:S(2)}, u32[]{:S(2)}) collective-permute-start(f32[384,256]{1,0:T(8,128)S(1)} %bitcast.162), channel_id=1, source_target_pairs={{0,1},{1,0},{2,3},{3,2},{4,5},{5,4},{6,7},{7,6},{8,9},{9,8},{10,11... | collective-permute-start | bytes 1179656 | tf_op jit(solution)/shard_map/ppermute | solution.py:45
  26.4 6.9 %collective-permute-start.9 = (f32[192,256]{1,0:T(8,128)S(1)}, f32[192,256]{1,0:T(8,128)S(1)}, u32[]{:S(2)}, u32[]{:S(2)}) collective-permute-start(f32[192,256]{1,0:T(8,128)S(1)} %bitcast.175), channel_id=1, source_target_pairs={{0,16},{1,17},{2,18},{3,19},{4,20},{5,21},{6,22},{7,23},{8,24},{9,... | collective-permute-start | bytes 589832 | tf_op jit(solution)/shard_map/ppermute | solution.py:45
  28.9 8.9 %collective-permute-start.4 = (f32[32,256]{1,0:T(8,128)S(1)}, f32[32,256]{1,0:T(8,128)S(1)}, u32[]{:S(2)}, u32[]{:S(2)}) collective-permute-start(f32[32,256]{1,0:T(8,128)S(1)} %slice_add_fusion.4), channel_id=1, source_target_pairs={{0,16},{1,17},{2,18},{3,19},{4,20},{5,21},{6,22},{7,23},{8,24},{9,... | collective-permute-start | bytes 98312 | tf_op jit(solution)/shard_map/ppermute | solution.py:45
  30.3 7.5 %collective-permute-start.5 = (f32[256,256]{1,0:T(8,128)S(1)}, f32[256,256]{1,0:T(8,128)S(1)}, u32[]{:S(2)}, u32[]{:S(2)}) collective-permute-start(f32[256,256]{1,0:T(8,128)S(1)} %bitcast.141), channel_id=1, source_target_pairs={{0,1},{1,0},{2,3},{3,2},{4,5},{5,4},{6,7},{7,6},{8,9},{9,8},{10,11... | collective-permute-start | bytes 786440 | tf_op jit(solution)/shard_map/ppermute | solution.py:45
  33.3 4.4 %collective-permute-start.10 = (f32[64,256]{1,0:T(8,128)S(1)}, f32[64,256]{1,0:T(8,128)S(1)}, u32[]{:S(2)}, u32[]{:S(2)}) collective-permute-start(f32[64,256]{1,0:T(8,128)S(1)} %slice.295), channel_id=1, source_target_pairs={{0,48},{1,49},{2,50},{3,51},{4,52},{5,53},{6,54},{7,55},{8,56},{9,... | collective-permute-start | bytes 196616 | tf_op jit(solution)/shard_map/ppermute | solution.py:45
  40.6 4.7 %collective-permute-start.11 = (f32[96,256]{1,0:T(8,128)S(1)}, f32[96,256]{1,0:T(8,128)S(1)}, u32[]{:S(2)}, u32[]{:S(2)}) collective-permute-start(f32[96,256]{1,0:T(8,128)S(1)} %bitcast.183), channel_id=1, source_target_pairs={{0,2},{1,3},{2,0},{3,1},{4,6},{5,7},{6,4},{7,5},{8,10},{9,11},{10,... | collective-permute-start | bytes 294920 | tf_op jit(solution)/shard_map/ppermute | solution.py:45
  41.6 8.3 %collective-permute-start.18 = (f32[128,256]{1,0:T(8,128)S(1)}, f32[128,256]{1,0:T(8,128)S(1)}, u32[]{:S(2)}, u32[]{:S(2)}) collective-permute-start(f32[128,256]{1,0:T(8,128)S(1)} %bitcast.155), channel_id=1, source_target_pairs={{0,2},{1,3},{2,0},{3,1},{4,6},{5,7},{6,4},{7,5},{8,10},{9,11},{10,... | collective-permute-start | bytes 393224 | tf_op jit(solution)/shard_map/ppermute | solution.py:45
  50.0 6.0 %collective-permute-start.13 = (f32[144,256]{1,0:T(8,128)S(1)}, f32[144,256]{1,0:T(8,128)S(1)}, u32[]{:S(2)}, u32[]{:S(2)}) collective-permute-start(f32[144,256]{1,0:T(8,128)S(1)} %pad_maximum_fusion.8), channel_id=1, source_target_pairs={{0,6},{1,7},{2,12},{3,13},{4,10},{5,11},{6,0},{7,1},{8,14},{9,15},... | collective-permute-start | bytes 442376 | tf_op jit(solution)/shard_map/ppermute | solution.py:45
  53.1 6.0 %collective-permute-start.19 = (f32[224,256]{1,0:T(8,128)S(1)}, f32[224,256]{1,0:T(8,128)S(1)}, u32[]{:S(2)}, u32[]{:S(2)}) collective-permute-start(f32[224,256]{1,0:T(8,128)S(1)} %pad_maximum_fusion.1), channel_id=1, source_target_pairs={{0,16},{1,17},{2,18},{3,19},{4,20},{5,21},{6,22},{7,23},{8,24},{9,... | collective-permute-start | bytes 688136 | tf_op jit(solution)/shard_map/ppermute | solution.py:45
  56.0 10.2 %collective-permute-start.14 = (f32[144,256]{1,0:T(8,128)S(1)}, f32[144,256]{1,0:T(8,128)S(1)}, u32[]{:S(2)}, u32[]{:S(2)}) collective-permute-start(f32[144,256]{1,0:T(8,128)S(1)} %pad_maximum_fusion.9), channel_id=1, source_target_pairs={{0,14},{1,15},{2,4},{3,5},{4,2},{5,3},{6,8},{7,9},{8,6},{9,7},{10,... | collective-permute-start | bytes 442376 | tf_op jit(solution)/shard_map/ppermute | solution.py:45
  59.2 16.3 %collective-permute-start.20 = (f32[256,256]{1,0:T(8,128)S(1)}, f32[256,256]{1,0:T(8,128)S(1)}, u32[]{:S(2)}, u32[]{:S(2)}) collective-permute-start(f32[256,256]{1,0:T(8,128)S(1)} %bitcast.140), channel_id=1, source_target_pairs={{0,1},{1,0},{2,3},{3,2},{4,5},{5,4},{6,7},{7,6},{8,9},{9,8},{10,11... | collective-permute-start | bytes 786440 | tf_op jit(solution)/shard_map/ppermute | solution.py:45
  63.7 7.8 %collective-permute-start.26 = (f32[192,256]{1,0:T(8,128)S(1)}, f32[192,256]{1,0:T(8,128)S(1)}, u32[]{:S(2)}, u32[]{:S(2)}) collective-permute-start(f32[192,256]{1,0:T(8,128)S(1)} %pad_maximum_fusion.5), channel_id=1, source_target_pairs={{0,48},{1,49},{2,50},{3,51},{4,52},{5,53},{6,54},{7,55},{8,56},{9,... | collective-permute-start | bytes 589832 | tf_op jit(solution)/shard_map/ppermute | solution.py:45
  66.3 7.5 %collective-permute-start.15 = (f32[192,256]{1,0:T(8,128)S(1)}, f32[192,256]{1,0:T(8,128)S(1)}, u32[]{:S(2)}, u32[]{:S(2)}) collective-permute-start(f32[192,256]{1,0:T(8,128)S(1)} %pad_maximum_fusion.4), channel_id=1, source_target_pairs={{0,2},{1,3},{2,0},{3,1},{4,6},{5,7},{6,4},{7,5},{8,10},{9,11},{10,... | collective-permute-start | bytes 589832 | tf_op jit(solution)/shard_map/ppermute | solution.py:45
  71.6 19.1 %collective-permute-start.27 = (f32[256,256]{1,0:T(8,128)S(1)}, f32[256,256]{1,0:T(8,128)S(1)}, u32[]{:S(2)}, u32[]{:S(2)}) collective-permute-start(f32[256,256]{1,0:T(8,128)S(1)} %bitcast.138), channel_id=1, source_target_pairs={{0,1},{1,0},{2,3},{3,2},{4,5},{5,4},{6,7},{7,6},{8,9},{9,8},{10,11... | collective-permute-start | bytes 786440 | tf_op jit(solution)/shard_map/ppermute | solution.py:45
  72.5 5.2 %collective-permute-start.31 = (f32[128,256]{1,0:T(8,128)S(1)}, f32[128,256]{1,0:T(8,128)S(1)}, u32[]{:S(2)}, u32[]{:S(2)}) collective-permute-start(f32[128,256]{1,0:T(8,128)S(1)} %bitcast.156), channel_id=1, source_target_pairs={{0,64},{1,65},{2,66},{3,67},{4,68},{5,69},{6,70},{7,71},{8,72},{9,... | collective-permute-start | bytes 393224 | tf_op jit(solution)/shard_map/ppermute | solution.py:45
  73.9 9.1 %collective-permute-start.21 = (f32[192,256]{1,0:T(8,128)S(1)}, f32[192,256]{1,0:T(8,128)S(1)}, u32[]{:S(2)}, u32[]{:S(2)}) collective-permute-start(f32[192,256]{1,0:T(8,128)S(1)} %bitcast.148), channel_id=1, source_target_pairs={{0,16},{1,17},{2,18},{3,19},{4,20},{5,21},{6,22},{7,23},{8,24},{9,... | collective-permute-start | bytes 589832 | tf_op jit(solution)/shard_map/ppermute | solution.py:45
  78.0 4.7 %collective-permute-start.17 = (f32[32,256]{1,0:T(8,128)S(1)}, f32[32,256]{1,0:T(8,128)S(1)}, u32[]{:S(2)}, u32[]{:S(2)}) collective-permute-start(f32[32,256]{1,0:T(8,128)S(1)} %slice.305), channel_id=1, source_target_pairs={{0,48},{1,49},{2,50},{3,51},{4,52},{5,53},{6,54},{7,55},{8,56},{9,... | collective-permute-start | bytes 98312 | tf_op jit(solution)/shard_map/ppermute | solution.py:45
  80.5 12.5 %collective-permute-start.32 = (f32[256,256]{1,0:T(8,128)S(1)}, f32[256,256]{1,0:T(8,128)S(1)}, u32[]{:S(2)}, u32[]{:S(2)}) collective-permute-start(f32[256,256]{1,0:T(8,128)S(1)} %bitcast.139), channel_id=1, source_target_pairs={{0,1},{1,0},{2,3},{3,2},{4,5},{5,4},{6,7},{7,6},{8,9},{9,8},{10,11... | collective-permute-start | bytes 786440 | tf_op jit(solution)/shard_map/ppermute | solution.py:45
  87.4 4.6 %collective-permute-start.24 = (f32[64,256]{1,0:T(8,128)S(1)}, f32[64,256]{1,0:T(8,128)S(1)}, u32[]{:S(2)}, u32[]{:S(2)}) collective-permute-start(f32[64,256]{1,0:T(8,128)S(1)} %slice_subtract_fusion), channel_id=1, source_target_pairs={{0,48},{1,49},{2,50},{3,51},{4,52},{5,53},{6,54},{7,55},{8,56},{9,... | collective-permute-start | bytes 196616 | tf_op jit(solution)/shard_map/ppermute | solution.py:45
  96.9 5.6 %collective-permute-start.29 = (f32[32,256]{1,0:T(8,128)S(1)}, f32[32,256]{1,0:T(8,128)S(1)}, u32[]{:S(2)}, u32[]{:S(2)}) collective-permute-start(f32[32,256]{1,0:T(8,128)S(1)} %fusion.72), channel_id=1, source_target_pairs={{0,1},{1,0},{2,3},{3,2},{4,5},{5,4},{6,7},{7,6},{8,9},{9,8},{10,11... | collective-permute-start | bytes 98312 | tf_op jit(solution)/shard_map/ppermute | solution.py:45
  104.5 4.6 %collective-permute-start.33 = (f32[32,256]{1,0:T(8,128)S(1)}, f32[32,256]{1,0:T(8,128)S(1)}, u32[]{:S(2)}, u32[]{:S(2)}) collective-permute-start(f32[32,256]{1,0:T(8,128)S(1)} %convolution_add_fusion), channel_id=1, source_target_pairs={{0,1},{1,0},{2,3},{3,2},{4,5},{5,4},{6,7},{7,6},{8,9},{9,8},{10,11... | collective-permute-start | bytes 98312 | tf_op jit(solution)/shard_map/ppermute | solution.py:45
  (28 other events, 317.6 us)

commit v4 on v3

v4 whole, which is shorter than its diff:
```python
import jax
import jax.numpy as jnp
import numpy as np
from jax import lax
from jax.experimental.layout import Layout, with_layout_constraint
from jax.sharding import PartitionSpec as P

CORE, Y_A, Y_B, X_A, X_B, X_AB = (
    [i ^ mask for i in range(256)] for mask in (1, 16, 48, 64, 192, 128)
)


def ring_pairs(partner):
    return [i - i % 16 + 2 * partner[i // 2 % 8] + i % 2 for i in range(256)]


Z_A = ring_pairs([1, 0, 3, 2, 5, 4, 7, 6])
Z_B = ring_pairs([7, 2, 1, 4, 3, 6, 5, 0])
Z_C = ring_pairs([3, 6, 5, 0, 7, 2, 1, 4])
SIDE_A, SIDE_B, SIDE_C = 0b01100110, 0b10110100, 0b11101000
RING_ORDER = [0, 3, 4, 7, 1, 6, 2, 5]


def one_hot(source, size):
    matrix = np.zeros((len(source), size), np.float32)
    matrix[np.arange(len(source)), source] = 1
    return matrix


def ring_order(rows):
    source = [
        (z * 2 + core) * rows + row
        for core in range(2)
        for z in RING_ORDER
        for row in range(rows)
    ]
    return one_hot(source, len(source))


def tree_order(highs, pairs, rows):
    source = [
        (((high + pair) * 8 + z) * 2 + core) * rows + row
        for core in range(2)
        for high in highs
        for z in RING_ORDER
        for pair in pairs
        for _ in range(2)
        for row in range(rows)
    ]
    return one_hot(source, len(source) // 2)


def by_rows(value):
    return with_layout_constraint(value, Layout(major_to_minor=(0, 1)))


def after(value, token):
    return lax.optimization_barrier((value, token))[0]


def swapped(value, partner):
    return lax.ppermute(value, "leaf", list(enumerate(partner)))


def sent(partner, *parts):
    got = swapped(jnp.concatenate(parts), partner)
    ends = [0]
    for part in parts:
        ends.append(ends[-1] + part.shape[0])
    return [got[first:last] for first, last in zip(ends, ends[1:])]


def product(left, right, dims, precision=lax.Precision.HIGH):
    return lax.dot_general(
        left,
        right,
        ((dims[:1], dims[1:]), ((), ())),
        precision=precision,
        preferred_element_type=jnp.float32,
    )


def product_nn(left, right):
    return product(left, right, (1, 0))


def product_nt(left, right):
    return product(left, right, (1, 1))


def product_tn(left, right):
    return product(left, right, (0, 0))


def placed(part, offset, size):
    rest = size - offset - part.shape[0]
    return lax.pad(part, jnp.float32(0), ((offset, rest, 0), (0, 0, 0)))


def halves(value, side, blocks=1):
    value = value.reshape(blocks, 2, -1, value.shape[1])
    kept = jnp.where(side, value[:, 1], value[:, 0])
    other = jnp.where(side, value[:, 0], value[:, 1])
    return kept.reshape(-1, value.shape[3]), other.reshape(-1, value.shape[3])


def ordered(own, other, side, blocks=1):
    width = own.shape[1]
    own, other = own.reshape(blocks, -1, width), other.reshape(blocks, -1, width)
    both = jnp.where(
        side,
        jnp.concatenate([other, own], axis=1),
        jnp.concatenate([own, other], axis=1),
    )
    return both.reshape(-1, width)


def two_halves(*capacities):
    rank = capacities[0].shape[1] // 2
    return [part for one in capacities for part in (one[:, :rank], one[:, rank:])]


def solved_weights(own, other, side, capacity):
    upper, lower = jnp.where(side, own, other), jnp.where(side, other, own)
    rank = capacity.shape[1]
    return product_nt(upper, capacity[:rank]) + product_nt(lower, capacity[rank:])


def ordered_weights(own, other, side, capacity, order, rows):
    upper, lower = jnp.where(side, own, other), jnp.where(side, other, own)
    both = product_nt(jnp.concatenate([upper, lower]), capacity)
    both = both.reshape(2, -1, both.shape[1])
    first = np.arange(both.shape[2]) // rows % 2 == 0
    first = jnp.asarray(first[None].astype(np.float32))
    return product_nn(jnp.where(first == 1, both[0], both[1]), order)


def corrected(current, weights, solved, core):
    weights = ordered(weights, swapped(weights, CORE), core)
    return current - product_nt(weights, solved)


def per_device(
    right_sides,
    leaf_inverse,
    coupling_first,
    coupling_second,
    coupling_third,
    coupling_fourth,
    solved_first,
    solved_second,
    solved_third,
    solved_fourth,
    first_level_inverse,
    second_level_inverse,
    third_level_inverse,
    root_level_inverse,
):
    rank = coupling_first.shape[1]
    device_id = lax.axis_index("leaf")
    core, y_low, y_high, x_low, x_high = (
        (device_id >> place) & 1 == 1 for place in (0, 4, 5, 6, 7)
    )
    z = (device_id >> 1) & 7
    side_a, side_b, side_c = ((side >> z) & 1 == 1 for side in (SIDE_A, SIDE_B, SIDE_C))
    y_side = y_low != y_high
    rows = second_level_inverse.shape[0]
    orders = [
        ring_order(2 * rows),
        tree_order((0, 1), (0,), rows),
        tree_order((0, 1, 2, 3), (0,), rows // 2),
        tree_order((0, 2, 4, 6), (0, 1), rows // 4),
    ]
    orders = [jnp.asarray(order) for order in orders]

    sides = [core, y_low, y_high, x_low, x_high, y_side, side_a, side_b, side_c]
    sides, right_sides = lax.optimization_barrier((sides, right_sides))
    core, y_low, y_high, x_low, x_high, y_side, side_a, side_b, side_c = sides
    current = product_nt(right_sides, leaf_inverse)
    kept, away = halves(product_nn(current, coupling_first), core)

    near = jnp.concatenate(two_halves(after(first_level_inverse, away)))
    far = [second_level_inverse, third_level_inverse, root_level_inverse]
    far = two_halves(*after(far, away))
    size, offset, whole = 4 * rows, 0, 0
    for part in far[:4]:
        whole = whole + placed(part, offset, size)
        offset += part.shape[0]
    low = placed(far[4], offset, size) + placed(far[5], offset + rows // 4, size)
    offset += rows // 2
    high = placed(far[4], offset, size) + placed(far[5], offset + rows // 4, size)
    far = whole + jnp.where(y_low, high, low)
    near, far = lax.optimization_barrier((near, far))
    sums = kept + swapped(away, CORE)

    other, near_other, far_other = sent(Z_C, sums, near, far)
    cross_second, cross_third = after((solved_second, solved_third), sums)
    cross = by_rows(
        jnp.concatenate(
            [
                product_tn(cross_second, coupling_third),
                product_tn(cross_second, coupling_fourth),
                product_tn(cross_third, coupling_fourth),
            ]
        )
    )
    cross, cross_away = halves(cross, core, 3)
    cross_other = swapped(cross_away, CORE)
    sums = sums + other
    near, far = ordered(near, near_other, side_c, 2), ordered(far, far_other, side_c)

    sums, cross = lax.optimization_barrier((sums, cross + cross_other))
    other, near_other, far_other = sent(Z_B, sums, near, far)
    cross, cross_away = halves(cross, y_side, 3)
    cross_other = swapped(cross_away, Y_A)
    sums = sums + other
    near, far = ordered(near, near_other, side_b, 2), ordered(far, far_other, side_b)

    other, near_other = sent(Z_A, sums, near)
    cross, cross_away = halves(cross + after(cross_other, sums), side_a, 3)
    cross_other = swapped(cross_away, Z_A)
    sums, near = sums + other, ordered(near, near_other, side_a, 2)

    other = swapped(sums, Y_A)
    near = ordered(near, swapped(near, CORE), core, 2)
    cross, cross_away = halves(cross + after(cross_other, sums), side_b, 3)
    cross_other = swapped(cross_away, Z_B)
    solved_first = product_nt(after(solved_first, sums), orders[0])
    first = solved_weights(sums, other, y_low, near)

    far_other = swapped(after(far, first), Z_A)
    current = corrected(current, first, solved_first, core)

    sums = [
        product_nn(current, coupling)
        for coupling in (coupling_second, coupling_third, coupling_fourth)
    ]
    kept, away = halves(jnp.concatenate(sums), core, 3)
    share = kept.shape[0] // 3
    sums = kept + swapped(away, CORE)

    other = swapped(sums, Y_A)
    cross = cross + after(cross_other, away)
    cross_other = swapped(cross, Z_C)
    far = ordered(far, after(far_other, sums), side_a).reshape(8, -1, rank)
    ends = [0, 2 * rows, 3 * rows, 4 * rows]
    far = [far[:, a:b].reshape(-1, rank) for a, b in zip(ends, ends[1:])]
    sums = sums + other

    other = swapped(sums, Z_C)
    cross = cross + after(cross_other, sums)
    cross_other = swapped(cross, Y_A)
    far_other = sent(Y_A, *after(far, sums))
    sums, cross = sums + other, ordered(cross, after(cross_other, other), y_side, 3)

    other, cross_other = sent(Z_B, sums, cross)
    sums, cross = sums + other, ordered(cross, cross_other, side_b, 6)

    other, cross_other = sent(Z_A, sums, cross)
    far_other = after(far_other, sums)
    far[:2] = [ordered(own, got, y_low) for own, got in zip(far[:2], far_other)]
    far[2] = far[2] + far_other[2]
    far_other = sent(Y_B, *far[1:])
    capacity_other = swapped(far[0], CORE)
    sums, cross = sums + other, ordered(cross, cross_other, side_a, 6)
    capacity = [ordered(far[0], after(capacity_other, sums), core)]

    own = sums[:share]
    cross, last = cross[:rank], cross[rank:]
    other, last_other = sent(Y_B, own, last)
    cross_other = swapped(cross, CORE)
    far_other = after(far_other, sums)
    far = [ordered(own, got, y_high) for own, got in zip(far[1:], far_other)]
    far_other = swapped(far[1], X_A)
    capacity_other = swapped(far[0], CORE)
    second = ordered_weights(own, other, y_high, capacity[0], orders[1], rows)
    cross = ordered(cross, after(cross_other, other), core, 2)
    sums = sums[share:] - jnp.concatenate(
        [product_nn(second, cross[:rank]), product_nn(second, cross[rank:])]
    )

    other = swapped(sums, Y_B)
    second_other = swapped(after(second, sums), CORE)
    last = last + last_other
    last_other = swapped(last, CORE)
    capacity.append(ordered(far[0], after(capacity_other, sums), core))
    far = ordered(far[1], after(far_other, sums), x_low)
    capacity_other = swapped(far, CORE)
    sums = sums + other

    own = sums[:share]
    other = swapped(own, X_A)
    second = ordered(second, after(second_other, sums), core)
    current = current - product_nt(second, solved_second)
    third = ordered_weights(own, other, x_low, capacity[1], orders[2], rows // 2)
    last = ordered(last, after(last_other, sums), core)
    sums = sums[share:] - product_nn(third, last)

    other = swapped(sums, X_A)
    sibling = swapped(sums, X_B) + swapped(sums, X_AB)
    capacity.append(ordered(far, after(capacity_other, third), core))
    third_other = swapped(after(third, sums), CORE)
    sums = sums + other
    third = ordered(third, after(third_other, sums), core)
    current = after(current, sums) - product_nt(third, solved_third)
    fourth = ordered_weights(sums, sibling, x_high, capacity[2], orders[3], rows // 4)
    return corrected(current, fourth, solved_fourth, core)


def solution(mesh):
    in_specs = (P(None, "leaf"),) + (P("leaf", None),) * 13
    return jax.shard_map(
        per_device,
        mesh=mesh,
        in_specs=in_specs,
        out_specs=P(None, "leaf"),
        check_vma=False,
    )
```

time: 111 us -> 102 us (0.919)
  waiting for transfers between devices: 21.7 us -> 18.9 us
  other arithmetic: 3.33 us -> 0.96 us
  matrix products: 17.8 us -> 15.9 us
    ppermute x34 -> x36, waiting for transfers between devices: 21.7 us -> 18.9 us  [swapped(): return lax.ppermute(value, 'leaf', list(enumerate(partner)))]
    dot_general x27 -> x24, matrix products: 17.8 us -> 15.9 us  [product(): lax.dot_general(left, right, ((dims[:1], dims[1:]), ((), ())), precision=...]
    ppermute x34 -> x36, starting transfers between devices: 65.7 us -> 65 us  [swapped(): return lax.ppermute(value, 'leaf', list(enumerate(partner)))]
  transfers between devices with their start and end apart: 34 -> 36, of which waited for: 15 -> 15; matrix products, arithmetic and copies ran while one was open for 12% -> 10% of each run, Pallas kernels for 0% -> 0%
where the time goes in v4:
time: 102 us
  starting transfers between devices  65 us (64%)
  waiting for transfers between devices  18.9 us (19%)
  matrix products  15.9 us (16%)
    ppermute x36, starting transfers between devices, swapped(): return lax.ppermute(value, 'leaf', list(enumerate(partner)))  65 us
    ppermute x36, waiting for transfers between devices, swapped(): return lax.ppermute(value, 'leaf', list(enumerate(partner)))  18.9 us
    dot_general x24, matrix products, product(): lax.dot_general(left, right, ((dims[:1], dims[1:]), ((), ())), precision=...  15.9 us
  transfers between devices with their start and end apart: 36, of which 15 were waited for; matrix products, arithmetic and copies ran while one was open for 10% of the time, Pallas kernels for 0%

profile of v4, /device:TPU:1, one launch (start us, length us, event | category | flops | bytes accessed | tf_op | source)
XLA Modules:
  0.0 101.9 jit_solution(15295000528937433014)
XLA Ops:
  0.1 4.5 %fusion.93 = f32[64,1024]{1,0:T(8,128)S(1)} fusion(f32[64,1024]{1,0:T(8,128)} %param.21, f32[1024,1024]{1,0:T(8,128)} %param.22), kind=kOutput, calls=%fused_computation.175 | convolution fusion | flops 402653184 | bytes 4718592 | tf_op jit(solution)/shard_map/dot_general | solution.py:74
  5.0 3.3 %collective-permute-start = (f32[32,256]{1,0:T(8,128)S(1)}, f32[32,256]{1,0:T(8,128)S(1)}, u32[]{:S(2)}, u32[]{:S(2)}) collective-permute-start(f32[32,256]{1,0:T(8,128)S(1)} %select_bitcast_fusion), channel_id=1, source_target_pairs={{0,1},{1,0},{2,3},{3,2},{4,5},{5,4},{6,7},{7,6},{8,9},{9,8},{10,11... | collective-permute-start | bytes 98312 | tf_op jit(solution)/shard_map/ppermute | solution.py:62
  9.2 2.7 %collective-permute-start.1 = (f32[96,256]{1,0:T(8,128)S(1)}, f32[96,256]{1,0:T(8,128)S(1)}, u32[]{:S(2)}, u32[]{:S(2)}) collective-permute-start(f32[96,256]{1,0:T(8,128)S(1)} %pad_maximum_fusion.9), channel_id=1, source_target_pairs={{0,6},{1,7},{2,12},{3,13},{4,10},{5,11},{6,0},{7,1},{8,14},{9,15},... | collective-permute-start | bytes 294920 | tf_op jit(solution)/shard_map/ppermute | solution.py:62
  17.3 2.9 %collective-permute-start.3 = (f32[160,256]{1,0:T(8,128)S(1)}, f32[160,256]{1,0:T(8,128)S(1)}, u32[]{:S(2)}, u32[]{:S(2)}) collective-permute-start(f32[160,256]{1,0:T(8,128)S(1)} %pad_maximum_fusion.6), channel_id=1, source_target_pairs={{0,14},{1,15},{2,4},{3,5},{4,2},{5,3},{6,8},{7,9},{8,6},{9,7},{10,... | collective-permute-start | bytes 491528 | tf_op jit(solution)/shard_map/ppermute | solution.py:62
  21.6 2.7 %collective-permute-done.3 = f32[160,256]{1,0:T(8,128)S(1)} collective-permute-done((f32[160,256]{1,0:T(8,128)S(1)}, f32[160,256]{1,0:T(8,128)S(1)}, u32[]{:S(2)}, u32[]{:S(2)}) %collective-permute-start.3) | collective-permute-done | bytes 163872 | tf_op jit(solution)/shard_map/ppermute | solution.py:62
  27.0 2.2 %collective-permute-done.4 = f32[160,256]{1,0:T(8,128)S(1)} collective-permute-done((f32[160,256]{1,0:T(8,128)S(1)}, f32[160,256]{1,0:T(8,128)S(1)}, u32[]{:S(2)}, u32[]{:S(2)}) %collective-permute-start.4) | collective-permute-done | bytes 163872 | tf_op jit(solution)/shard_map/ppermute | solution.py:62
  31.3 2.6 %collective-permute-start.6 = (f32[256,256]{1,0:T(8,128)S(1)}, f32[256,256]{1,0:T(8,128)S(1)}, u32[]{:S(2)}, u32[]{:S(2)}) collective-permute-start(f32[256,256]{1,0:T(8,128)S(1)} %bitcast.107), channel_id=1, source_target_pairs={{0,1},{1,0},{2,3},{3,2},{4,5},{5,4},{6,7},{7,6},{8,9},{9,8},{10,11... | collective-permute-start | bytes 786440 | tf_op jit(solution)/shard_map/ppermute | solution.py:62
  33.9 2.6 %collective-permute-start.13 = (f32[48,256]{1,0:T(8,128)S(1)}, f32[48,256]{1,0:T(8,128)S(1)}, u32[]{:S(2)}, u32[]{:S(2)}) collective-permute-start(f32[48,256]{1,0:T(8,128)S(1)} %bitcast.133), channel_id=1, source_target_pairs={{0,14},{1,15},{2,4},{3,5},{4,2},{5,3},{6,8},{7,9},{8,6},{9,7},{10,... | collective-permute-start | bytes 147464 | tf_op jit(solution)/shard_map/ppermute | solution.py:62
  41.2 1.7 %collective-permute-start.14 = (f32[48,256]{1,0:T(8,128)S(1)}, f32[48,256]{1,0:T(8,128)S(1)}, u32[]{:S(2)}, u32[]{:S(2)}) collective-permute-start(f32[48,256]{1,0:T(8,128)S(1)} %bitcast_add_fusion.4), channel_id=1, source_target_pairs={{0,6},{1,7},{2,12},{3,13},{4,10},{5,11},{6,0},{7,1},{8,14},{9,15},... | collective-permute-start | bytes 147464 | tf_op jit(solution)/shard_map/ppermute | solution.py:62
  44.4 2.5 %collective-permute-done.9 = f32[96,256]{1,0:T(8,128)S(1)} collective-permute-done((f32[96,256]{1,0:T(8,128)S(1)}, f32[96,256]{1,0:T(8,128)S(1)}, u32[]{:S(2)}, u32[]{:S(2)}) %collective-permute-start.9) | collective-permute-done | bytes 98336 | tf_op jit(solution)/shard_map/ppermute | solution.py:62
  46.9 1.7 %collective-permute-start.10 = (f32[96,256]{1,0:T(8,128)S(1)}, f32[96,256]{1,0:T(8,128)S(1)}, u32[]{:S(2)}, u32[]{:S(2)}) collective-permute-start(f32[96,256]{1,0:T(8,128)S(1)} %add.107), channel_id=1, source_target_pairs={{0,6},{1,7},{2,12},{3,13},{4,10},{5,11},{6,0},{7,1},{8,14},{9,15},... | collective-permute-start | bytes 294920 | tf_op jit(solution)/shard_map/ppermute | solution.py:62
  52.4 1.6 %collective-permute-start.16 = (f32[192,256]{1,0:T(8,128)S(1)}, f32[192,256]{1,0:T(8,128)S(1)}, u32[]{:S(2)}, u32[]{:S(2)}) collective-permute-start(f32[192,256]{1,0:T(8,128)S(1)} %pad_maximum_fusion.4), channel_id=1, source_target_pairs={{0,14},{1,15},{2,4},{3,5},{4,2},{5,3},{6,8},{7,9},{8,6},{9,7},{10,... | collective-permute-start | bytes 589832 | tf_op jit(solution)/shard_map/ppermute | solution.py:62
  53.9 3.2 %collective-permute-done.20 = f32[256,256]{1,0:T(8,128)S(1)} collective-permute-done((f32[256,256]{1,0:T(8,128)S(1)}, f32[256,256]{1,0:T(8,128)S(1)}, u32[]{:S(2)}, u32[]{:S(2)}) %collective-permute-start.20) | collective-permute-done | bytes 262176 | tf_op jit(solution)/shard_map/ppermute | solution.py:62
  57.2 1.5 %collective-permute-done.16 = f32[192,256]{1,0:T(8,128)S(1)} collective-permute-done((f32[192,256]{1,0:T(8,128)S(1)}, f32[192,256]{1,0:T(8,128)S(1)}, u32[]{:S(2)}, u32[]{:S(2)}) %collective-permute-start.16) | collective-permute-done | bytes 196640 | tf_op jit(solution)/shard_map/ppermute | solution.py:62
  58.8 3.9 %collective-permute-start.17 = (f32[288,256]{1,0:T(8,128)S(1)}, f32[288,256]{1,0:T(8,128)S(1)}, u32[]{:S(2)}, u32[]{:S(2)}) collective-permute-start(f32[288,256]{1,0:T(8,128)S(1)} %pad_maximum_fusion.1), channel_id=1, source_target_pairs={{0,2},{1,3},{2,0},{3,1},{4,6},{5,7},{6,4},{7,5},{8,10},{9,11},{10,... | collective-permute-start | bytes 884744 | tf_op jit(solution)/shard_map/ppermute | solution.py:62
  62.7 2.8 %collective-permute-start.26 = (f32[192,256]{1,0:T(8,128)S(1)}, f32[192,256]{1,0:T(8,128)S(1)}, u32[]{:S(2)}, u32[]{:S(2)}) collective-permute-start(f32[192,256]{1,0:T(8,128)S(1)} %pad_maximum_fusion.5), channel_id=1, source_target_pairs={{0,48},{1,49},{2,50},{3,51},{4,52},{5,53},{6,54},{7,55},{8,56},{9,... | collective-permute-start | bytes 589832 | tf_op jit(solution)/shard_map/ppermute | solution.py:62
  65.6 2.9 %collective-permute-start.21 = (f32[256,256]{1,0:T(8,128)S(1)}, f32[256,256]{1,0:T(8,128)S(1)}, u32[]{:S(2)}, u32[]{:S(2)}) collective-permute-start(f32[256,256]{1,0:T(8,128)S(1)} %maximum_select_fusion.11), channel_id=1, source_target_pairs={{0,1},{1,0},{2,3},{3,2},{4,5},{5,4},{6,7},{7,6},{8,9},{9,8},{10,11... | collective-permute-start | bytes 786440 | tf_op jit(solution)/shard_map/ppermute | solution.py:62
  68.8 2.8 %collective-permute-start.18 = (f32[160,256]{1,0:T(8,128)S(1)}, f32[160,256]{1,0:T(8,128)S(1)}, u32[]{:S(2)}, u32[]{:S(2)}) collective-permute-start(f32[160,256]{1,0:T(8,128)S(1)} %pad_maximum_fusion.8), channel_id=1, source_target_pairs={{0,48},{1,49},{2,50},{3,51},{4,52},{5,53},{6,54},{7,55},{8,56},{9,... | collective-permute-start | bytes 491528 | tf_op jit(solution)/shard_map/ppermute | solution.py:62
  72.9 4.2 %collective-permute-start.22 = (f32[256,256]{1,0:T(8,128)S(1)}, f32[256,256]{1,0:T(8,128)S(1)}, u32[]{:S(2)}, u32[]{:S(2)}) collective-permute-start(f32[256,256]{1,0:T(8,128)S(1)} %bitcast.109), channel_id=1, source_target_pairs={{0,1},{1,0},{2,3},{3,2},{4,5},{5,4},{6,7},{7,6},{8,9},{9,8},{10,11... | collective-permute-start | bytes 786440 | tf_op jit(solution)/shard_map/ppermute | solution.py:62
  78.9 4.7 %collective-permute-start.28 = (f32[128,256]{1,0:T(8,128)S(1)}, f32[128,256]{1,0:T(8,128)S(1)}, u32[]{:S(2)}, u32[]{:S(2)}) collective-permute-start(f32[128,256]{1,0:T(8,128)S(1)} %slice_add_fusion), channel_id=1, source_target_pairs={{0,1},{1,0},{2,3},{3,2},{4,5},{5,4},{6,7},{7,6},{8,9},{9,8},{10,11... | collective-permute-start | bytes 393224 | tf_op jit(solution)/shard_map/ppermute | solution.py:62
  85.1 2.4 %collective-permute-start.34 = (f32[256,256]{1,0:T(8,128)S(1)}, f32[256,256]{1,0:T(8,128)S(1)}, u32[]{:S(2)}, u32[]{:S(2)}) collective-permute-start(f32[256,256]{1,0:T(8,128)S(1)} %maximum_select_fusion.15), channel_id=1, source_target_pairs={{0,1},{1,0},{2,3},{3,2},{4,5},{5,4},{6,7},{7,6},{8,9},{9,8},{10,11... | collective-permute-start | bytes 786440 | tf_op jit(solution)/shard_map/ppermute | solution.py:62
  88.4 2.5 %collective-permute-start.32 = (f32[32,256]{1,0:T(8,128)S(1)}, f32[32,256]{1,0:T(8,128)S(1)}, u32[]{:S(2)}, u32[]{:S(2)}) collective-permute-start(f32[32,256]{1,0:T(8,128)S(1)} %slice_subtract_fusion.1), channel_id=1, source_target_pairs={{0,128},{1,129},{2,130},{3,131},{4,132},{5,133},{6,134},{7,135},{8... | collective-permute-start | bytes 98312 | tf_op jit(solution)/shard_map/ppermute | solution.py:62
  91.8 3.8 %collective-permute-start.30 = (f32[32,256]{1,0:T(8,128)S(1)}, f32[32,256]{1,0:T(8,128)S(1)}, u32[]{:S(2)}, u32[]{:S(2)}) collective-permute-start(f32[32,256]{1,0:T(8,128)S(1)} %fusion.63), channel_id=1, source_target_pairs={{0,1},{1,0},{2,3},{3,2},{4,5},{5,4},{6,7},{7,6},{8,9},{9,8},{10,11... | collective-permute-start | bytes 98312 | tf_op jit(solution)/shard_map/ppermute | solution.py:62
  97.1 2.6 %collective-permute-start.35 = (f32[32,256]{1,0:T(8,128)S(1)}, f32[32,256]{1,0:T(8,128)S(1)}, u32[]{:S(2)}, u32[]{:S(2)}) collective-permute-start(f32[32,256]{1,0:T(8,128)S(1)} %fusion.64), channel_id=1, source_target_pairs={{0,1},{1,0},{2,3},{3,2},{4,5},{5,4},{6,7},{7,6},{8,9},{9,8},{10,11... | collective-permute-start | bytes 98312 | tf_op jit(solution)/shard_map/ppermute | solution.py:62
  (184 shorter events, 32.7 us)
Async XLA Ops:
  9.2 6.6 %collective-permute-start.1 = (f32[96,256]{1,0:T(8,128)S(1)}, f32[96,256]{1,0:T(8,128)S(1)}, u32[]{:S(2)}, u32[]{:S(2)}) collective-permute-start(f32[96,256]{1,0:T(8,128)S(1)} %pad_maximum_fusion.9), channel_id=1, source_target_pairs={{0,6},{1,7},{2,12},{3,13},{4,10},{5,11},{6,0},{7,1},{8,14},{9,15},... | collective-permute-start | bytes 294920 | tf_op jit(solution)/shard_map/ppermute | solution.py:62
  17.3 7.1 %collective-permute-start.3 = (f32[160,256]{1,0:T(8,128)S(1)}, f32[160,256]{1,0:T(8,128)S(1)}, u32[]{:S(2)}, u32[]{:S(2)}) collective-permute-start(f32[160,256]{1,0:T(8,128)S(1)} %pad_maximum_fusion.6), channel_id=1, source_target_pairs={{0,14},{1,15},{2,4},{3,5},{4,2},{5,3},{6,8},{7,9},{8,6},{9,7},{10,... | collective-permute-start | bytes 491528 | tf_op jit(solution)/shard_map/ppermute | solution.py:62
  20.2 5.9 %collective-permute-start.11 = (f32[192,256]{1,0:T(8,128)S(1)}, f32[192,256]{1,0:T(8,128)S(1)}, u32[]{:S(2)}, u32[]{:S(2)}) collective-permute-start(f32[192,256]{1,0:T(8,128)S(1)} %bitcast.127), channel_id=1, source_target_pairs={{0,16},{1,17},{2,18},{3,19},{4,20},{5,21},{6,22},{7,23},{8,24},{9,... | collective-permute-start | bytes 589832 | tf_op jit(solution)/shard_map/ppermute | solution.py:62
  24.4 4.8 %collective-permute-start.4 = (f32[160,256]{1,0:T(8,128)S(1)}, f32[160,256]{1,0:T(8,128)S(1)}, u32[]{:S(2)}, u32[]{:S(2)}) collective-permute-start(f32[160,256]{1,0:T(8,128)S(1)} %pad_maximum_fusion.7), channel_id=1, source_target_pairs={{0,2},{1,3},{2,0},{3,1},{4,6},{5,7},{6,4},{7,5},{8,10},{9,11},{10,... | collective-permute-start | bytes 491528 | tf_op jit(solution)/shard_map/ppermute | solution.py:62
  26.2 5.1 %collective-permute-start.12 = (f32[96,256]{1,0:T(8,128)S(1)}, f32[96,256]{1,0:T(8,128)S(1)}, u32[]{:S(2)}, u32[]{:S(2)}) collective-permute-start(f32[96,256]{1,0:T(8,128)S(1)} %bitcast.131), channel_id=1, source_target_pairs={{0,2},{1,3},{2,0},{3,1},{4,6},{5,7},{6,4},{7,5},{8,10},{9,11},{10,... | collective-permute-start | bytes 294920 | tf_op jit(solution)/shard_map/ppermute | solution.py:62
  29.2 7.3 %collective-permute-start.5 = (f32[32,256]{1,0:T(8,128)S(1)}, f32[32,256]{1,0:T(8,128)S(1)}, u32[]{:S(2)}, u32[]{:S(2)}) collective-permute-start(f32[32,256]{1,0:T(8,128)S(1)} %slice_add_fusion.3), channel_id=1, source_target_pairs={{0,16},{1,17},{2,18},{3,19},{4,20},{5,21},{6,22},{7,23},{8,24},{9,... | collective-permute-start | bytes 98312 | tf_op jit(solution)/shard_map/ppermute | solution.py:62
  31.3 5.2 %collective-permute-start.6 = (f32[256,256]{1,0:T(8,128)S(1)}, f32[256,256]{1,0:T(8,128)S(1)}, u32[]{:S(2)}, u32[]{:S(2)}) collective-permute-start(f32[256,256]{1,0:T(8,128)S(1)} %bitcast.107), channel_id=1, source_target_pairs={{0,1},{1,0},{2,3},{3,2},{4,5},{5,4},{6,7},{7,6},{8,9},{9,8},{10,11... | collective-permute-start | bytes 786440 | tf_op jit(solution)/shard_map/ppermute | solution.py:62
  33.9 7.3 %collective-permute-start.13 = (f32[48,256]{1,0:T(8,128)S(1)}, f32[48,256]{1,0:T(8,128)S(1)}, u32[]{:S(2)}, u32[]{:S(2)}) collective-permute-start(f32[48,256]{1,0:T(8,128)S(1)} %bitcast.133), channel_id=1, source_target_pairs={{0,14},{1,15},{2,4},{3,5},{4,2},{5,3},{6,8},{7,9},{8,6},{9,7},{10,... | collective-permute-start | bytes 147464 | tf_op jit(solution)/shard_map/ppermute | solution.py:62
  38.3 6.0 %collective-permute-start.19 = (f32[128,256]{1,0:T(8,128)S(1)}, f32[128,256]{1,0:T(8,128)S(1)}, u32[]{:S(2)}, u32[]{:S(2)}) collective-permute-start(f32[128,256]{1,0:T(8,128)S(1)} %maximum_select_fusion.18), channel_id=1, source_target_pairs={{0,2},{1,3},{2,0},{3,1},{4,6},{5,7},{6,4},{7,5},{8,10},{9,11},{10,... | collective-permute-start | bytes 393224 | tf_op jit(solution)/shard_map/ppermute | solution.py:62
  41.2 7.5 %collective-permute-start.14 = (f32[48,256]{1,0:T(8,128)S(1)}, f32[48,256]{1,0:T(8,128)S(1)}, u32[]{:S(2)}, u32[]{:S(2)}) collective-permute-start(f32[48,256]{1,0:T(8,128)S(1)} %bitcast_add_fusion.4), channel_id=1, source_target_pairs={{0,6},{1,7},{2,12},{3,13},{4,10},{5,11},{6,0},{7,1},{8,14},{9,15},... | collective-permute-start | bytes 147464 | tf_op jit(solution)/shard_map/ppermute | solution.py:62
  46.9 5.4 %collective-permute-start.10 = (f32[96,256]{1,0:T(8,128)S(1)}, f32[96,256]{1,0:T(8,128)S(1)}, u32[]{:S(2)}, u32[]{:S(2)}) collective-permute-start(f32[96,256]{1,0:T(8,128)S(1)} %add.107), channel_id=1, source_target_pairs={{0,6},{1,7},{2,12},{3,13},{4,10},{5,11},{6,0},{7,1},{8,14},{9,15},... | collective-permute-start | bytes 294920 | tf_op jit(solution)/shard_map/ppermute | solution.py:62
  50.1 7.1 %collective-permute-start.20 = (f32[256,256]{1,0:T(8,128)S(1)}, f32[256,256]{1,0:T(8,128)S(1)}, u32[]{:S(2)}, u32[]{:S(2)}) collective-permute-start(f32[256,256]{1,0:T(8,128)S(1)} %pad_maximum_fusion.2), channel_id=1, source_target_pairs={{0,16},{1,17},{2,18},{3,19},{4,20},{5,21},{6,22},{7,23},{8,24},{9,... | collective-permute-start | bytes 786440 | tf_op jit(solution)/shard_map/ppermute | solution.py:62
  52.4 6.3 %collective-permute-start.16 = (f32[192,256]{1,0:T(8,128)S(1)}, f32[192,256]{1,0:T(8,128)S(1)}, u32[]{:S(2)}, u32[]{:S(2)}) collective-permute-start(f32[192,256]{1,0:T(8,128)S(1)} %pad_maximum_fusion.4), channel_id=1, source_target_pairs={{0,14},{1,15},{2,4},{3,5},{4,2},{5,3},{6,8},{7,9},{8,6},{9,7},{10,... | collective-permute-start | bytes 589832 | tf_op jit(solution)/shard_map/ppermute | solution.py:62
  58.8 9.8 %collective-permute-start.17 = (f32[288,256]{1,0:T(8,128)S(1)}, f32[288,256]{1,0:T(8,128)S(1)}, u32[]{:S(2)}, u32[]{:S(2)}) collective-permute-start(f32[288,256]{1,0:T(8,128)S(1)} %pad_maximum_fusion.1), channel_id=1, source_target_pairs={{0,2},{1,3},{2,0},{3,1},{4,6},{5,7},{6,4},{7,5},{8,10},{9,11},{10,... | collective-permute-start | bytes 884744 | tf_op jit(solution)/shard_map/ppermute | solution.py:62
  62.7 5.9 %collective-permute-start.26 = (f32[192,256]{1,0:T(8,128)S(1)}, f32[192,256]{1,0:T(8,128)S(1)}, u32[]{:S(2)}, u32[]{:S(2)}) collective-permute-start(f32[192,256]{1,0:T(8,128)S(1)} %pad_maximum_fusion.5), channel_id=1, source_target_pairs={{0,48},{1,49},{2,50},{3,51},{4,52},{5,53},{6,54},{7,55},{8,56},{9,... | collective-permute-start | bytes 589832 | tf_op jit(solution)/shard_map/ppermute | solution.py:62
  65.6 6.0 %collective-permute-start.21 = (f32[256,256]{1,0:T(8,128)S(1)}, f32[256,256]{1,0:T(8,128)S(1)}, u32[]{:S(2)}, u32[]{:S(2)}) collective-permute-start(f32[256,256]{1,0:T(8,128)S(1)} %maximum_select_fusion.11), channel_id=1, source_target_pairs={{0,1},{1,0},{2,3},{3,2},{4,5},{5,4},{6,7},{7,6},{8,9},{9,8},{10,11... | collective-permute-start | bytes 786440 | tf_op jit(solution)/shard_map/ppermute | solution.py:62
  68.8 8.4 %collective-permute-start.18 = (f32[160,256]{1,0:T(8,128)S(1)}, f32[160,256]{1,0:T(8,128)S(1)}, u32[]{:S(2)}, u32[]{:S(2)}) collective-permute-start(f32[160,256]{1,0:T(8,128)S(1)} %pad_maximum_fusion.8), channel_id=1, source_target_pairs={{0,48},{1,49},{2,50},{3,51},{4,52},{5,53},{6,54},{7,55},{8,56},{9,... | collective-permute-start | bytes 491528 | tf_op jit(solution)/shard_map/ppermute | solution.py:62
  71.6 12.0 %collective-permute-start.33 = (f32[128,256]{1,0:T(8,128)S(1)}, f32[128,256]{1,0:T(8,128)S(1)}, u32[]{:S(2)}, u32[]{:S(2)}) collective-permute-start(f32[128,256]{1,0:T(8,128)S(1)} %maximum_select_fusion.21), channel_id=1, source_target_pairs={{0,64},{1,65},{2,66},{3,67},{4,68},{5,69},{6,70},{7,71},{8,72},{9,... | collective-permute-start | bytes 393224 | tf_op jit(solution)/shard_map/ppermute | solution.py:62
  72.9 5.4 %collective-permute-start.22 = (f32[256,256]{1,0:T(8,128)S(1)}, f32[256,256]{1,0:T(8,128)S(1)}, u32[]{:S(2)}, u32[]{:S(2)}) collective-permute-start(f32[256,256]{1,0:T(8,128)S(1)} %bitcast.109), channel_id=1, source_target_pairs={{0,1},{1,0},{2,3},{3,2},{4,5},{5,4},{6,7},{7,6},{8,9},{9,8},{10,11... | collective-permute-start | bytes 786440 | tf_op jit(solution)/shard_map/ppermute | solution.py:62
  77.1 10.3 %collective-permute-start.27 = (f32[256,256]{1,0:T(8,128)S(1)}, f32[256,256]{1,0:T(8,128)S(1)}, u32[]{:S(2)}, u32[]{:S(2)}) collective-permute-start(f32[256,256]{1,0:T(8,128)S(1)} %maximum_select_fusion.12), channel_id=1, source_target_pairs={{0,1},{1,0},{2,3},{3,2},{4,5},{5,4},{6,7},{7,6},{8,9},{9,8},{10,11... | collective-permute-start | bytes 786440 | tf_op jit(solution)/shard_map/ppermute | solution.py:62
  78.8 5.0 %collective-permute-start.24 = (f32[64,256]{1,0:T(8,128)S(1)}, f32[64,256]{1,0:T(8,128)S(1)}, u32[]{:S(2)}, u32[]{:S(2)}) collective-permute-start(f32[64,256]{1,0:T(8,128)S(1)} %slice_subtract_fusion), channel_id=1, source_target_pairs={{0,48},{1,49},{2,50},{3,51},{4,52},{5,53},{6,54},{7,55},{8,56},{9,... | collective-permute-start | bytes 196616 | tf_op jit(solution)/shard_map/ppermute | solution.py:62
  78.9 8.6 %collective-permute-start.28 = (f32[128,256]{1,0:T(8,128)S(1)}, f32[128,256]{1,0:T(8,128)S(1)}, u32[]{:S(2)}, u32[]{:S(2)}) collective-permute-start(f32[128,256]{1,0:T(8,128)S(1)} %slice_add_fusion), channel_id=1, source_target_pairs={{0,1},{1,0},{2,3},{3,2},{4,5},{5,4},{6,7},{7,6},{8,9},{9,8},{10,11... | collective-permute-start | bytes 393224 | tf_op jit(solution)/shard_map/ppermute | solution.py:62
  85.1 11.4 %collective-permute-start.34 = (f32[256,256]{1,0:T(8,128)S(1)}, f32[256,256]{1,0:T(8,128)S(1)}, u32[]{:S(2)}, u32[]{:S(2)}) collective-permute-start(f32[256,256]{1,0:T(8,128)S(1)} %maximum_select_fusion.15), channel_id=1, source_target_pairs={{0,1},{1,0},{2,3},{3,2},{4,5},{5,4},{6,7},{7,6},{8,9},{9,8},{10,11... | collective-permute-start | bytes 786440 | tf_op jit(solution)/shard_map/ppermute | solution.py:62
  88.4 7.2 %collective-permute-start.32 = (f32[32,256]{1,0:T(8,128)S(1)}, f32[32,256]{1,0:T(8,128)S(1)}, u32[]{:S(2)}, u32[]{:S(2)}) collective-permute-start(f32[32,256]{1,0:T(8,128)S(1)} %slice_subtract_fusion.1), channel_id=1, source_target_pairs={{0,128},{1,129},{2,130},{3,131},{4,132},{5,133},{6,134},{7,135},{8... | collective-permute-start | bytes 98312 | tf_op jit(solution)/shard_map/ppermute | solution.py:62
  (31 other events, 337.1 us)

commit v5 on v4

--- a/solution.py
+++ b/solution.py
@@ -242,15 +242,15 @@
     other = swapped(sums, Y_A)
     cross = cross + after(cross_other, away)
     cross_other = swapped(cross, Z_C)
+    sums = sums + other
     far = ordered(far, after(far_other, sums), side_a).reshape(8, -1, rank)
     ends = [0, 2 * rows, 3 * rows, 4 * rows]
     far = [far[:, a:b].reshape(-1, rank) for a, b in zip(ends, ends[1:])]
-    sums = sums + other
 
     other = swapped(sums, Z_C)
     cross = cross + after(cross_other, sums)
     cross_other = swapped(cross, Y_A)
-    far_other = sent(Y_A, *after(far, sums))
+    far_other = sent(Y_A, *far)
     sums, cross = sums + other, ordered(cross, after(cross_other, other), y_side, 3)
 
     other, cross_other = sent(Z_B, sums, cross)
@@ -269,17 +269,17 @@
     cross, last = cross[:rank], cross[rank:]
     other, last_other = sent(Y_B, own, last)
     cross_other = swapped(cross, CORE)
+    second = ordered_weights(own, other, y_high, capacity[0], orders[1], rows)
+    cross = ordered(cross, after(cross_other, other), core, 2)
+    sums = sums[share:] - jnp.concatenate(
+        [product_nn(second, cross[:rank]), product_nn(second, cross[rank:])]
+    )
+
+    other = swapped(sums, Y_B)
     far_other = after(far_other, sums)
     far = [ordered(own, got, y_high) for own, got in zip(far[1:], far_other)]
     far_other = swapped(far[1], X_A)
     capacity_other = swapped(far[0], CORE)
-    second = ordered_weights(own, other, y_high, capacity[0], orders[1], rows)
-    cross = ordered(cross, after(cross_other, other), core, 2)
-    sums = sums[share:] - jnp.concatenate(
-        [product_nn(second, cross[:rank]), product_nn(second, cross[rank:])]
-    )
-
-    other = swapped(sums, Y_B)
     second_other = swapped(after(second, sums), CORE)
     last = last + last_other
     last_other = swapped(last, CORE)

time: 102 us -> 98.9 us (0.970)
  starting transfers between devices: 65 us -> 59.2 us
  waiting for transfers between devices: 18.9 us -> 21.6 us
    ppermute x36, starting transfers between devices: 65 us -> 59.2 us  [swapped(): return lax.ppermute(value, 'leaf', list(enumerate(partner)))]
    ppermute x36, waiting for transfers between devices: 18.9 us -> 21.6 us  [swapped(): return lax.ppermute(value, 'leaf', list(enumerate(partner)))]
  transfers between devices with their start and end apart: 36 -> 36, of which waited for: 15 -> 18; matrix products, arithmetic and copies ran while one was open for 10% -> 9% of each run, Pallas kernels for 0% -> 0%
where the time goes in v5:
time: 98.9 us; the launch traced here: 98.8 us
  starting transfers between devices  59.2 us (60%)
  waiting for transfers between devices  21.6 us (22%)
  matrix products  15.9 us (16%)
  other arithmetic  0.99 us (1%)
    ppermute x36, starting transfers between devices, swapped(): return lax.ppermute(value, 'leaf', list(enumerate(partner)))  59.2 us
    ppermute x36, waiting for transfers between devices, swapped(): return lax.ppermute(value, 'leaf', list(enumerate(partner)))  21.6 us
    dot_general x24, matrix products, product(): lax.dot_general(left, right, ((dims[:1], dims[1:]), ((), ())), precision=...  15.9 us
  transfers between devices with their start and end apart: 36, of which 18 were waited for; matrix products, arithmetic and copies ran while one was open for 9% of the time, Pallas kernels for 0%

profile of v5, /device:TPU:1, one launch (start us, length us, event | category | flops | bytes accessed | tf_op | source)
XLA Modules:
  0.0 98.8 jit_solution(17350014390843280399)
XLA Ops:
  0.1 4.5 %fusion.95 = f32[64,1024]{1,0:T(8,128)S(1)} fusion(f32[64,1024]{1,0:T(8,128)} %param.21, f32[1024,1024]{1,0:T(8,128)} %param.22), kind=kOutput, calls=%fused_computation.177 | convolution fusion | flops 402653184 | bytes 4718592 | tf_op jit(solution)/shard_map/dot_general | solution.py:74
  5.0 3.3 %collective-permute-start = (f32[32,256]{1,0:T(8,128)S(1)}, f32[32,256]{1,0:T(8,128)S(1)}, u32[]{:S(2)}, u32[]{:S(2)}) collective-permute-start(f32[32,256]{1,0:T(8,128)S(1)} %select_bitcast_fusion), channel_id=1, source_target_pairs={{0,1},{1,0},{2,3},{3,2},{4,5},{5,4},{6,7},{7,6},{8,9},{9,8},{10,11... | collective-permute-start | bytes 98312 | tf_op jit(solution)/shard_map/ppermute | solution.py:62
  9.2 2.7 %collective-permute-start.1 = (f32[96,256]{1,0:T(8,128)S(1)}, f32[96,256]{1,0:T(8,128)S(1)}, u32[]{:S(2)}, u32[]{:S(2)}) collective-permute-start(f32[96,256]{1,0:T(8,128)S(1)} %pad_maximum_fusion.10), channel_id=1, source_target_pairs={{0,6},{1,7},{2,12},{3,13},{4,10},{5,11},{6,0},{7,1},{8,14},{9,15},... | collective-permute-start | bytes 294920 | tf_op jit(solution)/shard_map/ppermute | solution.py:62
  17.3 2.9 %collective-permute-start.3 = (f32[160,256]{1,0:T(8,128)S(1)}, f32[160,256]{1,0:T(8,128)S(1)}, u32[]{:S(2)}, u32[]{:S(2)}) collective-permute-start(f32[160,256]{1,0:T(8,128)S(1)} %pad_maximum_fusion.7), channel_id=1, source_target_pairs={{0,14},{1,15},{2,4},{3,5},{4,2},{5,3},{6,8},{7,9},{8,6},{9,7},{10,... | collective-permute-start | bytes 491528 | tf_op jit(solution)/shard_map/ppermute | solution.py:62
  21.6 2.7 %collective-permute-done.3 = f32[160,256]{1,0:T(8,128)S(1)} collective-permute-done((f32[160,256]{1,0:T(8,128)S(1)}, f32[160,256]{1,0:T(8,128)S(1)}, u32[]{:S(2)}, u32[]{:S(2)}) %collective-permute-start.3) | collective-permute-done | bytes 163872 | tf_op jit(solution)/shard_map/ppermute | solution.py:62
  27.0 2.2 %collective-permute-done.4 = f32[160,256]{1,0:T(8,128)S(1)} collective-permute-done((f32[160,256]{1,0:T(8,128)S(1)}, f32[160,256]{1,0:T(8,128)S(1)}, u32[]{:S(2)}, u32[]{:S(2)}) %collective-permute-start.4) | collective-permute-done | bytes 163872 | tf_op jit(solution)/shard_map/ppermute | solution.py:62
  31.3 2.6 %collective-permute-start.6 = (f32[256,256]{1,0:T(8,128)S(1)}, f32[256,256]{1,0:T(8,128)S(1)}, u32[]{:S(2)}, u32[]{:S(2)}) collective-permute-start(f32[256,256]{1,0:T(8,128)S(1)} %bitcast.107), channel_id=1, source_target_pairs={{0,1},{1,0},{2,3},{3,2},{4,5},{5,4},{6,7},{7,6},{8,9},{9,8},{10,11... | collective-permute-start | bytes 786440 | tf_op jit(solution)/shard_map/ppermute | solution.py:62
  34.0 2.6 %collective-permute-start.13 = (f32[48,256]{1,0:T(8,128)S(1)}, f32[48,256]{1,0:T(8,128)S(1)}, u32[]{:S(2)}, u32[]{:S(2)}) collective-permute-start(f32[48,256]{1,0:T(8,128)S(1)} %bitcast.133), channel_id=1, source_target_pairs={{0,14},{1,15},{2,4},{3,5},{4,2},{5,3},{6,8},{7,9},{8,6},{9,7},{10,... | collective-permute-start | bytes 147464 | tf_op jit(solution)/shard_map/ppermute | solution.py:62
  42.9 1.7 %collective-permute-start.14 = (f32[48,256]{1,0:T(8,128)S(1)}, f32[48,256]{1,0:T(8,128)S(1)}, u32[]{:S(2)}, u32[]{:S(2)}) collective-permute-start(f32[48,256]{1,0:T(8,128)S(1)} %bitcast_add_fusion.4), channel_id=1, source_target_pairs={{0,6},{1,7},{2,12},{3,13},{4,10},{5,11},{6,0},{7,1},{8,14},{9,15},... | collective-permute-start | bytes 147464 | tf_op jit(solution)/shard_map/ppermute | solution.py:62
  46.1 1.8 %collective-permute-start.10 = (f32[96,256]{1,0:T(8,128)S(1)}, f32[96,256]{1,0:T(8,128)S(1)}, u32[]{:S(2)}, u32[]{:S(2)}) collective-permute-start(f32[96,256]{1,0:T(8,128)S(1)} %add.107), channel_id=1, source_target_pairs={{0,6},{1,7},{2,12},{3,13},{4,10},{5,11},{6,0},{7,1},{8,14},{9,15},... | collective-permute-start | bytes 294920 | tf_op jit(solution)/shard_map/ppermute | solution.py:62
  52.1 1.7 %collective-permute-start.16 = (f32[192,256]{1,0:T(8,128)S(1)}, f32[192,256]{1,0:T(8,128)S(1)}, u32[]{:S(2)}, u32[]{:S(2)}) collective-permute-start(f32[192,256]{1,0:T(8,128)S(1)} %pad_maximum_fusion.5), channel_id=1, source_target_pairs={{0,14},{1,15},{2,4},{3,5},{4,2},{5,3},{6,8},{7,9},{8,6},{9,7},{10,... | collective-permute-start | bytes 589832 | tf_op jit(solution)/shard_map/ppermute | solution.py:62
  53.8 2.2 %collective-permute-done.20 = f32[256,256]{1,0:T(8,128)S(1)} collective-permute-done((f32[256,256]{1,0:T(8,128)S(1)}, f32[256,256]{1,0:T(8,128)S(1)}, u32[]{:S(2)}, u32[]{:S(2)}) %collective-permute-start.20) | collective-permute-done | bytes 262176 | tf_op jit(solution)/shard_map/ppermute | solution.py:62
  56.0 1.9 %collective-permute-done.16 = f32[192,256]{1,0:T(8,128)S(1)} collective-permute-done((f32[192,256]{1,0:T(8,128)S(1)}, f32[192,256]{1,0:T(8,128)S(1)}, u32[]{:S(2)}, u32[]{:S(2)}) %collective-permute-start.16) | collective-permute-done | bytes 196640 | tf_op jit(solution)/shard_map/ppermute | solution.py:62
  58.0 1.5 %collective-permute-start.17 = (f32[288,256]{1,0:T(8,128)S(1)}, f32[288,256]{1,0:T(8,128)S(1)}, u32[]{:S(2)}, u32[]{:S(2)}) collective-permute-start(f32[288,256]{1,0:T(8,128)S(1)} %pad_maximum_fusion.3), channel_id=1, source_target_pairs={{0,2},{1,3},{2,0},{3,1},{4,6},{5,7},{6,4},{7,5},{8,10},{9,11},{10,... | collective-permute-start | bytes 884744 | tf_op jit(solution)/shard_map/ppermute | solution.py:62
  59.5 1.7 %collective-permute-start.26 = (f32[192,256]{1,0:T(8,128)S(1)}, f32[192,256]{1,0:T(8,128)S(1)}, u32[]{:S(2)}, u32[]{:S(2)}) collective-permute-start(f32[192,256]{1,0:T(8,128)S(1)} %pad_maximum_fusion.6), channel_id=1, source_target_pairs={{0,48},{1,49},{2,50},{3,51},{4,52},{5,53},{6,54},{7,55},{8,56},{9,... | collective-permute-start | bytes 589832 | tf_op jit(solution)/shard_map/ppermute | solution.py:62
  61.2 5.6 %collective-permute-start.21 = (f32[256,256]{1,0:T(8,128)S(1)}, f32[256,256]{1,0:T(8,128)S(1)}, u32[]{:S(2)}, u32[]{:S(2)}) collective-permute-start(f32[256,256]{1,0:T(8,128)S(1)} %fusion.19), channel_id=1, source_target_pairs={{0,1},{1,0},{2,3},{3,2},{4,5},{5,4},{6,7},{7,6},{8,9},{9,8},{10,11... | collective-permute-start | bytes 786440 | tf_op jit(solution)/shard_map/ppermute | solution.py:62
  68.0 3.9 %collective-permute-start.22 = (f32[256,256]{1,0:T(8,128)S(1)}, f32[256,256]{1,0:T(8,128)S(1)}, u32[]{:S(2)}, u32[]{:S(2)}) collective-permute-start(f32[256,256]{1,0:T(8,128)S(1)} %bitcast.109), channel_id=1, source_target_pairs={{0,1},{1,0},{2,3},{3,2},{4,5},{5,4},{6,7},{7,6},{8,9},{9,8},{10,11... | collective-permute-start | bytes 786440 | tf_op jit(solution)/shard_map/ppermute | solution.py:62
  72.4 3.2 %collective-permute-start.28 = (f32[128,256]{1,0:T(8,128)S(1)}, f32[128,256]{1,0:T(8,128)S(1)}, u32[]{:S(2)}, u32[]{:S(2)}) collective-permute-start(f32[128,256]{1,0:T(8,128)S(1)} %slice_add_fusion), channel_id=1, source_target_pairs={{0,1},{1,0},{2,3},{3,2},{4,5},{5,4},{6,7},{7,6},{8,9},{9,8},{10,11... | collective-permute-start | bytes 393224 | tf_op jit(solution)/shard_map/ppermute | solution.py:62
  76.7 2.6 %collective-permute-start.24 = (f32[64,256]{1,0:T(8,128)S(1)}, f32[64,256]{1,0:T(8,128)S(1)}, u32[]{:S(2)}, u32[]{:S(2)}) collective-permute-start(f32[64,256]{1,0:T(8,128)S(1)} %slice_subtract_fusion), channel_id=1, source_target_pairs={{0,48},{1,49},{2,50},{3,51},{4,52},{5,53},{6,54},{7,55},{8,56},{9,... | collective-permute-start | bytes 196616 | tf_op jit(solution)/shard_map/ppermute | solution.py:62
  79.8 1.5 %collective-permute-start.33 = (f32[128,256]{1,0:T(8,128)S(1)}, f32[128,256]{1,0:T(8,128)S(1)}, u32[]{:S(2)}, u32[]{:S(2)}) collective-permute-start(f32[128,256]{1,0:T(8,128)S(1)} %maximum_select_fusion.20), channel_id=1, source_target_pairs={{0,64},{1,65},{2,66},{3,67},{4,68},{5,69},{6,70},{7,71},{8,72},{9,... | collective-permute-start | bytes 393224 | tf_op jit(solution)/shard_map/ppermute | solution.py:62
  83.7 2.0 %collective-permute-done.25 = f32[32,256]{1,0:T(8,128)S(1)} collective-permute-done((f32[32,256]{1,0:T(8,128)S(1)}, f32[32,256]{1,0:T(8,128)S(1)}, u32[]{:S(2)}, u32[]{:S(2)}) %collective-permute-start.25) | collective-permute-done | bytes 32800 | tf_op jit(solution)/shard_map/ppermute | solution.py:62
  86.6 2.8 %collective-permute-start.32 = (f32[32,256]{1,0:T(8,128)S(1)}, f32[32,256]{1,0:T(8,128)S(1)}, u32[]{:S(2)}, u32[]{:S(2)}) collective-permute-start(f32[32,256]{1,0:T(8,128)S(1)} %slice_subtract_fusion.1), channel_id=1, source_target_pairs={{0,128},{1,129},{2,130},{3,131},{4,132},{5,133},{6,134},{7,135},{8... | collective-permute-start | bytes 98312 | tf_op jit(solution)/shard_map/ppermute | solution.py:62
  90.3 1.7 %collective-permute-start.34 = (f32[256,256]{1,0:T(8,128)S(1)}, f32[256,256]{1,0:T(8,128)S(1)}, u32[]{:S(2)}, u32[]{:S(2)}) collective-permute-start(f32[256,256]{1,0:T(8,128)S(1)} %maximum_select_fusion.14), channel_id=1, source_target_pairs={{0,1},{1,0},{2,3},{3,2},{4,5},{5,4},{6,7},{7,6},{8,9},{9,8},{10,11... | collective-permute-start | bytes 786440 | tf_op jit(solution)/shard_map/ppermute | solution.py:62
  94.1 2.5 %collective-permute-start.35 = (f32[32,256]{1,0:T(8,128)S(1)}, f32[32,256]{1,0:T(8,128)S(1)}, u32[]{:S(2)}, u32[]{:S(2)}) collective-permute-start(f32[32,256]{1,0:T(8,128)S(1)} %fusion.66), channel_id=1, source_target_pairs={{0,1},{1,0},{2,3},{3,2},{4,5},{5,4},{6,7},{7,6},{8,9},{9,8},{10,11... | collective-permute-start | bytes 98312 | tf_op jit(solution)/shard_map/ppermute | solution.py:62
  (184 shorter events, 36.2 us)
Async XLA Ops:
  5.0 4.2 %collective-permute-start = (f32[32,256]{1,0:T(8,128)S(1)}, f32[32,256]{1,0:T(8,128)S(1)}, u32[]{:S(2)}, u32[]{:S(2)}) collective-permute-start(f32[32,256]{1,0:T(8,128)S(1)} %select_bitcast_fusion), channel_id=1, source_target_pairs={{0,1},{1,0},{2,3},{3,2},{4,5},{5,4},{6,7},{7,6},{8,9},{9,8},{10,11... | collective-permute-start | bytes 98312 | tf_op jit(solution)/shard_map/ppermute | solution.py:62
  9.2 6.6 %collective-permute-start.1 = (f32[96,256]{1,0:T(8,128)S(1)}, f32[96,256]{1,0:T(8,128)S(1)}, u32[]{:S(2)}, u32[]{:S(2)}) collective-permute-start(f32[96,256]{1,0:T(8,128)S(1)} %pad_maximum_fusion.10), channel_id=1, source_target_pairs={{0,6},{1,7},{2,12},{3,13},{4,10},{5,11},{6,0},{7,1},{8,14},{9,15},... | collective-permute-start | bytes 294920 | tf_op jit(solution)/shard_map/ppermute | solution.py:62
  17.3 7.1 %collective-permute-start.3 = (f32[160,256]{1,0:T(8,128)S(1)}, f32[160,256]{1,0:T(8,128)S(1)}, u32[]{:S(2)}, u32[]{:S(2)}) collective-permute-start(f32[160,256]{1,0:T(8,128)S(1)} %pad_maximum_fusion.7), channel_id=1, source_target_pairs={{0,14},{1,15},{2,4},{3,5},{4,2},{5,3},{6,8},{7,9},{8,6},{9,7},{10,... | collective-permute-start | bytes 491528 | tf_op jit(solution)/shard_map/ppermute | solution.py:62
  20.3 5.9 %collective-permute-start.11 = (f32[192,256]{1,0:T(8,128)S(1)}, f32[192,256]{1,0:T(8,128)S(1)}, u32[]{:S(2)}, u32[]{:S(2)}) collective-permute-start(f32[192,256]{1,0:T(8,128)S(1)} %bitcast.127), channel_id=1, source_target_pairs={{0,16},{1,17},{2,18},{3,19},{4,20},{5,21},{6,22},{7,23},{8,24},{9,... | collective-permute-start | bytes 589832 | tf_op jit(solution)/shard_map/ppermute | solution.py:62
  24.4 4.8 %collective-permute-start.4 = (f32[160,256]{1,0:T(8,128)S(1)}, f32[160,256]{1,0:T(8,128)S(1)}, u32[]{:S(2)}, u32[]{:S(2)}) collective-permute-start(f32[160,256]{1,0:T(8,128)S(1)} %pad_maximum_fusion.8), channel_id=1, source_target_pairs={{0,2},{1,3},{2,0},{3,1},{4,6},{5,7},{6,4},{7,5},{8,10},{9,11},{10,... | collective-permute-start | bytes 491528 | tf_op jit(solution)/shard_map/ppermute | solution.py:62
  26.2 5.1 %collective-permute-start.12 = (f32[96,256]{1,0:T(8,128)S(1)}, f32[96,256]{1,0:T(8,128)S(1)}, u32[]{:S(2)}, u32[]{:S(2)}) collective-permute-start(f32[96,256]{1,0:T(8,128)S(1)} %bitcast.131), channel_id=1, source_target_pairs={{0,2},{1,3},{2,0},{3,1},{4,6},{5,7},{6,4},{7,5},{8,10},{9,11},{10,... | collective-permute-start | bytes 294920 | tf_op jit(solution)/shard_map/ppermute | solution.py:62
  29.2 7.3 %collective-permute-start.5 = (f32[32,256]{1,0:T(8,128)S(1)}, f32[32,256]{1,0:T(8,128)S(1)}, u32[]{:S(2)}, u32[]{:S(2)}) collective-permute-start(f32[32,256]{1,0:T(8,128)S(1)} %slice_add_fusion.3), channel_id=1, source_target_pairs={{0,16},{1,17},{2,18},{3,19},{4,20},{5,21},{6,22},{7,23},{8,24},{9,... | collective-permute-start | bytes 98312 | tf_op jit(solution)/shard_map/ppermute | solution.py:62
  31.3 5.2 %collective-permute-start.6 = (f32[256,256]{1,0:T(8,128)S(1)}, f32[256,256]{1,0:T(8,128)S(1)}, u32[]{:S(2)}, u32[]{:S(2)}) collective-permute-start(f32[256,256]{1,0:T(8,128)S(1)} %bitcast.107), channel_id=1, source_target_pairs={{0,1},{1,0},{2,3},{3,2},{4,5},{5,4},{6,7},{7,6},{8,9},{9,8},{10,11... | collective-permute-start | bytes 786440 | tf_op jit(solution)/shard_map/ppermute | solution.py:62
  34.0 7.6 %collective-permute-start.13 = (f32[48,256]{1,0:T(8,128)S(1)}, f32[48,256]{1,0:T(8,128)S(1)}, u32[]{:S(2)}, u32[]{:S(2)}) collective-permute-start(f32[48,256]{1,0:T(8,128)S(1)} %bitcast.133), channel_id=1, source_target_pairs={{0,14},{1,15},{2,4},{3,5},{4,2},{5,3},{6,8},{7,9},{8,6},{9,7},{10,... | collective-permute-start | bytes 147464 | tf_op jit(solution)/shard_map/ppermute | solution.py:62
  40.9 6.9 %collective-permute-start.19 = (f32[128,256]{1,0:T(8,128)S(1)}, f32[128,256]{1,0:T(8,128)S(1)}, u32[]{:S(2)}, u32[]{:S(2)}) collective-permute-start(f32[128,256]{1,0:T(8,128)S(1)} %maximum_select_fusion.17), channel_id=1, source_target_pairs={{0,2},{1,3},{2,0},{3,1},{4,6},{5,7},{6,4},{7,5},{8,10},{9,11},{10,... | collective-permute-start | bytes 393224 | tf_op jit(solution)/shard_map/ppermute | solution.py:62
  42.9 5.0 %collective-permute-start.14 = (f32[48,256]{1,0:T(8,128)S(1)}, f32[48,256]{1,0:T(8,128)S(1)}, u32[]{:S(2)}, u32[]{:S(2)}) collective-permute-start(f32[48,256]{1,0:T(8,128)S(1)} %bitcast_add_fusion.4), channel_id=1, source_target_pairs={{0,6},{1,7},{2,12},{3,13},{4,10},{5,11},{6,0},{7,1},{8,14},{9,15},... | collective-permute-start | bytes 147464 | tf_op jit(solution)/shard_map/ppermute | solution.py:62
  46.1 5.9 %collective-permute-start.10 = (f32[96,256]{1,0:T(8,128)S(1)}, f32[96,256]{1,0:T(8,128)S(1)}, u32[]{:S(2)}, u32[]{:S(2)}) collective-permute-start(f32[96,256]{1,0:T(8,128)S(1)} %add.107), channel_id=1, source_target_pairs={{0,6},{1,7},{2,12},{3,13},{4,10},{5,11},{6,0},{7,1},{8,14},{9,15},... | collective-permute-start | bytes 294920 | tf_op jit(solution)/shard_map/ppermute | solution.py:62
  48.9 7.1 %collective-permute-start.20 = (f32[256,256]{1,0:T(8,128)S(1)}, f32[256,256]{1,0:T(8,128)S(1)}, u32[]{:S(2)}, u32[]{:S(2)}) collective-permute-start(f32[256,256]{1,0:T(8,128)S(1)} %fusion.18), channel_id=1, source_target_pairs={{0,16},{1,17},{2,18},{3,19},{4,20},{5,21},{6,22},{7,23},{8,24},{9,... | collective-permute-start | bytes 786440 | tf_op jit(solution)/shard_map/ppermute | solution.py:62
  52.1 5.8 %collective-permute-start.16 = (f32[192,256]{1,0:T(8,128)S(1)}, f32[192,256]{1,0:T(8,128)S(1)}, u32[]{:S(2)}, u32[]{:S(2)}) collective-permute-start(f32[192,256]{1,0:T(8,128)S(1)} %pad_maximum_fusion.5), channel_id=1, source_target_pairs={{0,14},{1,15},{2,4},{3,5},{4,2},{5,3},{6,8},{7,9},{8,6},{9,7},{10,... | collective-permute-start | bytes 589832 | tf_op jit(solution)/shard_map/ppermute | solution.py:62
  58.0 8.8 %collective-permute-start.17 = (f32[288,256]{1,0:T(8,128)S(1)}, f32[288,256]{1,0:T(8,128)S(1)}, u32[]{:S(2)}, u32[]{:S(2)}) collective-permute-start(f32[288,256]{1,0:T(8,128)S(1)} %pad_maximum_fusion.3), channel_id=1, source_target_pairs={{0,2},{1,3},{2,0},{3,1},{4,6},{5,7},{6,4},{7,5},{8,10},{9,11},{10,... | collective-permute-start | bytes 884744 | tf_op jit(solution)/shard_map/ppermute | solution.py:62
  59.5 7.5 %collective-permute-start.26 = (f32[192,256]{1,0:T(8,128)S(1)}, f32[192,256]{1,0:T(8,128)S(1)}, u32[]{:S(2)}, u32[]{:S(2)}) collective-permute-start(f32[192,256]{1,0:T(8,128)S(1)} %pad_maximum_fusion.6), channel_id=1, source_target_pairs={{0,48},{1,49},{2,50},{3,51},{4,52},{5,53},{6,54},{7,55},{8,56},{9,... | collective-permute-start | bytes 589832 | tf_op jit(solution)/shard_map/ppermute | solution.py:62
  61.2 6.7 %collective-permute-start.21 = (f32[256,256]{1,0:T(8,128)S(1)}, f32[256,256]{1,0:T(8,128)S(1)}, u32[]{:S(2)}, u32[]{:S(2)}) collective-permute-start(f32[256,256]{1,0:T(8,128)S(1)} %fusion.19), channel_id=1, source_target_pairs={{0,1},{1,0},{2,3},{3,2},{4,5},{5,4},{6,7},{7,6},{8,9},{9,8},{10,11... | collective-permute-start | bytes 786440 | tf_op jit(solution)/shard_map/ppermute | solution.py:62
  66.9 5.5 %collective-permute-start.18 = (f32[160,256]{1,0:T(8,128)S(1)}, f32[160,256]{1,0:T(8,128)S(1)}, u32[]{:S(2)}, u32[]{:S(2)}) collective-permute-start(f32[160,256]{1,0:T(8,128)S(1)} %pad_maximum_fusion.9), channel_id=1, source_target_pairs={{0,48},{1,49},{2,50},{3,51},{4,52},{5,53},{6,54},{7,55},{8,56},{9,... | collective-permute-start | bytes 491528 | tf_op jit(solution)/shard_map/ppermute | solution.py:62
  68.0 8.3 %collective-permute-start.22 = (f32[256,256]{1,0:T(8,128)S(1)}, f32[256,256]{1,0:T(8,128)S(1)}, u32[]{:S(2)}, u32[]{:S(2)}) collective-permute-start(f32[256,256]{1,0:T(8,128)S(1)} %bitcast.109), channel_id=1, source_target_pairs={{0,1},{1,0},{2,3},{3,2},{4,5},{5,4},{6,7},{7,6},{8,9},{9,8},{10,11... | collective-permute-start | bytes 786440 | tf_op jit(solution)/shard_map/ppermute | solution.py:62
  72.4 11.3 %collective-permute-start.28 = (f32[128,256]{1,0:T(8,128)S(1)}, f32[128,256]{1,0:T(8,128)S(1)}, u32[]{:S(2)}, u32[]{:S(2)}) collective-permute-start(f32[128,256]{1,0:T(8,128)S(1)} %slice_add_fusion), channel_id=1, source_target_pairs={{0,1},{1,0},{2,3},{3,2},{4,5},{5,4},{6,7},{7,6},{8,9},{9,8},{10,11... | collective-permute-start | bytes 393224 | tf_op jit(solution)/shard_map/ppermute | solution.py:62
  76.7 5.0 %collective-permute-start.24 = (f32[64,256]{1,0:T(8,128)S(1)}, f32[64,256]{1,0:T(8,128)S(1)}, u32[]{:S(2)}, u32[]{:S(2)}) collective-permute-start(f32[64,256]{1,0:T(8,128)S(1)} %slice_subtract_fusion), channel_id=1, source_target_pairs={{0,48},{1,49},{2,50},{3,51},{4,52},{5,53},{6,54},{7,55},{8,56},{9,... | collective-permute-start | bytes 196616 | tf_op jit(solution)/shard_map/ppermute | solution.py:62
  79.8 5.9 %collective-permute-start.33 = (f32[128,256]{1,0:T(8,128)S(1)}, f32[128,256]{1,0:T(8,128)S(1)}, u32[]{:S(2)}, u32[]{:S(2)}) collective-permute-start(f32[128,256]{1,0:T(8,128)S(1)} %maximum_select_fusion.20), channel_id=1, source_target_pairs={{0,64},{1,65},{2,66},{3,67},{4,68},{5,69},{6,70},{7,71},{8,72},{9,... | collective-permute-start | bytes 393224 | tf_op jit(solution)/shard_map/ppermute | solution.py:62
  81.3 4.4 %collective-permute-start.27 = (f32[256,256]{1,0:T(8,128)S(1)}, f32[256,256]{1,0:T(8,128)S(1)}, u32[]{:S(2)}, u32[]{:S(2)}) collective-permute-start(f32[256,256]{1,0:T(8,128)S(1)} %maximum_select_fusion.11), channel_id=1, source_target_pairs={{0,1},{1,0},{2,3},{3,2},{4,5},{5,4},{6,7},{7,6},{8,9},{9,8},{10,11... | collective-permute-start | bytes 786440 | tf_op jit(solution)/shard_map/ppermute | solution.py:62
  86.6 5.5 %collective-permute-start.32 = (f32[32,256]{1,0:T(8,128)S(1)}, f32[32,256]{1,0:T(8,128)S(1)}, u32[]{:S(2)}, u32[]{:S(2)}) collective-permute-start(f32[32,256]{1,0:T(8,128)S(1)} %slice_subtract_fusion.1), channel_id=1, source_target_pairs={{0,128},{1,129},{2,130},{3,131},{4,132},{5,133},{6,134},{7,135},{8... | collective-permute-start | bytes 98312 | tf_op jit(solution)/shard_map/ppermute | solution.py:62
  (31 other events, 320.4 us)

commit v6 on v5

--- a/solution.py
+++ b/solution.py
@@ -126,13 +126,15 @@
     return product_nt(upper, capacity[:rank]) + product_nt(lower, capacity[rank:])
 
 
-def ordered_weights(own, other, side, capacity, order, rows):
+def in_tree_order(capacity, order, rows):
+    first = (np.arange(capacity.shape[0]) // rows % 2 == 0)[:, None]
+    parts = [product_tn(jnp.asarray(order * half), capacity) for half in (first, ~first)]
+    return jnp.concatenate(parts, axis=1)
+
+
+def ordered_weights(own, other, side, capacity):
     upper, lower = jnp.where(side, own, other), jnp.where(side, other, own)
-    both = product_nt(jnp.concatenate([upper, lower]), capacity)
-    both = both.reshape(2, -1, both.shape[1])
-    first = np.arange(both.shape[2]) // rows % 2 == 0
-    first = jnp.asarray(first[None].astype(np.float32))
-    return product_nn(jnp.where(first == 1, both[0], both[1]), order)
+    return product_nt(jnp.concatenate([upper, lower], axis=1), capacity)
 
 
 def corrected(current, weights, solved, core):
@@ -171,7 +173,6 @@
         tree_order((0, 1, 2, 3), (0,), rows // 2),
         tree_order((0, 2, 4, 6), (0, 1), rows // 4),
     ]
-    orders = [jnp.asarray(order) for order in orders]
 
     sides = [core, y_low, y_high, x_low, x_high, y_side, side_a, side_b, side_c]
     sides, right_sides = lax.optimization_barrier((sides, right_sides))
@@ -225,7 +226,7 @@
     near = ordered(near, swapped(near, CORE), core, 2)
     cross, cross_away = halves(cross + after(cross_other, sums), side_b, 3)
     cross_other = swapped(cross_away, Z_B)
-    solved_first = product_nt(after(solved_first, sums), orders[0])
+    solved_first = product_nt(after(solved_first, sums), jnp.asarray(orders[0]))
     first = solved_weights(sums, other, y_low, near)
 
     far_other = swapped(after(far, first), Z_A)
@@ -264,12 +265,13 @@
     capacity_other = swapped(far[0], CORE)
     sums, cross = sums + other, ordered(cross, cross_other, side_a, 6)
     capacity = [ordered(far[0], after(capacity_other, sums), core)]
+    capacity[0] = in_tree_order(capacity[0], orders[1], rows)
 
     own = sums[:share]
     cross, last = cross[:rank], cross[rank:]
     other, last_other = sent(Y_B, own, last)
     cross_other = swapped(cross, CORE)
-    second = ordered_weights(own, other, y_high, capacity[0], orders[1], rows)
+    second = ordered_weights(own, other, y_high, capacity[0])
     cross = ordered(cross, after(cross_other, other), core, 2)
     sums = sums[share:] - jnp.concatenate(
         [product_nn(second, cross[:rank]), product_nn(second, cross[rank:])]
@@ -284,6 +286,7 @@
     last = last + last_other
     last_other = swapped(last, CORE)
     capacity.append(ordered(far[0], after(capacity_other, sums), core))
+    capacity[1] = in_tree_order(capacity[1], orders[2], rows // 2)
     far = ordered(far[1], after(far_other, sums), x_low)
     capacity_other = swapped(far, CORE)
     sums = sums + other
@@ -292,18 +295,19 @@
     other = swapped(own, X_A)
     second = ordered(second, after(second_other, sums), core)
     current = current - product_nt(second, solved_second)
-    third = ordered_weights(own, other, x_low, capacity[1], orders[2], rows // 2)
+    third = ordered_weights(own, other, x_low, capacity[1])
     last = ordered(last, after(last_other, sums), core)
     sums = sums[share:] - product_nn(third, last)
 
     other = swapped(sums, X_A)
     sibling = swapped(sums, X_B) + swapped(sums, X_AB)
     capacity.append(ordered(far, after(capacity_other, third), core))
+    capacity[2] = in_tree_order(capacity[2], orders[3], rows // 4)
     third_other = swapped(after(third, sums), CORE)
     sums = sums + other
     third = ordered(third, after(third_other, sums), core)
     current = after(current, sums) - product_nt(third, solved_third)
-    fourth = ordered_weights(sums, sibling, x_high, capacity[2], orders[3], rows // 4)
+    fourth = ordered_weights(sums, sibling, x_high, capacity[2])
     return corrected(current, fourth, solved_fourth, core)
 
 

time: 98.9 us -> 103 us (1.041)
  matrix products: 15.9 us -> 18.4 us
  starting transfers between devices: 59.2 us -> 61.4 us
    dot_general x24 -> x27, matrix products: 15.9 us -> 18.4 us  [product(): lax.dot_general(left, right, ((dims[:1], dims[1:]), ((), ())), precision=...]
    ppermute x36, starting transfers between devices: 59.2 us -> 61.4 us  [swapped(): return lax.ppermute(value, 'leaf', list(enumerate(partner)))]
  transfers between devices with their start and end apart: 36 -> 36, of which waited for: 18 -> 18; matrix products, arithmetic and copies ran while one was open for 9% -> 10% of each run, Pallas kernels for 0% -> 0%
where the time goes in v6:
time: 103 us
  starting transfers between devices  61.4 us (60%)
  waiting for transfers between devices  21.2 us (21%)
  matrix products  18.4 us (18%)
    ppermute x36, starting transfers between devices, swapped(): return lax.ppermute(value, 'leaf', list(enumerate(partner)))  61.4 us
    ppermute x36, waiting for transfers between devices, swapped(): return lax.ppermute(value, 'leaf', list(enumerate(partner)))  21.2 us
    dot_general x27, matrix products, product(): lax.dot_general(left, right, ((dims[:1], dims[1:]), ((), ())), precision=...  18.4 us
  transfers between devices with their start and end apart: 36, of which 18 were waited for; matrix products, arithmetic and copies ran while one was open for 10% of the time, Pallas kernels for 0%

profile of v6, /device:TPU:1, one launch (start us, length us, event | category | flops | bytes accessed | tf_op | source)
XLA Modules:
  0.0 103.1 jit_solution(11848496146111788675)
XLA Ops:
  0.1 4.5 %fusion.98 = f32[64,1024]{1,0:T(8,128)S(1)} fusion(f32[64,1024]{1,0:T(8,128)} %param.21, f32[1024,1024]{1,0:T(8,128)} %param.22), kind=kOutput, calls=%fused_computation.177 | convolution fusion | flops 402653184 | bytes 4718592 | tf_op jit(solution)/shard_map/dot_general | solution.py:74
  5.0 3.3 %collective-permute-start = (f32[32,256]{1,0:T(8,128)S(1)}, f32[32,256]{1,0:T(8,128)S(1)}, u32[]{:S(2)}, u32[]{:S(2)}) collective-permute-start(f32[32,256]{1,0:T(8,128)S(1)} %select_bitcast_fusion), channel_id=1, source_target_pairs={{0,1},{1,0},{2,3},{3,2},{4,5},{5,4},{6,7},{7,6},{8,9},{9,8},{10,11... | collective-permute-start | bytes 98312 | tf_op jit(solution)/shard_map/ppermute | solution.py:62
  9.2 2.7 %collective-permute-start.1 = (f32[96,256]{1,0:T(8,128)S(1)}, f32[96,256]{1,0:T(8,128)S(1)}, u32[]{:S(2)}, u32[]{:S(2)}) collective-permute-start(f32[96,256]{1,0:T(8,128)S(1)} %pad_maximum_fusion.10), channel_id=1, source_target_pairs={{0,6},{1,7},{2,12},{3,13},{4,10},{5,11},{6,0},{7,1},{8,14},{9,15},... | collective-permute-start | bytes 294920 | tf_op jit(solution)/shard_map/ppermute | solution.py:62
  17.3 2.9 %collective-permute-start.3 = (f32[160,256]{1,0:T(8,128)S(1)}, f32[160,256]{1,0:T(8,128)S(1)}, u32[]{:S(2)}, u32[]{:S(2)}) collective-permute-start(f32[160,256]{1,0:T(8,128)S(1)} %pad_maximum_fusion.7), channel_id=1, source_target_pairs={{0,14},{1,15},{2,4},{3,5},{4,2},{5,3},{6,8},{7,9},{8,6},{9,7},{10,... | collective-permute-start | bytes 491528 | tf_op jit(solution)/shard_map/ppermute | solution.py:62
  21.6 2.7 %collective-permute-done.3 = f32[160,256]{1,0:T(8,128)S(1)} collective-permute-done((f32[160,256]{1,0:T(8,128)S(1)}, f32[160,256]{1,0:T(8,128)S(1)}, u32[]{:S(2)}, u32[]{:S(2)}) %collective-permute-start.3) | collective-permute-done | bytes 163872 | tf_op jit(solution)/shard_map/ppermute | solution.py:62
  27.0 2.2 %collective-permute-done.4 = f32[160,256]{1,0:T(8,128)S(1)} collective-permute-done((f32[160,256]{1,0:T(8,128)S(1)}, f32[160,256]{1,0:T(8,128)S(1)}, u32[]{:S(2)}, u32[]{:S(2)}) %collective-permute-start.4) | collective-permute-done | bytes 163872 | tf_op jit(solution)/shard_map/ppermute | solution.py:62
  31.3 2.6 %collective-permute-start.6 = (f32[256,256]{1,0:T(8,128)S(1)}, f32[256,256]{1,0:T(8,128)S(1)}, u32[]{:S(2)}, u32[]{:S(2)}) collective-permute-start(f32[256,256]{1,0:T(8,128)S(1)} %bitcast.110), channel_id=1, source_target_pairs={{0,1},{1,0},{2,3},{3,2},{4,5},{5,4},{6,7},{7,6},{8,9},{9,8},{10,11... | collective-permute-start | bytes 786440 | tf_op jit(solution)/shard_map/ppermute | solution.py:62
  34.0 2.6 %collective-permute-start.13 = (f32[48,256]{1,0:T(8,128)S(1)}, f32[48,256]{1,0:T(8,128)S(1)}, u32[]{:S(2)}, u32[]{:S(2)}) collective-permute-start(f32[48,256]{1,0:T(8,128)S(1)} %bitcast.136), channel_id=1, source_target_pairs={{0,14},{1,15},{2,4},{3,5},{4,2},{5,3},{6,8},{7,9},{8,6},{9,7},{10,... | collective-permute-start | bytes 147464 | tf_op jit(solution)/shard_map/ppermute | solution.py:62
  42.9 1.7 %collective-permute-start.14 = (f32[48,256]{1,0:T(8,128)S(1)}, f32[48,256]{1,0:T(8,128)S(1)}, u32[]{:S(2)}, u32[]{:S(2)}) collective-permute-start(f32[48,256]{1,0:T(8,128)S(1)} %bitcast_add_fusion.4), channel_id=1, source_target_pairs={{0,6},{1,7},{2,12},{3,13},{4,10},{5,11},{6,0},{7,1},{8,14},{9,15},... | collective-permute-start | bytes 147464 | tf_op jit(solution)/shard_map/ppermute | solution.py:62
  44.6 1.4 %collective-permute-done.9 = f32[96,256]{1,0:T(8,128)S(1)} collective-permute-done((f32[96,256]{1,0:T(8,128)S(1)}, f32[96,256]{1,0:T(8,128)S(1)}, u32[]{:S(2)}, u32[]{:S(2)}) %collective-permute-start.9) | collective-permute-done | bytes 98336 | tf_op jit(solution)/shard_map/ppermute | solution.py:62
  46.1 1.8 %collective-permute-start.10 = (f32[96,256]{1,0:T(8,128)S(1)}, f32[96,256]{1,0:T(8,128)S(1)}, u32[]{:S(2)}, u32[]{:S(2)}) collective-permute-start(f32[96,256]{1,0:T(8,128)S(1)} %add.107), channel_id=1, source_target_pairs={{0,6},{1,7},{2,12},{3,13},{4,10},{5,11},{6,0},{7,1},{8,14},{9,15},... | collective-permute-start | bytes 294920 | tf_op jit(solution)/shard_map/ppermute | solution.py:62
  52.1 1.7 %collective-permute-start.16 = (f32[192,256]{1,0:T(8,128)S(1)}, f32[192,256]{1,0:T(8,128)S(1)}, u32[]{:S(2)}, u32[]{:S(2)}) collective-permute-start(f32[192,256]{1,0:T(8,128)S(1)} %pad_maximum_fusion.5), channel_id=1, source_target_pairs={{0,14},{1,15},{2,4},{3,5},{4,2},{5,3},{6,8},{7,9},{8,6},{9,7},{10,... | collective-permute-start | bytes 589832 | tf_op jit(solution)/shard_map/ppermute | solution.py:62
  53.8 2.2 %collective-permute-done.20 = f32[256,256]{1,0:T(8,128)S(1)} collective-permute-done((f32[256,256]{1,0:T(8,128)S(1)}, f32[256,256]{1,0:T(8,128)S(1)}, u32[]{:S(2)}, u32[]{:S(2)}) %collective-permute-start.20) | collective-permute-done | bytes 262176 | tf_op jit(solution)/shard_map/ppermute | solution.py:62
  56.0 1.8 %collective-permute-done.16 = f32[192,256]{1,0:T(8,128)S(1)} collective-permute-done((f32[192,256]{1,0:T(8,128)S(1)}, f32[192,256]{1,0:T(8,128)S(1)}, u32[]{:S(2)}, u32[]{:S(2)}) %collective-permute-start.16) | collective-permute-done | bytes 196640 | tf_op jit(solution)/shard_map/ppermute | solution.py:62
  58.0 1.5 %collective-permute-start.17 = (f32[288,256]{1,0:T(8,128)S(1)}, f32[288,256]{1,0:T(8,128)S(1)}, u32[]{:S(2)}, u32[]{:S(2)}) collective-permute-start(f32[288,256]{1,0:T(8,128)S(1)} %pad_maximum_fusion.3), channel_id=1, source_target_pairs={{0,2},{1,3},{2,0},{3,1},{4,6},{5,7},{6,4},{7,5},{8,10},{9,11},{10,... | collective-permute-start | bytes 884744 | tf_op jit(solution)/shard_map/ppermute | solution.py:62
  59.5 1.7 %collective-permute-start.26 = (f32[192,256]{1,0:T(8,128)S(1)}, f32[192,256]{1,0:T(8,128)S(1)}, u32[]{:S(2)}, u32[]{:S(2)}) collective-permute-start(f32[192,256]{1,0:T(8,128)S(1)} %pad_maximum_fusion.6), channel_id=1, source_target_pairs={{0,48},{1,49},{2,50},{3,51},{4,52},{5,53},{6,54},{7,55},{8,56},{9,... | collective-permute-start | bytes 589832 | tf_op jit(solution)/shard_map/ppermute | solution.py:62
  61.2 5.6 %collective-permute-start.21 = (f32[256,256]{1,0:T(8,128)S(1)}, f32[256,256]{1,0:T(8,128)S(1)}, u32[]{:S(2)}, u32[]{:S(2)}) collective-permute-start(f32[256,256]{1,0:T(8,128)S(1)} %fusion.19), channel_id=1, source_target_pairs={{0,1},{1,0},{2,3},{3,2},{4,5},{5,4},{6,7},{7,6},{8,9},{9,8},{10,11... | collective-permute-start | bytes 786440 | tf_op jit(solution)/shard_map/ppermute | solution.py:62
  68.1 6.6 %collective-permute-start.22 = (f32[256,256]{1,0:T(8,128)S(1)}, f32[256,256]{1,0:T(8,128)S(1)}, u32[]{:S(2)}, u32[]{:S(2)}) collective-permute-start(f32[256,256]{1,0:T(8,128)S(1)} %bitcast.112), channel_id=1, source_target_pairs={{0,1},{1,0},{2,3},{3,2},{4,5},{5,4},{6,7},{7,6},{8,9},{9,8},{10,11... | collective-permute-start | bytes 786440 | tf_op jit(solution)/shard_map/ppermute | solution.py:62
  76.0 2.1 %collective-permute-start.28 = (f32[128,256]{1,0:T(8,128)S(1)}, f32[128,256]{1,0:T(8,128)S(1)}, u32[]{:S(2)}, u32[]{:S(2)}) collective-permute-start(f32[128,256]{1,0:T(8,128)S(1)} %slice_add_fusion), channel_id=1, source_target_pairs={{0,1},{1,0},{2,3},{3,2},{4,5},{5,4},{6,7},{7,6},{8,9},{9,8},{10,11... | collective-permute-start | bytes 393224 | tf_op jit(solution)/shard_map/ppermute | solution.py:62
  78.9 3.3 %collective-permute-start.24 = (f32[64,256]{1,0:T(8,128)S(1)}, f32[64,256]{1,0:T(8,128)S(1)}, u32[]{:S(2)}, u32[]{:S(2)}) collective-permute-start(f32[64,256]{1,0:T(8,128)S(1)} %slice_subtract_fusion), channel_id=1, source_target_pairs={{0,48},{1,49},{2,50},{3,51},{4,52},{5,53},{6,54},{7,55},{8,56},{9,... | collective-permute-start | bytes 196616 | tf_op jit(solution)/shard_map/ppermute | solution.py:62
  86.5 1.7 %collective-permute-done.25 = f32[32,256]{1,0:T(8,128)S(1)} collective-permute-done((f32[32,256]{1,0:T(8,128)S(1)}, f32[32,256]{1,0:T(8,128)S(1)}, u32[]{:S(2)}, u32[]{:S(2)}) %collective-permute-start.25) | collective-permute-done | bytes 32800 | tf_op jit(solution)/shard_map/ppermute | solution.py:62
  90.0 2.8 %collective-permute-start.32 = (f32[32,256]{1,0:T(8,128)S(1)}, f32[32,256]{1,0:T(8,128)S(1)}, u32[]{:S(2)}, u32[]{:S(2)}) collective-permute-start(f32[32,256]{1,0:T(8,128)S(1)} %slice_subtract_fusion.1), channel_id=1, source_target_pairs={{0,128},{1,129},{2,130},{3,131},{4,132},{5,133},{6,134},{7,135},{8... | collective-permute-start | bytes 98312 | tf_op jit(solution)/shard_map/ppermute | solution.py:62
  93.7 1.7 %collective-permute-start.34 = (f32[256,256]{1,0:T(8,128)S(1)}, f32[256,256]{1,0:T(8,128)S(1)}, u32[]{:S(2)}, u32[]{:S(2)}) collective-permute-start(f32[256,256]{1,0:T(8,128)S(1)} %maximum_select_fusion.17), channel_id=1, source_target_pairs={{0,1},{1,0},{2,3},{3,2},{4,5},{5,4},{6,7},{7,6},{8,9},{9,8},{10,11... | collective-permute-start | bytes 786440 | tf_op jit(solution)/shard_map/ppermute | solution.py:62
  98.4 2.5 %collective-permute-start.35 = (f32[32,256]{1,0:T(8,128)S(1)}, f32[32,256]{1,0:T(8,128)S(1)}, u32[]{:S(2)}, u32[]{:S(2)}) collective-permute-start(f32[32,256]{1,0:T(8,128)S(1)} %fusion.8), channel_id=1, source_target_pairs={{0,1},{1,0},{2,3},{3,2},{4,5},{5,4},{6,7},{7,6},{8,9},{9,8},{10,11... | collective-permute-start | bytes 98312 | tf_op jit(solution)/shard_map/ppermute | solution.py:62
  (187 shorter events, 38.4 us)
Async XLA Ops:
  5.0 4.2 %collective-permute-start = (f32[32,256]{1,0:T(8,128)S(1)}, f32[32,256]{1,0:T(8,128)S(1)}, u32[]{:S(2)}, u32[]{:S(2)}) collective-permute-start(f32[32,256]{1,0:T(8,128)S(1)} %select_bitcast_fusion), channel_id=1, source_target_pairs={{0,1},{1,0},{2,3},{3,2},{4,5},{5,4},{6,7},{7,6},{8,9},{9,8},{10,11... | collective-permute-start | bytes 98312 | tf_op jit(solution)/shard_map/ppermute | solution.py:62
  9.2 6.6 %collective-permute-start.1 = (f32[96,256]{1,0:T(8,128)S(1)}, f32[96,256]{1,0:T(8,128)S(1)}, u32[]{:S(2)}, u32[]{:S(2)}) collective-permute-start(f32[96,256]{1,0:T(8,128)S(1)} %pad_maximum_fusion.10), channel_id=1, source_target_pairs={{0,6},{1,7},{2,12},{3,13},{4,10},{5,11},{6,0},{7,1},{8,14},{9,15},... | collective-permute-start | bytes 294920 | tf_op jit(solution)/shard_map/ppermute | solution.py:62
  17.3 7.1 %collective-permute-start.3 = (f32[160,256]{1,0:T(8,128)S(1)}, f32[160,256]{1,0:T(8,128)S(1)}, u32[]{:S(2)}, u32[]{:S(2)}) collective-permute-start(f32[160,256]{1,0:T(8,128)S(1)} %pad_maximum_fusion.7), channel_id=1, source_target_pairs={{0,14},{1,15},{2,4},{3,5},{4,2},{5,3},{6,8},{7,9},{8,6},{9,7},{10,... | collective-permute-start | bytes 491528 | tf_op jit(solution)/shard_map/ppermute | solution.py:62
  20.3 5.9 %collective-permute-start.11 = (f32[192,256]{1,0:T(8,128)S(1)}, f32[192,256]{1,0:T(8,128)S(1)}, u32[]{:S(2)}, u32[]{:S(2)}) collective-permute-start(f32[192,256]{1,0:T(8,128)S(1)} %bitcast.130), channel_id=1, source_target_pairs={{0,16},{1,17},{2,18},{3,19},{4,20},{5,21},{6,22},{7,23},{8,24},{9,... | collective-permute-start | bytes 589832 | tf_op jit(solution)/shard_map/ppermute | solution.py:62
  24.4 4.8 %collective-permute-start.4 = (f32[160,256]{1,0:T(8,128)S(1)}, f32[160,256]{1,0:T(8,128)S(1)}, u32[]{:S(2)}, u32[]{:S(2)}) collective-permute-start(f32[160,256]{1,0:T(8,128)S(1)} %pad_maximum_fusion.8), channel_id=1, source_target_pairs={{0,2},{1,3},{2,0},{3,1},{4,6},{5,7},{6,4},{7,5},{8,10},{9,11},{10,... | collective-permute-start | bytes 491528 | tf_op jit(solution)/shard_map/ppermute | solution.py:62
  26.2 5.1 %collective-permute-start.12 = (f32[96,256]{1,0:T(8,128)S(1)}, f32[96,256]{1,0:T(8,128)S(1)}, u32[]{:S(2)}, u32[]{:S(2)}) collective-permute-start(f32[96,256]{1,0:T(8,128)S(1)} %bitcast.134), channel_id=1, source_target_pairs={{0,2},{1,3},{2,0},{3,1},{4,6},{5,7},{6,4},{7,5},{8,10},{9,11},{10,... | collective-permute-start | bytes 294920 | tf_op jit(solution)/shard_map/ppermute | solution.py:62
  29.2 7.3 %collective-permute-start.5 = (f32[32,256]{1,0:T(8,128)S(1)}, f32[32,256]{1,0:T(8,128)S(1)}, u32[]{:S(2)}, u32[]{:S(2)}) collective-permute-start(f32[32,256]{1,0:T(8,128)S(1)} %slice_add_fusion.3), channel_id=1, source_target_pairs={{0,16},{1,17},{2,18},{3,19},{4,20},{5,21},{6,22},{7,23},{8,24},{9,... | collective-permute-start | bytes 98312 | tf_op jit(solution)/shard_map/ppermute | solution.py:62
  31.3 5.2 %collective-permute-start.6 = (f32[256,256]{1,0:T(8,128)S(1)}, f32[256,256]{1,0:T(8,128)S(1)}, u32[]{:S(2)}, u32[]{:S(2)}) collective-permute-start(f32[256,256]{1,0:T(8,128)S(1)} %bitcast.110), channel_id=1, source_target_pairs={{0,1},{1,0},{2,3},{3,2},{4,5},{5,4},{6,7},{7,6},{8,9},{9,8},{10,11... | collective-permute-start | bytes 786440 | tf_op jit(solution)/shard_map/ppermute | solution.py:62
  34.0 7.6 %collective-permute-start.13 = (f32[48,256]{1,0:T(8,128)S(1)}, f32[48,256]{1,0:T(8,128)S(1)}, u32[]{:S(2)}, u32[]{:S(2)}) collective-permute-start(f32[48,256]{1,0:T(8,128)S(1)} %bitcast.136), channel_id=1, source_target_pairs={{0,14},{1,15},{2,4},{3,5},{4,2},{5,3},{6,8},{7,9},{8,6},{9,7},{10,... | collective-permute-start | bytes 147464 | tf_op jit(solution)/shard_map/ppermute | solution.py:62
  40.9 6.9 %collective-permute-start.19 = (f32[128,256]{1,0:T(8,128)S(1)}, f32[128,256]{1,0:T(8,128)S(1)}, u32[]{:S(2)}, u32[]{:S(2)}) collective-permute-start(f32[128,256]{1,0:T(8,128)S(1)} %maximum_select_fusion.20), channel_id=1, source_target_pairs={{0,2},{1,3},{2,0},{3,1},{4,6},{5,7},{6,4},{7,5},{8,10},{9,11},{10,... | collective-permute-start | bytes 393224 | tf_op jit(solution)/shard_map/ppermute | solution.py:62
  42.9 5.0 %collective-permute-start.14 = (f32[48,256]{1,0:T(8,128)S(1)}, f32[48,256]{1,0:T(8,128)S(1)}, u32[]{:S(2)}, u32[]{:S(2)}) collective-permute-start(f32[48,256]{1,0:T(8,128)S(1)} %bitcast_add_fusion.4), channel_id=1, source_target_pairs={{0,6},{1,7},{2,12},{3,13},{4,10},{5,11},{6,0},{7,1},{8,14},{9,15},... | collective-permute-start | bytes 147464 | tf_op jit(solution)/shard_map/ppermute | solution.py:62
  46.1 5.9 %collective-permute-start.10 = (f32[96,256]{1,0:T(8,128)S(1)}, f32[96,256]{1,0:T(8,128)S(1)}, u32[]{:S(2)}, u32[]{:S(2)}) collective-permute-start(f32[96,256]{1,0:T(8,128)S(1)} %add.107), channel_id=1, source_target_pairs={{0,6},{1,7},{2,12},{3,13},{4,10},{5,11},{6,0},{7,1},{8,14},{9,15},... | collective-permute-start | bytes 294920 | tf_op jit(solution)/shard_map/ppermute | solution.py:62
  48.9 7.1 %collective-permute-start.20 = (f32[256,256]{1,0:T(8,128)S(1)}, f32[256,256]{1,0:T(8,128)S(1)}, u32[]{:S(2)}, u32[]{:S(2)}) collective-permute-start(f32[256,256]{1,0:T(8,128)S(1)} %fusion.18), channel_id=1, source_target_pairs={{0,16},{1,17},{2,18},{3,19},{4,20},{5,21},{6,22},{7,23},{8,24},{9,... | collective-permute-start | bytes 786440 | tf_op jit(solution)/shard_map/ppermute | solution.py:62
  52.1 5.8 %collective-permute-start.16 = (f32[192,256]{1,0:T(8,128)S(1)}, f32[192,256]{1,0:T(8,128)S(1)}, u32[]{:S(2)}, u32[]{:S(2)}) collective-permute-start(f32[192,256]{1,0:T(8,128)S(1)} %pad_maximum_fusion.5), channel_id=1, source_target_pairs={{0,14},{1,15},{2,4},{3,5},{4,2},{5,3},{6,8},{7,9},{8,6},{9,7},{10,... | collective-permute-start | bytes 589832 | tf_op jit(solution)/shard_map/ppermute | solution.py:62
  58.0 8.8 %collective-permute-start.17 = (f32[288,256]{1,0:T(8,128)S(1)}, f32[288,256]{1,0:T(8,128)S(1)}, u32[]{:S(2)}, u32[]{:S(2)}) collective-permute-start(f32[288,256]{1,0:T(8,128)S(1)} %pad_maximum_fusion.3), channel_id=1, source_target_pairs={{0,2},{1,3},{2,0},{3,1},{4,6},{5,7},{6,4},{7,5},{8,10},{9,11},{10,... | collective-permute-start | bytes 884744 | tf_op jit(solution)/shard_map/ppermute | solution.py:62
  59.5 7.3 %collective-permute-start.26 = (f32[192,256]{1,0:T(8,128)S(1)}, f32[192,256]{1,0:T(8,128)S(1)}, u32[]{:S(2)}, u32[]{:S(2)}) collective-permute-start(f32[192,256]{1,0:T(8,128)S(1)} %pad_maximum_fusion.6), channel_id=1, source_target_pairs={{0,48},{1,49},{2,50},{3,51},{4,52},{5,53},{6,54},{7,55},{8,56},{9,... | collective-permute-start | bytes 589832 | tf_op jit(solution)/shard_map/ppermute | solution.py:62
  61.2 6.7 %collective-permute-start.21 = (f32[256,256]{1,0:T(8,128)S(1)}, f32[256,256]{1,0:T(8,128)S(1)}, u32[]{:S(2)}, u32[]{:S(2)}) collective-permute-start(f32[256,256]{1,0:T(8,128)S(1)} %fusion.19), channel_id=1, source_target_pairs={{0,1},{1,0},{2,3},{3,2},{4,5},{5,4},{6,7},{7,6},{8,9},{9,8},{10,11... | collective-permute-start | bytes 786440 | tf_op jit(solution)/shard_map/ppermute | solution.py:62
  68.0 8.0 %collective-permute-start.18 = (f32[160,256]{1,0:T(8,128)S(1)}, f32[160,256]{1,0:T(8,128)S(1)}, u32[]{:S(2)}, u32[]{:S(2)}) collective-permute-start(f32[160,256]{1,0:T(8,128)S(1)} %pad_maximum_fusion.9), channel_id=1, source_target_pairs={{0,48},{1,49},{2,50},{3,51},{4,52},{5,53},{6,54},{7,55},{8,56},{9,... | collective-permute-start | bytes 491528 | tf_op jit(solution)/shard_map/ppermute | solution.py:62
  68.1 10.3 %collective-permute-start.22 = (f32[256,256]{1,0:T(8,128)S(1)}, f32[256,256]{1,0:T(8,128)S(1)}, u32[]{:S(2)}, u32[]{:S(2)}) collective-permute-start(f32[256,256]{1,0:T(8,128)S(1)} %bitcast.112), channel_id=1, source_target_pairs={{0,1},{1,0},{2,3},{3,2},{4,5},{5,4},{6,7},{7,6},{8,9},{9,8},{10,11... | collective-permute-start | bytes 786440 | tf_op jit(solution)/shard_map/ppermute | solution.py:62
  76.0 10.6 %collective-permute-start.28 = (f32[128,256]{1,0:T(8,128)S(1)}, f32[128,256]{1,0:T(8,128)S(1)}, u32[]{:S(2)}, u32[]{:S(2)}) collective-permute-start(f32[128,256]{1,0:T(8,128)S(1)} %slice_add_fusion), channel_id=1, source_target_pairs={{0,1},{1,0},{2,3},{3,2},{4,5},{5,4},{6,7},{7,6},{8,9},{9,8},{10,11... | collective-permute-start | bytes 393224 | tf_op jit(solution)/shard_map/ppermute | solution.py:62
  78.9 5.7 %collective-permute-start.24 = (f32[64,256]{1,0:T(8,128)S(1)}, f32[64,256]{1,0:T(8,128)S(1)}, u32[]{:S(2)}, u32[]{:S(2)}) collective-permute-start(f32[64,256]{1,0:T(8,128)S(1)} %slice_subtract_fusion), channel_id=1, source_target_pairs={{0,48},{1,49},{2,50},{3,51},{4,52},{5,53},{6,54},{7,55},{8,56},{9,... | collective-permute-start | bytes 196616 | tf_op jit(solution)/shard_map/ppermute | solution.py:62
  82.6 5.7 %collective-permute-start.33 = (f32[128,256]{1,0:T(8,128)S(1)}, f32[128,256]{1,0:T(8,128)S(1)}, u32[]{:S(2)}, u32[]{:S(2)}) collective-permute-start(f32[128,256]{1,0:T(8,128)S(1)} %maximum_select_fusion.23), channel_id=1, source_target_pairs={{0,64},{1,65},{2,66},{3,67},{4,68},{5,69},{6,70},{7,71},{8,72},{9,... | collective-permute-start | bytes 393224 | tf_op jit(solution)/shard_map/ppermute | solution.py:62
  83.9 4.4 %collective-permute-start.27 = (f32[256,256]{1,0:T(8,128)S(1)}, f32[256,256]{1,0:T(8,128)S(1)}, u32[]{:S(2)}, u32[]{:S(2)}) collective-permute-start(f32[256,256]{1,0:T(8,128)S(1)} %maximum_select_fusion.14), channel_id=1, source_target_pairs={{0,1},{1,0},{2,3},{3,2},{4,5},{5,4},{6,7},{7,6},{8,9},{9,8},{10,11... | collective-permute-start | bytes 786440 | tf_op jit(solution)/shard_map/ppermute | solution.py:62
  90.0 5.5 %collective-permute-start.32 = (f32[32,256]{1,0:T(8,128)S(1)}, f32[32,256]{1,0:T(8,128)S(1)}, u32[]{:S(2)}, u32[]{:S(2)}) collective-permute-start(f32[32,256]{1,0:T(8,128)S(1)} %slice_subtract_fusion.1), channel_id=1, source_target_pairs={{0,128},{1,129},{2,130},{3,131},{4,132},{5,133},{6,134},{7,135},{8... | collective-permute-start | bytes 98312 | tf_op jit(solution)/shard_map/ppermute | solution.py:62
  (31 other events, 311.6 us)
